TPU v7x, 32 devices: a whole 2x2x4 slice. The times are simulated.
32 devices in a mesh: dp: 2 (over x), seq: 16 (over z, y, core).
Axes of the slice: x: 2, y: 2, z: 4, core: 2. Of those that a mesh axis runs over, the one named last changes fastest.
Arguments:
- mixed: bfloat16 [2, 2048, 4096], P('dp', 'seq'), may hold values from -6 to 6
- conv_weight: bfloat16 [4, 4096], replicated, may hold values from -3 to 3
- log_decay: float32 [2, 16, 2048], P('dp', None, 'seq'), may hold values from -0.75 to 0, as said below
- beta: float32 [2, 16, 2048], P('dp', None, 'seq'), may hold values from 0.01 to 0.5
- doc_ids: int32 [2, 2048], P('dp', 'seq'), may hold values from 0 to 7, never falling along the last dimension, each value on 1 to 1024 neighbouring positions
- out_grad: bfloat16 [2, 2048, 2048], P('dp', 'seq'), may hold values from -6 to 6
Outputs:
- output: bfloat16 [2, 2048, 2048], P('dp', 'seq')
- d_mixed: bfloat16 [2, 2048, 4096], P('dp', 'seq')
- d_conv_weight: float32 [4, 4096], replicated
- d_log_decay: float32 [2, 16, 2048], P('dp', None, 'seq')
- d_beta: float32 [2, 16, 2048], P('dp', None, 'seq')
Inputs may be any that keep to these rules, and one draw needn't show every extreme that they name: `doc_ids`: document numbers never fall along a slab; each of the 8 documents holds 1 to 1024 tokens, and one holds exactly 1024. `log_decay`: every entry is negative.
All inputs are finite; a program needn't handle non-finite values.
Results may differ from a plain program's by a relative error of at most 0.00115.
Values may be sent and summed in bfloat16 or wider, within the bound.
No kernel may reach another device: no remote copies, remote signals or barrier semaphores. Data moves between devices by JAX's collectives and lax.ppermute only.
A program may use at most 128 MiB of HBM per device.

v0:
```python
import jax
import jax.numpy as jnp
from jax import lax
from jax.sharding import PartitionSpec as P

DK = 128
KH = 8
VH = 16
CH = 64
SPAN = 8


highest_precision = lax.Precision.HIGHEST
epsilon = 1e-06


def passed_along(array, axis, by):
    length = lax.axis_size(axis)
    pairs = [(i, i + by) for i in range(length) if 0 <= i + by < length]
    return lax.ppermute(array, axis, pairs)


def unit_norm(values):
    return values * lax.rsqrt(jnp.sum(values * values, -1, keepdims=True) + epsilon)


def compose(earlier, later):
    first_map, first_shift = earlier
    second_map, second_shift = later
    joined = jnp.einsum("hij,hjk->hik", second_map, first_map, precision=highest_precision)
    moved = (
        jnp.einsum("hij,hjk->hik", second_map, first_shift, precision=highest_precision)
        + second_shift
    )
    return (joined, moved)


def advance(transition, offset_term, carried):
    return (
        jnp.einsum("hij,hjk->hik", transition, carried, precision=highest_precision) + offset_term
    )


def prepare(rows_ext, weight, decay, rate, docs_ext, key_heads, per_key, value_width):
    length = rows_ext.shape[0] - 3
    head_count = decay.shape[0]
    own_docs = docs_ext[3:]
    summed = weight[3] * rows_ext[3:]
    for offset in (1, 2, 3):
        earlier_docs = docs_ext[3 - offset : 3 - offset + length]
        earlier_rows = rows_ext[3 - offset : 3 - offset + length]
        summed = summed + weight[3 - offset] * jnp.where(
            (earlier_docs == own_docs)[:, None], earlier_rows, 0.0
        )
    active = jax.nn.silu(summed)
    query_matrix = active[:, : key_heads * DK].reshape(length, key_heads, DK)
    key_rows = active[:, key_heads * DK : 2 * key_heads * DK].reshape(length, key_heads, DK)
    values = active[:, 2 * key_heads * DK :].reshape(length, head_count, value_width)
    query_matrix = jnp.repeat(unit_norm(query_matrix) * DK ** (-0.5), per_key, axis=1)
    key_rows = jnp.repeat(unit_norm(key_rows), per_key, axis=1)
    blocks = length // CH

    def split_blocks(array):
        return array.reshape(blocks, CH, head_count, -1).transpose(0, 2, 1, 3)

    query_blocks = split_blocks(query_matrix)
    key_blocks = split_blocks(key_rows)
    value_blocks = split_blocks(values)
    cumulated = jnp.cumsum(decay.reshape(head_count, blocks, CH).transpose(1, 0, 2), axis=-1)
    rate_blocks = rate.reshape(head_count, blocks, CH).transpose(1, 0, 2)
    doc_blocks = own_docs.reshape(blocks, CH)
    before = docs_ext[2 : 2 + length].reshape(blocks, CH)[:, 0]
    carry_in = (doc_blocks == before[:, None]).astype(jnp.float32)
    positions = jnp.arange(CH)
    lower = positions[:, None] >= positions[None, :]
    strict = positions[:, None] > positions[None, :]
    same_doc = doc_blocks[:, :, None] == doc_blocks[:, None, :]
    gaps = cumulated[..., :, None] - cumulated[..., None, :]
    fading = jnp.where((same_doc & lower)[:, None], jnp.exp(jnp.minimum(gaps, 0.0)), 0.0)
    key_inner = jnp.einsum("nhik,nhjk->nhij", key_blocks, key_blocks, precision=highest_precision)
    triangle = jnp.eye(CH, dtype=jnp.float32) + jnp.where(
        strict, rate_blocks[..., :, None] * key_inner * fading, 0.0
    )
    entry_scale = carry_in[:, None, :] * jnp.exp(cumulated)
    right_side = jnp.concatenate(
        [
            (rate_blocks * entry_scale)[..., None] * key_blocks,
            rate_blocks[..., None] * value_blocks,
        ],
        -1,
    )
    solved = jax.scipy.linalg.solve_triangular(triangle, right_side, lower=True, unit_diagonal=True)
    woodbury_keys = solved[..., :DK]
    woodbury_values = solved[..., DK:]
    scores = (
        jnp.einsum("nhik,nhjk->nhij", query_blocks, key_blocks, precision=highest_precision)
        * fading
    )
    query_entering = entry_scale[..., None] * query_blocks
    tail = jnp.where(
        (doc_blocks == doc_blocks[:, -1:])[:, None, :],
        jnp.exp(cumulated[..., -1:] - cumulated),
        0.0,
    )
    key_result = tail[..., None] * key_blocks
    keep_last = carry_in[:, None, -1] * jnp.exp(cumulated[..., -1])
    return (query_entering, scores, woodbury_keys, woodbury_values, key_result, keep_last)


def chain_terms(parts):
    query_entering, scores, woodbury_keys, woodbury_values, key_result, keep_last = parts
    identity_block = jnp.eye(DK, dtype=jnp.float32)
    transitions = keep_last[..., None, None] * identity_block - jnp.einsum(
        "nhik,nhil->nhkl", key_result, woodbury_keys, precision=highest_precision
    )
    offsets = jnp.einsum(
        "nhik,nhiv->nhkv", key_result, woodbury_values, precision=highest_precision
    )

    def fold(accumulated, item):
        return (compose(accumulated, item), None)

    start = (jnp.broadcast_to(identity_block, (VH, DK, DK)), jnp.zeros((VH, DK, DK), jnp.float32))
    result, unused = lax.scan(fold, start, (transitions, offsets))
    return result


def finish(parts, state_in):

    def advance_block(memory_state, block):
        query_entering, scores, woodbury_keys, woodbury_values, key_result, keep_last = block
        delta_update = woodbury_values - jnp.einsum(
            "uab,ubf->uaf", woodbury_keys, memory_state, precision=highest_precision
        )
        emitted_output = jnp.einsum(
            "uab,ubf->uaf", query_entering, memory_state, precision=highest_precision
        )
        emitted_output = emitted_output + jnp.einsum(
            "hij,hjv->hiv", scores, delta_update, precision=highest_precision
        )
        memory_state = keep_last[:, None, None] * memory_state + jnp.einsum(
            "qno,qnb->qob", key_result, delta_update, precision=highest_precision
        )
        return (memory_state, emitted_output)

    state_out, emitted_output = lax.scan(advance_block, state_in, parts)
    blocks = emitted_output.shape[0]
    flat = emitted_output.transpose(0, 2, 1, 3).reshape(blocks * CH, -1)
    return (flat, state_out)


def token_layout(mixed, weight, log_decay, beta, doc_ids, out_grad):
    rows_local = mixed[0]
    docs_local = doc_ids[0]
    rim_rows, rim_docs = passed_along((rows_local[-3:], docs_local[-3:]), "seq", 1)
    rows_ext = jnp.concatenate([rim_rows, rows_local], 0).astype(jnp.float32)
    docs_ext = jnp.concatenate([rim_docs, docs_local], 0)

    def local_terms(rows_in, weight_in, decay_in, rate_in):
        return prepare(rows_in, weight_in, decay_in, rate_in, docs_ext, KH, VH // KH, DK)

    parts, prepare_pull = jax.vjp(local_terms, rows_ext, weight, log_decay[0], beta[0])
    transitions, offsets = chain_terms(parts)
    identity = (
        jnp.broadcast_to(jnp.eye(DK, dtype=jnp.float32), (VH, DK, DK)),
        jnp.zeros((VH, DK, DK), jnp.float32),
    )
    state_in = identity[1]
    for relay_step in range(SPAN):
        state_in = passed_along(advance(transitions, offsets, state_in), "seq", 1)
    (output, state_out), finish_pull = jax.vjp(finish, parts, state_in)
    cotangent = out_grad[0].astype(jnp.float32)
    parts_former, local_back = finish_pull((cotangent, jnp.zeros_like(state_out)))
    back_maps = jnp.swapaxes(transitions, 1, 2)
    state_back = identity[1]
    for relay_step in range(SPAN):
        state_back = passed_along(advance(back_maps, local_back, state_back), "seq", -1)
    parts_latter, ignored = finish_pull((jnp.zeros_like(output), state_back))
    parts_total = jax.tree.map(lambda former, latter: former + latter, parts_former, parts_latter)
    grad_rows, grad_weight, grad_decay, grad_rate = prepare_pull(parts_total)
    incoming = passed_along(grad_rows[:3].astype(jnp.bfloat16), "seq", -1).astype(jnp.float32)
    grad_local = grad_rows[3:].at[-3:].add(incoming)
    return (
        output.astype(jnp.bfloat16),
        grad_local.astype(jnp.bfloat16),
        grad_weight,
        grad_decay,
        grad_rate,
    )


def local(mixed, conv_weight, log_decay, beta, doc_ids, out_grad):
    weight = conv_weight.astype(jnp.float32)
    output, grad_local, grad_weight, grad_decay, grad_rate = token_layout(
        mixed, weight, log_decay, beta, doc_ids, out_grad
    )
    total_weight = lax.psum(grad_weight, ("dp", "seq"))
    return (output[None], grad_local[None], total_weight, grad_decay[None], grad_rate[None])


def solution(mesh):
    in_specs = (
        P("dp", "seq", None),
        P(),
        P("dp", None, "seq"),
        P("dp", None, "seq"),
        P("dp", "seq"),
        P("dp", "seq", None),
    )
    out_specs = (
        P("dp", "seq", None),
        P("dp", "seq", None),
        P(),
        P("dp", None, "seq"),
        P("dp", None, "seq"),
    )
    return jax.shard_map(local, mesh=mesh, in_specs=in_specs, out_specs=out_specs, check_vma=False)
```

profile of v0, /device:TPU:0, one launch (start us, length us, event | category | flops | bytes accessed | tf_op | source)
XLA Modules:
  0.0 809.0 jit_solution(17101052796931969190)
XLA Ops:
  8.1 2.4 collective-permute-start.1
  11.2 4.5 collective-permute-start
  22.6 5.8 fusion.115
  31.2 2.5 reshape.316
  33.7 2.7 copy.240
  44.9 158.1 %custom-call.10 = f32[2,16,1,64,64]{3,4,2,1,0:T(8,128)S(1)} custom-call(f32[2,16,1,64,64]{4,3,2,1,0:T(8,128)} %get-tuple-element.1184), custom_call_target="InvertDiagBlocksLowerTriangular" | custom-call | tf_op jit(solution)/shard_map/jvp(jit(_solve_triangular))/vmap(vmap())/triangular_solve | solution.py:92
  206.8 4.8 fusion.196
  211.6 5.2 multiply_subtract_fusion
  216.9 11.3 %while.87 = (s32[]{:T(128)}, f32[16,128,128]{2,1,0:T(8,128)S(1)}, f32[16,128,128]{2,1,0:T(8,128)S(1)}, f32[2,16,128,128]{3,2,1,0:T(8,128)}, f32[2,16,128,128]{3,2,1,0:T(8,128)}, /*index=5*/s32[]{:T(128)}, s32[]{:T(128)}) while((s32[]{:T(128)}, f32[16,128,128]{2,1,0:T(8,128)S(1)}, f32[16,128,128]{2,1,0:T(8,128)S(1)}, ...), condition=%wide.region_3.4_spmd.clone, body=%wide.region_2.3_spmd.clone.sunk | while | flops 805830656 | bytes 19924604 | solution.py:124
  219.9 2.7 convolution_add_fusion.36
  225.5 2.7 convolution_add_fusion.36
  234.6 13.0 %collective-permute-start.3 = (f32[16,128,128]{2,1,0:T(8,128)S(1)}, f32[16,128,128]{2,1,0:T(8,128)S(1)}, u32[]{:S(2)}, u32[]{:S(2)}) collective-permute-start(f32[16,128,128]{2,1,0:T(8,128)S(1)} %convolution_add_fusion.25), channel_id=1, source_target_pairs={{0,1},{1,2},{2,3},{3,4},{4,5},{5,6},{6,7},{7,8},{8,9},{9,10},{10,1... | collective-permute-start | bytes 3145736 | tf_op jit(solution)/shard_map/ppermute | solution.py:20
  251.0 13.9 %collective-permute-start.4 = (f32[16,128,128]{2,1,0:T(8,128)S(1)}, f32[16,128,128]{2,1,0:T(8,128)S(1)}, u32[]{:S(2)}, u32[]{:S(2)}) collective-permute-start(f32[16,128,128]{2,1,0:T(8,128)S(1)} %convolution_add_fusion.24), channel_id=1, source_target_pairs={{0,1},{1,2},{2,3},{3,4},{4,5},{5,6},{6,7},{7,8},{8,9},{9,10},{10,1... | collective-permute-start | bytes 3145736 | tf_op jit(solution)/shard_map/ppermute | solution.py:20
  268.4 13.9 %collective-permute-start.5 = (f32[16,128,128]{2,1,0:T(8,128)S(1)}, f32[16,128,128]{2,1,0:T(8,128)S(1)}, u32[]{:S(2)}, u32[]{:S(2)}) collective-permute-start(f32[16,128,128]{2,1,0:T(8,128)S(1)} %convolution_add_fusion.23), channel_id=1, source_target_pairs={{0,1},{1,2},{2,3},{3,4},{4,5},{5,6},{6,7},{7,8},{8,9},{9,10},{10,1... | collective-permute-start | bytes 3145736 | tf_op jit(solution)/shard_map/ppermute | solution.py:20
  285.7 13.9 %collective-permute-start.6 = (f32[16,128,128]{2,1,0:T(8,128)S(1)}, f32[16,128,128]{2,1,0:T(8,128)S(1)}, u32[]{:S(2)}, u32[]{:S(2)}) collective-permute-start(f32[16,128,128]{2,1,0:T(8,128)S(1)} %convolution_add_fusion.22), channel_id=1, source_target_pairs={{0,1},{1,2},{2,3},{3,4},{4,5},{5,6},{6,7},{7,8},{8,9},{9,10},{10,1... | collective-permute-start | bytes 3145736 | tf_op jit(solution)/shard_map/ppermute | solution.py:20
  303.0 13.9 %collective-permute-start.7 = (f32[16,128,128]{2,1,0:T(8,128)S(1)}, f32[16,128,128]{2,1,0:T(8,128)S(1)}, u32[]{:S(2)}, u32[]{:S(2)}) collective-permute-start(f32[16,128,128]{2,1,0:T(8,128)S(1)} %convolution_add_fusion.21), channel_id=1, source_target_pairs={{0,1},{1,2},{2,3},{3,4},{4,5},{5,6},{6,7},{7,8},{8,9},{9,10},{10,1... | collective-permute-start | bytes 3145736 | tf_op jit(solution)/shard_map/ppermute | solution.py:20
  320.4 14.4 %collective-permute-start.8 = (f32[16,128,128]{2,1,0:T(8,128)S(1)}, f32[16,128,128]{2,1,0:T(8,128)S(1)}, u32[]{:S(2)}, u32[]{:S(2)}) collective-permute-start(f32[16,128,128]{2,1,0:T(8,128)S(1)} %convolution_add_fusion.20), channel_id=1, source_target_pairs={{0,1},{1,2},{2,3},{3,4},{4,5},{5,6},{6,7},{7,8},{8,9},{9,10},{10,1... | collective-permute-start | bytes 3145736 | tf_op jit(solution)/shard_map/ppermute | solution.py:20
  338.7 13.9 %collective-permute-start.9 = (f32[16,128,128]{2,1,0:T(8,128)}, f32[16,128,128]{2,1,0:T(8,128)S(1)}, u32[]{:S(2)}, u32[]{:S(2)}) collective-permute-start(f32[16,128,128]{2,1,0:T(8,128)} %convolution_add_fusion.19), channel_id=1, source_target_pairs={{0,1},{1,2},{2,3},{3,4},{4,5},{5,6},{6,7},{7,8},{8,9},{9,10},{10,1... | collective-permute-start | bytes 3145736 | tf_op jit(solution)/shard_map/ppermute | solution.py:20
  357.1 2.5 copy.248
  359.7 2.7 bitcast_multiply_fusion.3
  365.1 16.1 %while.85 = (s32[]{:T(128)}, f32[16,128,128]{2,1,0:T(8,128)S(1)}, bf16[2,16,64,128]{3,2,1,0:T(8,128)(2,1)}, f32[2,16,128,128]{3,2,1,0:T(8,128)}, f32[2,16,64,128...) while((s32[]{:T(128)}, f32[16,128,128]{2,1,0:T(8,128)S(1)}, ...), condition=%wide.region_6.7_spmd, body=%wide.region_5.6_spmd.sunk | while | flops 705429504 | bytes 39849976 | solution.py:146
  367.0 2.2 bitcast_dynamic-update-slice_fusion.8
  386.8 35.1 %while.88 = (s32[]{:T(128)}, f32[16,128,128]{2,1,0:T(8,128)S(1)}, f32[2,16,64,128]{3,2,1,0:T(8,128)}, f32[2,16,64,64]{3,2,1,0:T(8,128)}, f32[2,16,64,128]{3,2,1,...) while((s32[]{:T(128)}, f32[16,128,128]{2,1,0:T(8,128)S(1)}, ...), condition=%wide.region_9.10_spmd.clone, body=%wide.region_7.9_spmd.clone.sunk | while | flops 1412038656 | bytes 87039464 | solution.py:146
  425.0 5.9 collective-permute-done.10
  434.1 16.9 %collective-permute-done.11 = f32[16,128,128]{2,1,0:T(8,128)S(1)} collective-permute-done((f32[16,128,128]{2,1,0:T(8,128)S(1)}, f32[16,128,128]{2,1,0:T(8,128)S(1)}, u32[]{:S(2)}, u32[]{:S(2)}) %collective-permute-start.11) | collective-permute-done | bytes 1048608 | tf_op jit(solution)/shard_map/ppermute | solution.py:20
  454.2 14.8 %collective-permute-done.12 = f32[16,128,128]{2,1,0:T(8,128)S(1)} collective-permute-done((f32[16,128,128]{2,1,0:T(8,128)S(1)}, f32[16,128,128]{2,1,0:T(8,128)S(1)}, u32[]{:S(2)}, u32[]{:S(2)}) %collective-permute-start.12) | collective-permute-done | bytes 1048608 | tf_op jit(solution)/shard_map/ppermute | solution.py:20
  472.2 14.8 %collective-permute-done.13 = f32[16,128,128]{2,1,0:T(8,128)S(1)} collective-permute-done((f32[16,128,128]{2,1,0:T(8,128)S(1)}, f32[16,128,128]{2,1,0:T(8,128)S(1)}, u32[]{:S(2)}, u32[]{:S(2)}) %collective-permute-start.13) | collective-permute-done | bytes 1048608 | tf_op jit(solution)/shard_map/ppermute | solution.py:20
  490.2 14.8 %collective-permute-done.14 = f32[16,128,128]{2,1,0:T(8,128)S(1)} collective-permute-done((f32[16,128,128]{2,1,0:T(8,128)S(1)}, f32[16,128,128]{2,1,0:T(8,128)S(1)}, u32[]{:S(2)}, u32[]{:S(2)}) %collective-permute-start.14) | collective-permute-done | bytes 1048608 | tf_op jit(solution)/shard_map/ppermute | solution.py:20
  508.2 14.8 %collective-permute-done.15 = f32[16,128,128]{2,1,0:T(8,128)S(1)} collective-permute-done((f32[16,128,128]{2,1,0:T(8,128)S(1)}, f32[16,128,128]{2,1,0:T(8,128)S(1)}, u32[]{:S(2)}, u32[]{:S(2)}) %collective-permute-start.15) | collective-permute-done | bytes 1048608 | tf_op jit(solution)/shard_map/ppermute | solution.py:20
  526.4 14.8 %collective-permute-done.16 = f32[16,128,128]{2,1,0:T(8,128)S(1)} collective-permute-done((f32[16,128,128]{2,1,0:T(8,128)S(1)}, f32[16,128,128]{2,1,0:T(8,128)S(1)}, u32[]{:S(2)}, u32[]{:S(2)}) %collective-permute-start.16) | collective-permute-done | bytes 1048608 | tf_op jit(solution)/shard_map/ppermute | solution.py:20
  541.2 2.9 convolution_add_fusion.11
  547.0 13.5 %collective-permute-done.17 = f32[16,128,128]{2,1,0:T(8,128)S(1)} collective-permute-done((f32[16,128,128]{2,1,0:T(8,128)}, f32[16,128,128]{2,1,0:T(8,128)S(1)}, u32[]{:S(2)}, u32[]{:S(2)}) %collective-permute-start.17) | collective-permute-done | bytes 1048608 | tf_op jit(solution)/shard_map/ppermute | solution.py:20
  566.1 32.2 %while.86 = (s32[]{:T(128)}, f32[16,128,128]{2,1,0:T(8,128)S(1)}, f32[2,16,64,128]{3,2,1,0:T(8,128)}, f32[2,16,64,64]{3,2,1,0:T(8,128)}, f32[2,16,64,128]{3,2,1,...) while((s32[]{:T(128)}, f32[16,128,128]{2,1,0:T(8,128)S(1)}, ...), condition=%wide.region_12.13_spmd, body=%wide.region_10.12_spmd.sunk | while | flops 1410990080 | bytes 67115376 | solution.py:146
  567.3 2.9 fusion.331
  583.2 2.9 fusion.331
  603.4 2.3 fusion.116
  605.7 2.2 fusion.134
  608.0 3.5 multiply_reduce_fusion.4
  615.0 3.1 convolution_add_fusion.10
  629.2 2.3 copy.296
  631.5 2.7 reshape.317
  636.2 9.9 %multiply_reduce_fusion.3 = (f32[4096]{0:T(1024)S(1)}, f32[4096]{0:T(1024)S(1)}, f32[4096]{0:T(1024)S(1)}, f32[4096]{0:T(1024)S(1)}, f32[128,4096]{0,1:T(8,128)S(1)}) fusion(f32[131,4096]{0,1:T(8,128)} %copy-done.10, pred[128]{0:T(512)(128)(4,1)S(1)} %copy-done.99, pred[128]{0:T(512)(128)(4,1)S(1)} %copy-done.95, pred[128]{0:T(512)(128)(4,1)S(1)} %copy-done.97, ...), kind=kLoop, calls=%fused_computation.156 | loop fusion | flops 11517952 | bytes 14745984 | tf_op jit(solution)/shard_map/transpose(jvp())/reduce_sum | solution.py:52
  646.1 2.5 multiply_select_fusion.2
  648.6 3.3 pad_add_fusion
  660.0 9.5 %collective-permute-done.18 = bf16[3,4096]{1,0:T(4,128)(2,1)S(1)} collective-permute-done((bf16[3,4096]{1,0:T(4,128)(2,1)S(1)}, bf16[3,4096]{1,0:T(4,128)(2,1)S(1)}, u32[]{:S(2)}, u32[]{:S(2)}) %collective-permute-start.18) | collective-permute-done | bytes 24608 | tf_op jit(solution)/shard_map/ppermute | solution.py:20
  671.7 11.0 %scatter-add.4 = bf16[128,4096]{0,1:T(8,128)(2,1)} dynamic-update-slice(bf16[128,4096]{0,1:T(8,128)(2,1)} %slice.163, bf16[3,4096]{0,1:T(8,128)(2,1)S(1)} %slice_add_fusion, s32[]{:T(128)} %constant.228.clone.1, s32[]{:T(128)} %constant.221.clone.1) | dynamic-update-slice | bytes 49156 | tf_op jit(solution)/shard_map/scatter-add | solution.py:182
  682.7 2.3 copy.278
  685.0 115.5 %all-reduce.17.cloned.1.call-done = f32[4,4096]{1,0:T(4,128)} async-done(((f32[4,4096]{1,0:T(4,128)}), f32[4,4096]{1,0:T(4,128)}) %all-reduce.17.cloned.1.call-update) | async-done | bytes 65552 | tf_op jit(solution)/shard_map/psum | solution.py:197
  (499 shorter events, 206.0 us)
Async XLA Ops:
  7.2 11.1 %copy-start.106 = (s32[1,128]{1,0:T(1,128)S(1)}, s32[1,128]{1,0:T(1,128)}, u32[]{:S(2)}) copy-start(s32[1,128]{1,0:T(1,128)} %param.20) | copy-start | bytes 1540
  7.2 10.3 %copy-start.87 = (bf16[4,4096]{1,0:T(4,128)(2,1)S(1)}, bf16[4,4096]{1,0:T(4,128)(2,1)}, u32[]{:S(2)}) copy-start(bf16[4,4096]{1,0:T(4,128)(2,1)} %param.17) | copy-start | bytes 98308
  7.2 10.4 %copy-start.102 = (f32[1,16,128]{2,1,0:T(8,128)S(1)}, f32[1,16,128]{2,1,0:T(8,128)}, u32[]{:S(2)}) copy-start(f32[1,16,128]{2,1,0:T(8,128)} %param.19) | copy-start | bytes 24580
  7.2 10.5 %copy-start.103 = (f32[1,16,128]{2,1,0:T(8,128)S(1)}, f32[1,16,128]{2,1,0:T(8,128)}, u32[]{:S(2)}) copy-start(f32[1,16,128]{2,1,0:T(8,128)} %param.18) | copy-start | bytes 24580
  7.2 793.3 %all-reduce.17.cloned.1.call-start = ((), (), s32[]{:S(2)}) async-start(), calls=%async_computation | async-start | bytes 131072 | tf_op jit(solution)/shard_map/psum | solution.py:197
  8.1 13.1 %collective-permute-start.1 = (bf16[3,4096]{1,0:T(4,128)(2,1)S(1)}, bf16[3,4096]{1,0:T(4,128)(2,1)S(1)}, u32[]{:S(2)}, u32[]{:S(2)}) collective-permute-start(bf16[3,4096]{1,0:T(4,128)(2,1)S(1)} %slice_bitcast_fusion), channel_id=1, source_target_pairs={{0,1},{1,2},{2,3},{3,4},{4,5},{5,6},{6,7},{7,8},{8,9},{9,10},{10,1... | collective-permute-start | bytes 73736 | tf_op jit(solution)/shard_map/ppermute | solution.py:20
  11.2 8.8 %collective-permute-start = (s32[3]{0:T(128)S(1)}, s32[3]{0:T(128)S(1)}, u32[]{:S(2)}, u32[]{:S(2)}) collective-permute-start(s32[3]{0:T(128)S(1)} %slice_bitcast_fusion.1), channel_id=1, source_target_pairs={{0,1},{1,2},{2,3},{3,4},{4,5},{5,6},{6,7},{7,8},{8,9},{9,10},{10,1... | collective-permute-start | bytes 44 | tf_op jit(solution)/shard_map/ppermute | solution.py:20
  17.5 5.0 copy-start.79
  17.6 5.0 copy-start.81
  17.6 5.0 copy-start.83
  17.6 5.0 copy-start.85
  22.6 5.8 copy-start.10
  31.2 6.4 copy-start.59
  36.4 5.4 copy-start.38
  37.9 165.1 %copy-start.18 = (f32[128,8,2,128]{3,0,2,1:T(8,128)}, f32[128,8,2,128]{3,0,2,1:T(8,128)S(1)}, u32[]{:S(2)}) copy-start(f32[128,8,2,128]{3,0,2,1:T(8,128)S(1)} %broadcast_in_dim.266) | copy-start | bytes 3145732
  203.7 7.9 copy-start.6
  206.8 4.8 copy-start.22
  229.2 4.2 collective-permute-start.2
  234.6 15.3 %collective-permute-start.3 = (f32[16,128,128]{2,1,0:T(8,128)S(1)}, f32[16,128,128]{2,1,0:T(8,128)S(1)}, u32[]{:S(2)}, u32[]{:S(2)}) collective-permute-start(f32[16,128,128]{2,1,0:T(8,128)S(1)} %convolution_add_fusion.25), channel_id=1, source_target_pairs={{0,1},{1,2},{2,3},{3,4},{4,5},{5,6},{6,7},{7,8},{8,9},{9,10},{10,1... | collective-permute-start | bytes 3145736 | tf_op jit(solution)/shard_map/ppermute | solution.py:20
  251.0 16.1 %collective-permute-start.4 = (f32[16,128,128]{2,1,0:T(8,128)S(1)}, f32[16,128,128]{2,1,0:T(8,128)S(1)}, u32[]{:S(2)}, u32[]{:S(2)}) collective-permute-start(f32[16,128,128]{2,1,0:T(8,128)S(1)} %convolution_add_fusion.24), channel_id=1, source_target_pairs={{0,1},{1,2},{2,3},{3,4},{4,5},{5,6},{6,7},{7,8},{8,9},{9,10},{10,1... | collective-permute-start | bytes 3145736 | tf_op jit(solution)/shard_map/ppermute | solution.py:20
  268.4 16.1 %collective-permute-start.5 = (f32[16,128,128]{2,1,0:T(8,128)S(1)}, f32[16,128,128]{2,1,0:T(8,128)S(1)}, u32[]{:S(2)}, u32[]{:S(2)}) collective-permute-start(f32[16,128,128]{2,1,0:T(8,128)S(1)} %convolution_add_fusion.23), channel_id=1, source_target_pairs={{0,1},{1,2},{2,3},{3,4},{4,5},{5,6},{6,7},{7,8},{8,9},{9,10},{10,1... | collective-permute-start | bytes 3145736 | tf_op jit(solution)/shard_map/ppermute | solution.py:20
  285.7 16.1 %collective-permute-start.6 = (f32[16,128,128]{2,1,0:T(8,128)S(1)}, f32[16,128,128]{2,1,0:T(8,128)S(1)}, u32[]{:S(2)}, u32[]{:S(2)}) collective-permute-start(f32[16,128,128]{2,1,0:T(8,128)S(1)} %convolution_add_fusion.22), channel_id=1, source_target_pairs={{0,1},{1,2},{2,3},{3,4},{4,5},{5,6},{6,7},{7,8},{8,9},{9,10},{10,1... | collective-permute-start | bytes 3145736 | tf_op jit(solution)/shard_map/ppermute | solution.py:20
  303.0 16.1 %collective-permute-start.7 = (f32[16,128,128]{2,1,0:T(8,128)S(1)}, f32[16,128,128]{2,1,0:T(8,128)S(1)}, u32[]{:S(2)}, u32[]{:S(2)}) collective-permute-start(f32[16,128,128]{2,1,0:T(8,128)S(1)} %convolution_add_fusion.21), channel_id=1, source_target_pairs={{0,1},{1,2},{2,3},{3,4},{4,5},{5,6},{6,7},{7,8},{8,9},{9,10},{10,1... | collective-permute-start | bytes 3145736 | tf_op jit(solution)/shard_map/ppermute | solution.py:20
  320.4 32.3 %copy-start.76 = (bf16[1,128,2048]{2,1,0:T(8,128)(2,1)S(1)}, bf16[1,128,2048]{2,1,0:T(8,128)(2,1)}, u32[]{:S(2)}) copy-start(bf16[1,128,2048]{2,1,0:T(8,128)(2,1)} %param.21) | copy-start | bytes 1572868
  320.4 16.2 %collective-permute-start.8 = (f32[16,128,128]{2,1,0:T(8,128)S(1)}, f32[16,128,128]{2,1,0:T(8,128)S(1)}, u32[]{:S(2)}, u32[]{:S(2)}) collective-permute-start(f32[16,128,128]{2,1,0:T(8,128)S(1)} %convolution_add_fusion.20), channel_id=1, source_target_pairs={{0,1},{1,2},{2,3},{3,4},{4,5},{5,6},{6,7},{7,8},{8,9},{9,10},{10,1... | collective-permute-start | bytes 3145736 | tf_op jit(solution)/shard_map/ppermute | solution.py:20
  338.7 25.2 %collective-permute-start.9 = (f32[16,128,128]{2,1,0:T(8,128)}, f32[16,128,128]{2,1,0:T(8,128)S(1)}, u32[]{:S(2)}, u32[]{:S(2)}) collective-permute-start(f32[16,128,128]{2,1,0:T(8,128)} %convolution_add_fusion.19), channel_id=1, source_target_pairs={{0,1},{1,2},{2,3},{3,4},{4,5},{5,6},{6,7},{7,8},{8,9},{9,10},{10,1... | collective-permute-start | bytes 3145736 | tf_op jit(solution)/shard_map/ppermute | solution.py:20
  382.4 4.4 copy-start.4
  387.0 4.7 copy-start.37
  395.6 4.4 copy-start.64
  404.2 4.7 copy-start.37
  412.8 4.4 copy-start.64
  423.7 7.2 collective-permute-start.10
  432.8 18.2 %collective-permute-start.11 = (f32[16,128,128]{2,1,0:T(8,128)S(1)}, f32[16,128,128]{2,1,0:T(8,128)S(1)}, u32[]{:S(2)}, u32[]{:S(2)}) collective-permute-start(f32[16,128,128]{2,1,0:T(8,128)S(1)} %convolution_add_fusion.17), channel_id=1, source_target_pairs={{1,0},{2,1},{3,2},{4,3},{5,4},{6,5},{7,6},{8,7},{9,8},{10,9},{11,1... | collective-permute-start | bytes 3145736 | tf_op jit(solution)/shard_map/ppermute | solution.py:20
  452.9 16.1 %collective-permute-start.12 = (f32[16,128,128]{2,1,0:T(8,128)S(1)}, f32[16,128,128]{2,1,0:T(8,128)S(1)}, u32[]{:S(2)}, u32[]{:S(2)}) collective-permute-start(f32[16,128,128]{2,1,0:T(8,128)S(1)} %convolution_add_fusion.16), channel_id=1, source_target_pairs={{1,0},{2,1},{3,2},{4,3},{5,4},{6,5},{7,6},{8,7},{9,8},{10,9},{11,1... | collective-permute-start | bytes 3145736 | tf_op jit(solution)/shard_map/ppermute | solution.py:20
  470.9 16.1 %collective-permute-start.13 = (f32[16,128,128]{2,1,0:T(8,128)S(1)}, f32[16,128,128]{2,1,0:T(8,128)S(1)}, u32[]{:S(2)}, u32[]{:S(2)}) collective-permute-start(f32[16,128,128]{2,1,0:T(8,128)S(1)} %convolution_add_fusion.15), channel_id=1, source_target_pairs={{1,0},{2,1},{3,2},{4,3},{5,4},{6,5},{7,6},{8,7},{9,8},{10,9},{11,1... | collective-permute-start | bytes 3145736 | tf_op jit(solution)/shard_map/ppermute | solution.py:20
  488.9 16.1 %collective-permute-start.14 = (f32[16,128,128]{2,1,0:T(8,128)S(1)}, f32[16,128,128]{2,1,0:T(8,128)S(1)}, u32[]{:S(2)}, u32[]{:S(2)}) collective-permute-start(f32[16,128,128]{2,1,0:T(8,128)S(1)} %convolution_add_fusion.14), channel_id=1, source_target_pairs={{1,0},{2,1},{3,2},{4,3},{5,4},{6,5},{7,6},{8,7},{9,8},{10,9},{11,1... | collective-permute-start | bytes 3145736 | tf_op jit(solution)/shard_map/ppermute | solution.py:20
  506.9 16.1 %collective-permute-start.15 = (f32[16,128,128]{2,1,0:T(8,128)S(1)}, f32[16,128,128]{2,1,0:T(8,128)S(1)}, u32[]{:S(2)}, u32[]{:S(2)}) collective-permute-start(f32[16,128,128]{2,1,0:T(8,128)S(1)} %convolution_add_fusion.13), channel_id=1, source_target_pairs={{1,0},{2,1},{3,2},{4,3},{5,4},{6,5},{7,6},{8,7},{9,8},{10,9},{11,1... | collective-permute-start | bytes 3145736 | tf_op jit(solution)/shard_map/ppermute | solution.py:20
  525.0 20.6 %copy-start.75 = (bf16[2,16,64,128]{3,2,1,0:T(8,128)(2,1)S(1)}, bf16[2,16,64,128]{3,2,1,0:T(8,128)(2,1)}, u32[]{:S(2)}) copy-start(bf16[2,16,64,128]{3,2,1,0:T(8,128)(2,1)} %get-tuple-element.728) | copy-start | bytes 1572868
  525.0 16.2 %collective-permute-start.16 = (f32[16,128,128]{2,1,0:T(8,128)S(1)}, f32[16,128,128]{2,1,0:T(8,128)S(1)}, u32[]{:S(2)}, u32[]{:S(2)}) collective-permute-start(f32[16,128,128]{2,1,0:T(8,128)S(1)} %convolution_add_fusion.12), channel_id=1, source_target_pairs={{1,0},{2,1},{3,2},{4,3},{5,4},{6,5},{7,6},{8,7},{9,8},{10,9},{11,1... | collective-permute-start | bytes 3145736 | tf_op jit(solution)/shard_map/ppermute | solution.py:20
  544.1 16.3 %collective-permute-start.17 = (f32[16,128,128]{2,1,0:T(8,128)}, f32[16,128,128]{2,1,0:T(8,128)S(1)}, u32[]{:S(2)}, u32[]{:S(2)}) collective-permute-start(f32[16,128,128]{2,1,0:T(8,128)} %convolution_add_fusion.11), channel_id=1, source_target_pairs={{1,0},{2,1},{3,2},{4,3},{5,4},{6,5},{7,6},{8,7},{9,8},{10,9},{11,1... | collective-permute-start | bytes 3145736 | tf_op jit(solution)/shard_map/ppermute | solution.py:20
  561.6 4.5 copy-start.1
  567.3 4.8 copy-start.21
  583.2 4.8 copy-start.21
  636.2 9.9 %copy-start.80 = (f32[1,4096]{1,0:T(1,128)S(1)}, f32[1,4096]{1,0:T(1,128)}, u32[]{:S(2)}) copy-start(f32[1,4096]{1,0:T(1,128)} %copy-done.79) | copy-start | bytes 49156
  636.2 9.9 %copy-start.82 = (f32[1,4096]{1,0:T(1,128)S(1)}, f32[1,4096]{1,0:T(1,128)}, u32[]{:S(2)}) copy-start(f32[1,4096]{1,0:T(1,128)} %copy-done.81) | copy-start | bytes 49156
  636.2 9.9 %copy-start.84 = (f32[1,4096]{1,0:T(1,128)S(1)}, f32[1,4096]{1,0:T(1,128)}, u32[]{:S(2)}) copy-start(f32[1,4096]{1,0:T(1,128)} %copy-done.83) | copy-start | bytes 49156
  636.2 9.9 %copy-start.86 = (f32[1,4096]{1,0:T(1,128)S(1)}, f32[1,4096]{1,0:T(1,128)}, u32[]{:S(2)}) copy-start(f32[1,4096]{1,0:T(1,128)} %copy-done.85) | copy-start | bytes 49156
  654.8 14.7 %collective-permute-start.18 = (bf16[3,4096]{1,0:T(4,128)(2,1)S(1)}, bf16[3,4096]{1,0:T(4,128)(2,1)S(1)}, u32[]{:S(2)}, u32[]{:S(2)}) collective-permute-start(bf16[3,4096]{1,0:T(4,128)(2,1)S(1)} %copy.271), channel_id=1, source_target_pairs={{1,0},{2,1},{3,2},{4,3},{5,4},{6,5},{7,6},{8,7},{9,8},{10,9},{11,1... | collective-permute-start | bytes 73736 | tf_op jit(solution)/shard_map/ppermute | solution.py:20
  (117 other events, 282.1 us)
Sparse Core Ops, SparseCore 0:
  657.0 143.5 all-reduce.16
where the time goes:
time: 819 us; the launch traced here: 809 us
  waiting for transfers between devices  250 us (31%)
  other arithmetic  208 us (25%)
  matrix products  131 us (16%)
  starting transfers between devices  118 us (14%)
  local copies, waits for them, and re-layouts  84 us (10%)
  between operations  15.6 us (2%)
    another operation x4, other arithmetic, prepare(): jax.scipy.linalg.solve_triangular(triangle, right_side, lower=True, unit_...  158 us
    ppermute x19, waiting for transfers between devices, passed_along(): return lax.ppermute(array, axis, pairs)  135 us
    ppermute x19, starting transfers between devices, passed_along(): return lax.ppermute(array, axis, pairs)  118 us
    psum x1, waiting for transfers between devices, local(): total_weight = lax.psum(grad_weight, ('dp', 'seq'))  116 us
    dot_general x16, matrix products, advance(): jnp.einsum('hij,hjk->hik', transition, carried, precision=highest_precision)  26.3 us
    dot_general x10, matrix products, advance_block(): jnp.einsum('uab,ubf->uaf', woodbury_keys, memory_state, precision=highest...  20.2 us
    dot_general x10, matrix products, advance_block(): jnp.einsum('qno,qnb->qob', key_result, delta_update, precision=highest_pr...  18.3 us
    dot_general x10, matrix products, advance_block(): jnp.einsum('uab,ubf->uaf', query_entering, memory_state, precision=highes...  18.3 us
  transfers between devices with their start and end apart: 20, of which 17 were waited for; matrix products, arithmetic and copies ran while one was open for 5% of the time, Pallas kernels for 0%

commit v1 on v0

v1 whole, which is shorter than its diff:
```python
import functools

import jax
import jax.numpy as jnp
from jax import lax
from jax.experimental import pallas as pl
from jax.experimental.pallas import tpu as pltpu
from jax.sharding import PartitionSpec as P

DK = 128
DOC_MOST = 1024
EPS = 1e-6
RIM = 16
f32 = jnp.float32
bf16 = jnp.bfloat16


def dg(a, b, ca, cb):
    return lax.dot_general(a, b, (((ca,), (cb,)), ((), ())), preferred_element_type=f32)


def split(x):
    hi = x.astype(bf16)
    return (hi, (x - hi.astype(f32)).astype(bf16))


def cat(parts, axis):
    return tuple(jnp.concatenate(leaves, axis) for leaves in zip(*parts))


def mm(a, b, ca, cb):
    out = dg(a[0], b[0], ca, cb)
    if len(b) > 1:
        out = out + dg(a[0], b[1], ca, cb)
    if len(a) > 1:
        out = out + dg(a[1], b[0], ca, cb)
    return out


def iota2(shape, dim):
    return lax.broadcasted_iota(jnp.int32, shape, dim)


def conv_inputs(x_ref, n, shift_ref, docs):
    length = docs.shape[0]
    shift_ref[5:8, :] = x_ref[n, length : length + 3, :].astype(f32)
    rows = x_ref[n, :length, :].astype(f32)
    shift_ref[8 : 8 + length, :] = rows
    at = iota2((length, DK), 0)
    first = docs[0:1, :]
    taps = [rows]
    for off in (1, 2, 3):
        earlier = jnp.where(at >= off, pltpu.roll(docs, off, 0), first)
        ok = earlier == docs
        moved = shift_ref[8 - off : 8 - off + length, :]
        width = moved.shape[1] // DK
        taps.append(jnp.where(jnp.concatenate([ok] * width, 1), moved, 0.0))
    return taps


def conv_out(taps, w):
    return sum(w[3 - off : 4 - off, :] * taps[off] for off in range(4))


def heads_of(z):
    sig = 1.0 / (1.0 + jnp.exp(-z))
    act = z * sig
    q, k, v = act[:, :DK], act[:, DK : 2 * DK], act[:, 2 * DK :]
    rq = lax.rsqrt(jnp.sum(q * q, -1, keepdims=True) + EPS)
    rk = lax.rsqrt(jnp.sum(k * k, -1, keepdims=True) + EPS)
    return sig, q * rq, k * rk, v, rq, rk


class Meta:
    def __init__(self, numbers, per_key):
        length = numbers.shape[1]
        rows = numbers.astype(f32)
        row_at = iota2((RIM, DK), 0)
        i, j = iota2((length, length), 0), iota2((length, length), 1)
        self.lower, self.strict = i >= j, i > j

        def column(first, count):
            pick = ((row_at >= first) & (row_at < first + count)).astype(f32).astype(bf16)
            return dg(numbers, pick, 0, 0)

        self.docs = column(3, 1)
        doc_row = rows[3:4]
        self.same = (self.docs == doc_row) & self.lower
        carry = (self.docs > 0) & (self.docs == doc_row[:, 0:1])
        ending = self.docs == doc_row[:, length - 1 : length]
        until = (i <= j).astype(f32).astype(bf16)
        row_sums = dg(numbers, until, 1, 0)
        ones = jnp.ones((length, DK), bf16)
        self.c_row, self.c_col, self.beta, self.beta_row = [], [], [], []
        self.entry, self.tail, self.keep = [], [], []
        for h in range(per_key):
            at = 4 + 3 * h
            self.c_row.append(row_sums[at : at + 1] + row_sums[at + 1 : at + 2] + row_sums[at + 2 : at + 3])
            c_col = 0.0
            for part in (2, 1, 0):
                c_col = c_col + dg(jnp.where(self.lower, rows[at + part : at + part + 1], 0.0).astype(bf16), ones, 1, 0)
            self.c_col.append(c_col)
            at = 4 + 3 * per_key + 3 * h
            self.beta.append(column(at, 3))
            self.beta_row.append(rows[at : at + 1] + rows[at + 1 : at + 2] + rows[at + 2 : at + 3])
            self.entry.append(jnp.where(carry, jnp.exp(c_col), 0.0))
            last = self.c_row[h][:, length - 1 : length]
            self.tail.append(jnp.where(ending, jnp.exp(jnp.minimum(last - c_col, 0.0)), 0.0))
            self.keep.append(self.entry[h][length - 1 : length, :])

    def fading(self, h):
        gap = jnp.minimum(self.c_col[h] - self.c_row[h], 0.0)
        return jnp.where(self.same, jnp.exp(gap), 0.0)


def inverse(mats):
    length = mats[0].shape[0]
    i, j = iota2((length, length), 0), iota2((length, length), 1)
    eye = (i == j).astype(f32)
    inner = [jnp.where((i // 8) == (j // 8), n, 0.0) for n in mats]
    s1 = [split(n) for n in inner]
    s2 = [split(mm(a, a, 1, 0)) for a in s1]
    low = [eye - n + (a[0].astype(f32) + a[1].astype(f32)) - mm(b, a, 1, 0) for n, a, b in zip(inner, s2, s1)]
    s4 = [split(mm(a, a, 1, 0)) for a in s2]
    inv = [t + mm(split(t), a, 1, 0) for t, a in zip(low, s4)]
    width = 8
    while width < length:
        cross = ((i // (2 * width)) == (j // (2 * width))) & ((i // width) > (j // width))
        st = [split(t) for t in inv]
        half = [mm(split(jnp.where(cross, n, 0.0)), t, 1, 0) for n, t in zip(mats, st)]
        inv = [t - mm(s, split(x), 1, 0) for t, s, x in zip(inv, st, half)]
        width *= 2
    return inv


def rows_from(x):
    ones = jnp.ones((8, x.shape[1]), bf16)
    return mm((ones,), split(x), 1, 1)[0:1]


def first_kernel(per_key, count, x_ref, og_ref, w_ref, q_ref, k_ref, f_ref, n_ref, p_ref, t_ref, w_out, u_ref,
                 y_ref, pu_ref, r_ref, a_ref, b_ref, g_ref, fwd_ref, bwd_ref, shift_ref, a_all, g_all):
    step = pl.program_id(0)
    steps = pl.num_programs(0)
    length = og_ref.shape[1]
    eye = (iota2((DK, DK), 0) == iota2((DK, DK), 1)).astype(f32)

    @pl.when(step == 0)
    def _():
        fwd_ref[...] = jnp.zeros_like(fwd_ref)

    w = w_ref[...]
    pairs = [(n, h) for n in range(count) for h in range(per_key)]
    metas, qs, ks, vs = [], [], [], []
    for n in range(count):
        meta = Meta(x_ref[n, length:, DK : 2 * DK], per_key)
        taps = conv_inputs(x_ref, n, shift_ref.at[n], meta.docs)
        _, q, k, v, _, _ = heads_of(conv_out(taps, w))
        q = q * DK**-0.5
        q_ref[n], k_ref[n] = q, k
        metas.append(meta)
        qs.append(q)
        ks.append(k)
        vs.append(v)
    sk = [split(k) for k in ks]
    both = [mm(cat([s, split(q)], 0), s, 1, 1) for s, q in zip(sk, qs)]
    fs = [metas[n].fading(h) for n, h in pairs]
    ns = [jnp.where(metas[n].strict, metas[n].beta[h] * both[n][:length] * f, 0.0) for (n, h), f in zip(pairs, fs)]
    ps = [both[n][length:] * f for (n, h), f in zip(pairs, fs)]
    for (n, h), f, nn, p in zip(pairs, fs, ns, ps):
        f_ref[n, h], n_ref[n, h], p_ref[n, h] = f, nn, p
    ts = inverse(ns)
    rhs = [
        jnp.concatenate([metas[n].beta[h] * metas[n].entry[h] * ks[n], metas[n].beta[h] * vs[n][:, h * DK : (h + 1) * DK]], 1)
        for n, h in pairs
    ]
    wu = [mm(split(t), split(r), 1, 0) for t, r in zip(ts, rhs)]
    swu = [split(x) for x in wu]
    sp = [split(p) for p in ps]
    kwu = [mm(split(metas[n].tail[h] * ks[n]), s, 0, 0) for (n, h), s in zip(pairs, swu)]
    pwu = [mm(p, s, 1, 0) for p, s in zip(sp, swu)]
    ys = [metas[n].entry[h] * qs[n] - x[:, :DK] for (n, h), x in zip(pairs, pwu)]
    dos = [(og_ref[n, :, h * DK : (h + 1) * DK],) for n, h in pairs]
    gs = [mm(split(y), d, 0, 0) for y, d in zip(ys, dos)]
    rs = [mm(p, d, 0, 0) for p, d in zip(sp, dos)]
    for m, (n, h) in enumerate(pairs):
        a = metas[n].keep[h] * eye - kwu[m][:, :DK]
        t_ref[n, h], w_out[n, h], u_ref[n, h] = ts[m], wu[m][:, :DK], wu[m][:, DK:]
        y_ref[n, h], pu_ref[n, h], r_ref[n, h] = ys[m], pwu[m][:, DK:], rs[m]
        a_ref[n, h], b_ref[n, h], g_ref[n, h] = a, kwu[m][:, DK:], gs[m]
        a_all[step * count + n, h], g_all[step * count + n, h] = a, gs[m]
        fwd_ref[h] = mm(split(a), split(fwd_ref[h]), 1, 0) + kwu[m][:, DK:]

    @pl.when(step == steps - 1)
    def _():
        blocks = a_all.shape[0]

        def back(s, states):
            n = blocks - 1 - s
            return tuple(
                mm(split(a_all[n, h]), split(states[h]), 0, 0) + g_all[n, h] for h in range(per_key)
            )

        states = lax.fori_loop(0, blocks, back, tuple(jnp.zeros((DK, DK), f32) for h in range(per_key)))
        for h in range(per_key):
            bwd_ref[h] = states[h]


def second_kernel(per_key, count, in_ref, w_ref, u_ref, y_ref, pu_ref, a_ref, b_ref, o_ref, d_ref, s_ref, state):
    @pl.when(pl.program_id(0) == 0)
    def _():
        state[...] = in_ref[...]

    length = w_ref.shape[2]
    for n in range(count):
        for h in range(per_key):
            now = state[h]
            s_ref[n, h] = now
            sn = split(now)
            both = mm(cat([split(w_ref[n, h]), split(y_ref[n, h]), split(a_ref[n, h])], 0), sn, 1, 0)
            d_ref[n, h] = u_ref[n, h] - both[:length]
            o_ref[n, :, h * DK : (h + 1) * DK] = (both[length : 2 * length] + pu_ref[n, h]).astype(bf16)
            state[h] = both[2 * length :] + b_ref[n, h]


def third_kernel(per_key, count, in_ref, x_ref, og_ref, w_ref, q_ref, k_ref, f_ref, n_ref, p_ref, t_ref, r_ref, a_ref,
                 g_ref, d_ref, s_ref, dx_ref, gates_ref, rim_ref, dw_ref, state, shift_ref, dz_ref, doc_next):
    step = pl.program_id(0)

    @pl.when(step == 0)
    def _():
        state[...] = in_ref[...]
        dw_ref[...] = jnp.zeros_like(dw_ref)
        dz_ref[...] = jnp.zeros_like(dz_ref)
        doc_next[...] = jnp.zeros_like(doc_next)

    w = w_ref[...]
    length = og_ref.shape[1]
    i, j = iota2((length, length), 0), iota2((length, length), 1)
    from_here = (i >= j).astype(f32).astype(bf16)
    for n in reversed(range(count)):
        meta = Meta(x_ref[n, length:, DK : 2 * DK], per_key)
        taps = conv_inputs(x_ref, n, shift_ref, meta.docs)
        z = conv_out(taps, w)
        sig, q_hat, k_hat, v, rq, rk = heads_of(z)
        q, k = q_ref[n], k_ref[n]
        sq, sk = split(q), split(k)
        dq, dk = jnp.zeros_like(q), jnp.zeros_like(k)
        dvs = []
        for h in range(per_key):
            beta, entry, tail = meta.beta[h], meta.entry[h], meta.tail[h]
            later = state[h]
            s_later, s_state, s_d = split(later), split(s_ref[n, h]), split(d_ref[n, h])
            do = (og_ref[n, :, h * DK : (h + 1) * DK],)
            v_h = v[:, h * DK : (h + 1) * DK]
            f = f_ref[n, h]
            x1 = mm(split(tail * k), s_later, 1, 0)
            e = mm(split(t_ref[n, h]), split(r_ref[n, h] + x1), 0, 0)
            se = split(e)
            dp = mm(do, s_d, 1, 1)
            dn = -mm(se, s_d, 1, 1)
            dos = mm(do, s_state, 1, 1)
            es = mm(se, s_state, 1, 1)
            dds = mm(s_d, s_later, 1, 1)
            dpf = dp * f
            dkk = jnp.where(meta.strict, dn * beta * f, 0.0)
            s_dpf, s_dkk = split(dpf), split(dkk)
            dqk = mm(cat([s_dpf, s_dkk], 0), sk, 1, 0)
            ends = tail * dds
            enter = entry * dos
            bes = beta * entry * es
            dq = dq + enter + dqk[:length]
            dk = dk + dqk[length:] + mm(cat([s_dpf, s_dkk], 0), cat([sq, sk], 0), 0, 0) - bes + ends
            dvs.append(beta * e)
            nn = dn * n_ref[n, h]
            gaps = dp * p_ref[n, h] + nn
            ek = ends * k
            dc = rows_from(gaps + enter * q - bes * k - ek) - jnp.sum(gaps, 0, keepdims=True)
            at_end = jnp.sum(jnp.sum(ek, 0, keepdims=True), 1, keepdims=True) + jnp.sum(
                jnp.sum(later * s_ref[n, h] * meta.keep[h], 0, keepdims=True), 1, keepdims=True
            )
            dc = jnp.broadcast_to(dc, (8, length))
            d_decay = mm(split(dc), (from_here,), 1, 0)[0:1] + at_end
            d_beta = rows_from(e * v_h - entry * es * k) + rows_from(nn) / meta.beta_row[h]
            gates_ref[n, h : h + 1, :] = d_decay
            gates_ref[n, per_key + h : per_key + h + 1, :] = d_beta
            state[h] = mm(split(a_ref[n, h]), s_later, 0, 0) + g_ref[n, h]
        dq_act = (DK**-0.5) * rq * (dq - q_hat * jnp.sum(dq * q_hat, -1, keepdims=True))
        dk_act = rk * (dk - k_hat * jnp.sum(dk * k_hat, -1, keepdims=True))
        d_act = jnp.concatenate([dq_act, dk_act] + dvs, 1)
        dz = d_act * (sig + z * sig * (1.0 - sig))
        dz_ref[8 + length :, :] = dz_ref[8 : 16, :]
        dz_ref[8 : 8 + length, :] = dz
        docs_after = doc_next[...]
        at = iota2((length, DK), 0)
        dx = w[3:4, :] * dz
        width = dz.shape[1] // DK
        for off in (1, 2, 3):
            ahead = pltpu.roll(meta.docs, length - off, 0)
            for r in range(off):
                ahead = jnp.where(at == length - off + r, docs_after[r : r + 1, :], ahead)
            ok = jnp.abs(ahead) == jnp.abs(meta.docs)
            dx = dx + w[3 - off : 4 - off, :] * jnp.where(
                jnp.concatenate([ok] * width, 1), dz_ref[8 + off : 8 + off + length, :], 0.0
            )
        doc_next[...] = meta.docs[0:8, :]
        dx_ref[n] = dx.astype(bf16)
        for off in range(4):
            dw_ref[3 - off : 4 - off, :] += jnp.sum(dz * taps[off], 0, keepdims=True)
        head = jnp.where(
            jnp.concatenate([meta.docs[0:8, :] == meta.docs[0:1, :]] * width, 1), dz[0:8, :], 0.0
        )
        rims = []
        for r in range(3):
            total = 0.0
            for off in range(3 - r, 4):
                total = total + w[3 - off : 4 - off, :] * head[r + off - 3 : r + off - 2, :]
            rims.append(total)
        rim_ref[...] = jnp.concatenate(rims + [jnp.zeros((5, dz.shape[1]), f32)], 0)


def three(x):
    hi = lax.reduce_precision(x, 8, 7)
    mid = lax.reduce_precision(x - hi, 8, 7)
    return jnp.stack([hi, mid, x - hi - mid], -2).astype(bf16)


def local(mixed, conv_weight, log_decay, beta, doc_ids, out_grad):
    n_seq, n_dp = lax.axis_size("seq"), lax.axis_size("dp")
    rows, docs, og = mixed[0], doc_ids[0], out_grad[0]
    length, channels = rows.shape
    heads = log_decay.shape[1]
    key_heads = (channels - heads * DK) // (2 * DK)
    per_key = heads // key_heads
    G = key_heads
    assert n_seq % G == 0 and G * length >= DOC_MOST
    member = lax.axis_index("seq") % G
    team = [list(range(s, s + G)) for s in range(0, n_seq, G)]
    own = 2 * DK + per_key * DK

    def shifted(x, by):
        return lax.ppermute(x, "seq", [(s, s + by) for s in range(n_seq) if 0 <= s + by < n_seq])

    def by_member(x):
        lead = x.shape[:-1]
        parts = (x[..., : G * DK], x[..., G * DK : 2 * G * DK], x[..., 2 * G * DK :])
        return jnp.concatenate([jnp.moveaxis(y.reshape(lead + (G, -1)), -2, 0) for y in parts], -1)

    def to_channels(x):
        parts = (x[..., :DK], x[..., DK : 2 * DK], x[..., 2 * DK :])
        return jnp.concatenate(
            [jnp.moveaxis(y, 0, -2).reshape(x.shape[1:-1] + (-1,)) for y in parts], -1
        )

    def swap(x):
        return lax.all_to_all(x, "seq", 0, 0, axis_index_groups=team)

    rim_rows, rim_docs = shifted((rows[-3:], docs[-3:]), 1)
    doc_after = shifted(docs[:1], -1)
    rim_rows = jnp.where((rim_docs == docs[0])[:, None], rim_rows, 0)
    signed = jnp.where(rim_docs[-1] == docs[0], docs + 1, -docs - 1).astype(bf16)
    numbers = jnp.concatenate(
        [
            jnp.broadcast_to(signed, (G, 1, length)),
            three(log_decay[0].reshape(G, per_key, length)).reshape(G, -1, length),
            three(beta[0].reshape(G, per_key, length)).reshape(G, -1, length),
        ],
        1,
    )
    numbers = jnp.pad(numbers, ((0, 0), (0, 0), (DK, per_key * DK)))
    packed = jnp.concatenate([by_member(rows), by_member(rim_rows), numbers], 1)
    x = swap(packed)
    og_in = swap(jnp.moveaxis(og.reshape(length, G, per_key * DK), 1, 0))
    weight = lax.dynamic_index_in_dim(by_member(conv_weight.astype(f32)), member, 0, keepdims=False)

    count = 2
    steps = G // count
    pair = (per_key, DK, DK)

    def spec(shape, back=False):
        if back:
            return pl.BlockSpec((count,) + shape, lambda s: (steps - 1 - s,) + (0,) * len(shape))
        return pl.BlockSpec((count,) + shape, lambda s: (s,) + (0,) * len(shape))

    def full(shape):
        return pl.BlockSpec(shape, lambda s: (0,) * len(shape))

    def out(shape):
        return jax.ShapeDtypeStruct((G,) + shape, f32)

    params = pltpu.CompilerParams(vmem_limit_bytes=48 << 20)
    first = pl.pallas_call(
        functools.partial(first_kernel, per_key, count),
        grid=(steps,),
        in_specs=[spec((length + RIM, own)), spec((length, per_key * DK)), full((4, own))],
        out_specs=[spec((length, DK))] * 2 + [spec(pair)] * 12 + [full(pair)] * 2,
        out_shape=[out((length, DK))] * 2 + [out(pair)] * 12 + [jax.ShapeDtypeStruct(pair, f32)] * 2,
        scratch_shapes=[
            pltpu.VMEM((count, 8 + length, own), f32),
            pltpu.VMEM((G,) + pair, f32),
            pltpu.VMEM((G,) + pair, f32),
        ],
        compiler_params=params,
        name="blocks",
    )
    q, k, f, n, p, t, w_out, u, y, pu, r, a, b, g, fwd, bwd = first(x, og_in, weight)
    state_in = shifted(fwd, G)
    back_in = shifted(bwd, -G)
    o, d, s = pl.pallas_call(
        functools.partial(second_kernel, per_key, count),
        grid=(steps,),
        in_specs=[full(pair)] + [spec(pair)] * 6,
        out_specs=[spec((length, per_key * DK)), spec(pair), spec(pair)],
        out_shape=[jax.ShapeDtypeStruct((G, length, per_key * DK), bf16), out(pair), out(pair)],
        scratch_shapes=[pltpu.VMEM(pair, f32)],
        compiler_params=params,
        name="read",
    )(state_in, w_out, u, y, pu, a, b)
    dx, gates, rim, dw = pl.pallas_call(
        functools.partial(third_kernel, per_key, count),
        grid=(steps,),
        in_specs=[full(pair), spec((length + RIM, own), True), spec((length, per_key * DK), True), full((4, own))]
        + [spec((length, DK), True)] * 2
        + [spec(pair, True)] * 9,
        out_specs=[spec((length, own), True), spec((2 * per_key, length), True), full((8, own)), full((4, own))],
        out_shape=[
            jax.ShapeDtypeStruct((G, length, own), bf16),
            out((2 * per_key, length)),
            jax.ShapeDtypeStruct((8, own), f32),
            jax.ShapeDtypeStruct((4, own), f32),
        ],
        scratch_shapes=[
            pltpu.VMEM(pair, f32),
            pltpu.VMEM((8 + length, own), f32),
            pltpu.VMEM((16 + length, own), f32),
            pltpu.VMEM((8, DK), f32),
        ],
        compiler_params=params,
        name="gradients",
    )(back_in, x, og_in, weight, q, k, f, n, p, t, r, a, g, d, s)

    output = jnp.moveaxis(swap(o), 0, 1).reshape(length, -1)
    d_rows = to_channels(swap(dx))
    gates = swap(gates)
    rim = rim[:3].astype(bf16)
    pieces = [
        lax.ppermute(rim, "seq", [(s + m, s - 1) for s in range(G, n_seq, G)]) for m in range(G)
    ]
    incoming = to_channels(jnp.stack(pieces))
    incoming = jnp.where((docs[-3:] == doc_after)[:, None], incoming, 0).astype(f32)
    d_tail = (d_rows[-3:].astype(f32) + incoming).astype(bf16)
    d_rows = jnp.concatenate([d_rows[:-3], d_tail], 0)
    step = 1
    while step < n_dp:
        dw = dw + lax.ppermute(dw, "dp", [(s, s ^ step) for s in range(n_dp)])
        step *= 2
    step = G
    while step < n_seq:
        dw = dw + lax.ppermute(dw, "seq", [(s, s ^ step) for s in range(n_seq)])
        step *= 2
    gathered = jnp.zeros((G,) + dw.shape, f32)
    for m in range(G):
        piece = lax.ppermute(dw, "seq", [(s, s ^ m) for s in range(n_seq)]) if m else dw
        gathered = lax.dynamic_update_index_in_dim(gathered, piece, member ^ m, 0)
    d_weight = to_channels(gathered)
    d_decay = gates[:, :per_key].reshape(heads, length)
    d_beta = gates[:, per_key:].reshape(heads, length)
    return (output[None], d_rows[None], d_weight, d_decay[None], d_beta[None])


def solution(mesh):
    in_specs = (
        P("dp", "seq", None),
        P(),
        P("dp", None, "seq"),
        P("dp", None, "seq"),
        P("dp", "seq"),
        P("dp", "seq", None),
    )
    out_specs = (
        P("dp", "seq", None),
        P("dp", "seq", None),
        P(),
        P("dp", None, "seq"),
        P("dp", None, "seq"),
    )
    return jax.shard_map(
        local, mesh=mesh, in_specs=in_specs, out_specs=out_specs, check_vma=False
    )
```

time: 819 us -> 166 us (0.20); the launches traced: 809 us -> 165 us
  waiting for transfers between devices: 250 us -> 36.3 us
  other arithmetic: 208 us -> 4.01 us
  matrix products: 131 us -> 0 us
  local copies, waits for them, and re-layouts: 84 us -> 18.4 us
  starting transfers between devices: 118 us -> 55.4 us
  Pallas kernels: 0 us -> 49.1 us
  between operations: 15.6 us -> 2.01 us
    another operation x6 -> x4, other arithmetic: 160 us -> 0.03 us  [the longest x2 0.02 us: three(): return jnp.stack([hi, mid, x - hi - mid], -2).astype(bf16)]
    ppermute x19 -> x22, waiting for transfers between devices: 135 us -> 4.73 us  [the longest x7 2.33 us: local(): lax.ppermute(dw, 'seq', [(s, s ^ m) for s in range(n_seq)])]
    dot_general x69 -> x0, matrix products: 124 us -> none  [the longest x16 26.3 us: advance(): jnp.einsum('hij,hjk->hik', transition, carried, precision=highest_precision)]
    psum x1 -> x0, waiting for transfers between devices: 116 us -> none  [local(): total_weight = lax.psum(grad_weight, ('dp', 'seq'))]
    ppermute x19 -> x22, starting transfers between devices: 118 us -> 31.4 us  [the longest x5 13.6 us: shifted(): lax.ppermute(x, 'seq', [(s, s + by) for s in range(n_seq) if 0 <= s + by...]
    pallas_call x0 -> x3, Pallas kernels: none -> 49.1 us  [the longest x1 22.3 us: local(): first(x, og_in, weight)]
    all_to_all x0 -> x5, waiting for transfers between devices: none -> 31.6 us  [swap(): return lax.all_to_all(x, 'seq', 0, 0, axis_index_groups=team)]
    all_to_all x0 -> x5, starting transfers between devices: none -> 24 us  [swap(): return lax.all_to_all(x, 'seq', 0, 0, axis_index_groups=team)]
  transfers between devices with their start and end apart: 20 -> 27, of which waited for: 17 -> 6; matrix products, arithmetic and copies ran while one was open for 5% -> 6% of each run, Pallas kernels for 0% -> 16%
where the time goes in v1:
time: 166 us; the launch traced here: 165 us
  starting transfers between devices  55.4 us (33%)
  Pallas kernels  49.1 us (30%)
  waiting for transfers between devices  36.3 us (22%)
  local copies, waits for them, and re-layouts  18.4 us (11%)
  other arithmetic  4.01 us (2%)
  between operations  2.01 us (1%)
    all_to_all x5, waiting for transfers between devices, swap(): return lax.all_to_all(x, 'seq', 0, 0, axis_index_groups=team)  31.6 us
    all_to_all x5, starting transfers between devices, swap(): return lax.all_to_all(x, 'seq', 0, 0, axis_index_groups=team)  24 us
    pallas_call x1, Pallas kernels, local(): first(x, og_in, weight)  22.3 us
    pallas_call x1, Pallas kernels, local(): pl.pallas_call(functools.partial(third_kernel, per_key, count), grid=(ste...  21.9 us
    ppermute x5, starting transfers between devices, shifted(): lax.ppermute(x, 'seq', [(s, s + by) for s in range(n_seq) if 0 <= s + by...  13.6 us
    unnamed x43, local copies, waits for them, and re-layouts  12.1 us
    ppermute x7, starting transfers between devices, local(): lax.ppermute(dw, 'seq', [(s, s ^ m) for s in range(n_seq)])  7.51 us
    ppermute x8, starting transfers between devices, local(): lax.ppermute(rim, 'seq', [(s + m, s - 1) for s in range(G, n_seq, G)])  5.28 us
  transfers between devices with their start and end apart: 27, of which 6 were waited for; matrix products, arithmetic and copies ran while one was open for 6% of the time, Pallas kernels for 16%

profile of v1, /device:TPU:0, one launch (start us, length us, event | category | flops | bytes accessed | tf_op | source)
XLA Modules:
  0.0 165.3 jit_solution(991113297891664181)
XLA Ops:
  0.6 0.7 slice_bitcast_fusion.13
  1.4 2.3 %collective-permute-start = (s32[3]{0:T(128)S(1)}, s32[3]{0:T(128)S(1)}, u32[]{:S(2)}, u32[]{:S(2)}) collective-permute-start(s32[3]{0:T(128)S(1)} %slice_bitcast_fusion.13), channel_id=1, source_target_pairs={{0,1},{1,2},{2,3},{3,4},{4,5},{5,6},{6,7},{7,8},{8,9},{9,10},{10,1... | collective-permute-start | bytes 44 | tf_op jit(solution)/shard_map/ppermute | solution.py:342
  3.7 0.9 slice_bitcast_fusion.4
  4.6 4.5 %collective-permute-start.1 = (bf16[3,4096]{1,0:T(4,128)(2,1)S(1)}, bf16[3,4096]{1,0:T(4,128)(2,1)S(1)}, u32[]{:S(2)}, u32[]{:S(2)}) collective-permute-start(bf16[3,4096]{1,0:T(4,128)(2,1)S(1)} %slice_bitcast_fusion.4), channel_id=1, source_target_pairs={{0,1},{1,2},{2,3},{3,4},{4,5},{5,6},{6,7},{7,8},{8,9},{9,10},{10,1... | collective-permute-start | bytes 73736 | tf_op jit(solution)/shard_map/ppermute | solution.py:342
  9.1 1.3 copy.116
  10.5 1.0 copy.117
  11.5 3.8 %all-to-all-start.1 = ((bf16[8,128,256]{2,1,0:T(8,128)(2,1)}), bf16[8,128,256]{2,1,0:T(8,128)(2,1)S(1)}, u32[]{:S(2)}, u32[]{:S(2)}) async-start(bf16[8,128,256]{2,1,0:T(8,128)(2,1)} %bitcast.23), calls=%async_computation.1 | async-start | bytes 1048576 | tf_op jit(solution)/shard_map/all_to_all | solution.py:356
  15.3 0.7 copy.103
  18.8 1.2 pad_maximum_fusion
  20.0 4.1 %all-to-all-done.1.og_ref = bf16[8,128,256]{2,1,0:T(8,128)(2,1)S(1)} async-done(((bf16[8,128,256]{2,1,0:T(8,128)(2,1)}), bf16[8,128,256]{2,1,0:T(8,128)(2,1)S(1)}, u32[]{:S(2)}, u32[]{:S(2)}) %all-to-all-start.1) | async-done | bytes 524320 | tf_op jit(solution)/shard_map/all_to_all | solution.py:356
  24.1 4.3 %all-to-all-start = ((bf16[8,144,512]{2,1,0:T(8,128)(2,1)}), bf16[8,144,512]{2,1,0:T(8,128)(2,1)}, u32[]{:S(2)}, u32[]{:S(2)}) async-start(bf16[8,144,512]{2,1,0:T(8,128)(2,1)} %pad_maximum_fusion), calls=%async_computation | async-start | bytes 2359296 | tf_op jit(solution)/shard_map/all_to_all | solution.py:356
  28.5 15.8 %all-to-all-done.x_ref = bf16[8,144,512]{2,1,0:T(8,128)(2,1)} async-done(((bf16[8,144,512]{2,1,0:T(8,128)(2,1)}), bf16[8,144,512]{2,1,0:T(8,128)(2,1)}, u32[]{:S(2)}, u32[]{:S(2)}) %all-to-all-start) | async-done | bytes 1179680 | tf_op jit(solution)/shard_map/all_to_all | solution.py:356
  44.2 22.3 %blocks.1 = (f32[8,128,128]{2,1,0:T(8,128)S(1)}, f32[8,128,128]{2,1,0:T(8,128)S(1)}, f32[8,2,128,128]{3,2,1,0:T(8,128)S(1)}, f32[8,2,128,128]{3,2,1,0:T(8,128)S(...) custom-call(bf16[8,144,512]{2,1,0:T(8,128)(2,1)} %all-to-all-done.x_, ...), custom_call_target="tpu_custom_call" | custom-call | tf_op jit(solution)/shard_map/blocks/pallas_call | solution.py:406
  66.6 1.0 copy-done.3
  67.6 1.0 copy-done.5
  68.6 0.8 copy-done.8
  69.4 4.1 %collective-permute-start.2 = (f32[2,128,128]{2,1,0:T(8,128)}, f32[2,128,128]{2,1,0:T(8,128)S(1)}, u32[]{:S(2)}, u32[]{:S(2)}) collective-permute-start(f32[2,128,128]{2,1,0:T(8,128)} %get-tuple-element.28), channel_id=1, source_target_pairs={{0,8},{1,9},{2,10},{3,11},{4,12},{5,13},{6,14},{7,15},{16,24},{17,... | collective-permute-start | bytes 393224 | tf_op jit(solution)/shard_map/ppermute | solution.py:342
  73.5 1.3 collective-permute-start.3
  74.8 1.3 collective-permute-start.4
  76.4 1.2 copy-done
  77.6 1.2 copy-done.1
  78.8 1.2 copy-done.2
  80.0 4.9 %read.1 = (bf16[8,128,256]{2,1,0:T(8,128)(2,1)}, f32[8,2,128,128]{3,2,1,0:T(8,128)S(1)}, f32[8,2,128,128]{3,2,1,0:T(8,128)S(1)}) custom-call(f32[2,128,128]{2,1,0:T(8,128)S(1)} %collective-permute-done.2.in_ref, f32[8,2,128,128]{3,2,1,0:T(8,128)S(1)} %copy-done, f32[8,2,128,128]{3,2,1,0:T(8,128)S(1)} %copy-done.1, f32[8,2,128,128]{3,2,1,0:T(8,128)S(1)} %copy-done.2, ...), custom_call_target="tpu_custom_call" | custom-call | tf_op jit(solution)/shard_map/read/pallas_call | solution.py:409
  85.0 1.0 copy-done.6
  86.0 1.0 copy-done.7
  87.0 21.9 %gradients.1 = (bf16[8,128,512]{2,1,0:T(8,128)(2,1)}, f32[8,4,128]{2,1,0:T(4,128)}, f32[8,512]{1,0:T(8,128)S(1)}, f32[4,512]{1,0:T(4,128)S(1)}) custom-call(f32[2,128,128]{2,1,0:T(8,128)S(1)} %collective-permute-done.3.in_ref, bf16[8,144,512]{2,1,0:T(8,128)(2,1)} %all-to-all-done.x_ref, bf16[8,128,256]{2,1,0:T(8,128)(2,1)S(1)} %all-to-all-done.1.og_ref, ...), custom_call_target="tpu_custom_call" | custom-call | tf_op jit(solution)/shard_map/gradients/pallas_call | solution.py:419
  108.8 0.7 collective-permute-start.5
  109.5 0.7 broadcast_compare_fusion
  110.9 0.7 collective-permute-start.7
  111.5 0.7 collective-permute-start.8
  112.2 0.7 collective-permute-start.9
  112.9 7.2 %all-to-all-start.4 = ((f32[8,4,128]{2,1,0:T(4,128)}), f32[8,4,128]{2,1,0:T(4,128)S(1)}, u32[]{:S(2)}, u32[]{:S(2)}) async-start(f32[8,4,128]{2,1,0:T(4,128)} %get-tuple-element.50), calls=%async_computation.4 | async-start | bytes 32768 | tf_op jit(solution)/shard_map/all_to_all | solution.py:356
  120.0 0.7 collective-permute-start.10
  120.7 0.7 collective-permute-start.11
  121.4 0.7 collective-permute-start.12
  122.1 1.5 collective-permute-start.13
  123.7 2.1 %collective-permute-done.13 = f32[4,512]{1,0:T(4,128)S(1)} collective-permute-done((f32[4,512]{1,0:T(4,128)S(1)}, f32[4,512]{1,0:T(4,128)S(1)}, u32[]{:S(2)}, u32[]{:S(2)}) %collective-permute-start.13) | collective-permute-done | bytes 8224 | tf_op jit(solution)/shard_map/ppermute | solution.py:455
  125.8 3.5 %collective-permute-start.14 = (f32[4,512]{1,0:T(4,128)S(1)}, f32[4,512]{1,0:T(4,128)S(1)}, u32[]{:S(2)}, u32[]{:S(2)}) collective-permute-start(f32[4,512]{1,0:T(4,128)S(1)} %add.52), channel_id=1, source_target_pairs={{0,8},{1,9},{2,10},{3,11},{4,12},{5,13},{6,14},{7,15},{8,0},{9,1},... | collective-permute-start | bytes 24584 | tf_op jit(solution)/shard_map/ppermute | solution.py:459
  129.4 5.2 %all-to-all-start.2 = ((bf16[8,128,256]{2,1,0:T(8,128)(2,1)}), bf16[8,128,256]{2,1,0:T(8,128)(2,1)S(1)}, u32[]{:S(2)}, u32[]{:S(2)}) async-start(bf16[8,128,256]{2,1,0:T(8,128)(2,1)} %get-tuple-element.35), calls=%async_computation.2 | async-start | bytes 1048576 | tf_op jit(solution)/shard_map/all_to_all | solution.py:356
  135.3 1.7 %collective-permute-start.16 = (f32[4,512]{1,0:T(4,128)S(1)}, f32[4,512]{1,0:T(4,128)S(1)}, u32[]{:S(2)}, u32[]{:S(2)}) collective-permute-start(f32[4,512]{1,0:T(4,128)S(1)} %get-tuple-element.72), channel_id=1, source_target_pairs={{0,2},{1,3},{2,0},{3,1},{4,6},{5,7},{6,4},{7,5},{8,10},{9,11},{10,... | collective-permute-start | bytes 24584 | tf_op jit(solution)/shard_map/ppermute | solution.py:463
  137.0 1.7 %collective-permute-start.18 = (f32[4,512]{1,0:T(4,128)S(1)}, f32[4,512]{1,0:T(4,128)S(1)}, u32[]{:S(2)}, u32[]{:S(2)}) collective-permute-start(f32[4,512]{1,0:T(4,128)S(1)} %get-tuple-element.72), channel_id=1, source_target_pairs={{0,4},{1,5},{2,6},{3,7},{4,0},{5,1},{6,2},{7,3},{8,12},{9,13},{10,... | collective-permute-start | bytes 24584 | tf_op jit(solution)/shard_map/ppermute | solution.py:463
  138.8 2.6 %collective-permute-start.20 = (f32[4,512]{1,0:T(4,128)S(1)}, f32[4,512]{1,0:T(4,128)S(1)}, u32[]{:S(2)}, u32[]{:S(2)}) collective-permute-start(f32[4,512]{1,0:T(4,128)S(1)} %get-tuple-element.72), channel_id=1, source_target_pairs={{0,6},{1,7},{2,4},{3,5},{4,2},{5,3},{6,0},{7,1},{8,14},{9,15},{10,... | collective-permute-start | bytes 24584 | tf_op jit(solution)/shard_map/ppermute | solution.py:463
  141.4 2.3 %collective-permute-done.16 = f32[4,512]{1,0:T(4,128)S(1)} collective-permute-done((f32[4,512]{1,0:T(4,128)S(1)}, f32[4,512]{1,0:T(4,128)S(1)}, u32[]{:S(2)}, u32[]{:S(2)}) %collective-permute-start.16) | collective-permute-done | bytes 8224 | tf_op jit(solution)/shard_map/ppermute | solution.py:463
  143.7 0.8 collective-permute-start.21
  144.6 3.6 %all-to-all-start.3 = ((bf16[8,128,512]{2,1,0:T(8,128)(2,1)}), bf16[8,128,512]{2,1,0:T(8,128)(2,1)S(1)}, u32[]{:S(2)}, u32[]{:S(2)}) async-start(bf16[8,128,512]{2,1,0:T(8,128)(2,1)} %get-tuple-element.47), calls=%async_computation.3 | async-start | bytes 2097152 | tf_op jit(solution)/shard_map/all_to_all | solution.py:356
  150.0 1.0 copy.130
  151.0 11.7 %all-to-all-done.3 = bf16[8,128,512]{2,1,0:T(8,128)(2,1)S(1)} async-done(((bf16[8,128,512]{2,1,0:T(8,128)(2,1)}), bf16[8,128,512]{2,1,0:T(8,128)(2,1)S(1)}, u32[]{:S(2)}, u32[]{:S(2)}) %all-to-all-start.3) | async-done | bytes 1048608 | tf_op jit(solution)/shard_map/all_to_all | solution.py:356
  164.2 1.1 maximum_bitcast_fusion
  (111 shorter events, 7.1 us)
Async XLA Ops:
  1.4 16.0 %collective-permute-start = (s32[3]{0:T(128)S(1)}, s32[3]{0:T(128)S(1)}, u32[]{:S(2)}, u32[]{:S(2)}) collective-permute-start(s32[3]{0:T(128)S(1)} %slice_bitcast_fusion.13), channel_id=1, source_target_pairs={{0,1},{1,2},{2,3},{3,4},{4,5},{5,6},{6,7},{7,8},{8,9},{9,10},{10,1... | collective-permute-start | bytes 44 | tf_op jit(solution)/shard_map/ppermute | solution.py:342
  4.6 14.1 %collective-permute-start.1 = (bf16[3,4096]{1,0:T(4,128)(2,1)S(1)}, bf16[3,4096]{1,0:T(4,128)(2,1)S(1)}, u32[]{:S(2)}, u32[]{:S(2)}) collective-permute-start(bf16[3,4096]{1,0:T(4,128)(2,1)S(1)} %slice_bitcast_fusion.4), channel_id=1, source_target_pairs={{0,1},{1,2},{2,3},{3,4},{4,5},{5,6},{6,7},{7,8},{8,9},{9,10},{10,1... | collective-permute-start | bytes 73736 | tf_op jit(solution)/shard_map/ppermute | solution.py:342
  10.4 4.8 %copy-start.10 = (bf16[1,128,4096]{2,1,0:T(8,128)(2,1)S(1)}, bf16[1,128,4096]{2,1,0:T(8,128)(2,1)}, u32[]{:S(2)}) copy-start(bf16[1,128,4096]{2,1,0:T(8,128)(2,1)} %param.6) | copy-start | bytes 3145732
  11.5 12.7 %all-to-all-start.1 = ((bf16[8,128,256]{2,1,0:T(8,128)(2,1)}), bf16[8,128,256]{2,1,0:T(8,128)(2,1)S(1)}, u32[]{:S(2)}, u32[]{:S(2)}) async-start(bf16[8,128,256]{2,1,0:T(8,128)(2,1)} %bitcast.23), calls=%async_computation.1 | async-start | bytes 1048576 | tf_op jit(solution)/shard_map/all_to_all | solution.py:356
  16.0 0.7 copy-start.12
  16.0 0.7 copy-start.13
  16.1 1.9 %copy-start.14 = (s32[1,128]{1,0:T(1,128)S(1)}, s32[1,128]{1,0:T(1,128)}, u32[]{:S(2)}) copy-start(s32[1,128]{1,0:T(1,128)} %param.10) | copy-start | bytes 1540
  20.0 8.4 %copy-start.11 = (bf16[4,4096]{1,0:T(4,128)(2,1)S(1)}, bf16[4,4096]{1,0:T(4,128)(2,1)}, u32[]{:S(2)}) copy-start(bf16[4,4096]{1,0:T(4,128)(2,1)} %param.7) | copy-start | bytes 98308
  24.1 20.1 %all-to-all-start = ((bf16[8,144,512]{2,1,0:T(8,128)(2,1)}), bf16[8,144,512]{2,1,0:T(8,128)(2,1)}, u32[]{:S(2)}, u32[]{:S(2)}) async-start(bf16[8,144,512]{2,1,0:T(8,128)(2,1)} %pad_maximum_fusion), calls=%async_computation | async-start | bytes 2359296 | tf_op jit(solution)/shard_map/all_to_all | solution.py:356
  66.6 1.0 copy-start.3
  67.6 1.0 copy-start.5
  68.6 0.8 copy-start.8
  69.4 7.0 %collective-permute-start.2 = (f32[2,128,128]{2,1,0:T(8,128)}, f32[2,128,128]{2,1,0:T(8,128)S(1)}, u32[]{:S(2)}, u32[]{:S(2)}) collective-permute-start(f32[2,128,128]{2,1,0:T(8,128)} %get-tuple-element.28), channel_id=1, source_target_pairs={{0,8},{1,9},{2,10},{3,11},{4,12},{5,13},{6,14},{7,15},{16,24},{17,... | collective-permute-start | bytes 393224 | tf_op jit(solution)/shard_map/ppermute | solution.py:342
  73.5 13.5 %collective-permute-start.3 = (f32[2,128,128]{2,1,0:T(8,128)S(1)}, f32[2,128,128]{2,1,0:T(8,128)S(1)}, u32[]{:S(2)}, u32[]{:S(2)}) collective-permute-start(f32[2,128,128]{2,1,0:T(8,128)S(1)} %get-tuple-element.36), channel_id=1, source_target_pairs={{8,0},{9,1},{10,2},{11,3},{12,4},{13,5},{14,6},{15,7},{24,16},{25,... | collective-permute-start | bytes 393224 | tf_op jit(solution)/shard_map/ppermute | solution.py:342
  74.8 34.7 %collective-permute-start.4 = (s32[1]{0:T(128)S(1)}, s32[1]{0:T(128)}, u32[]{:S(2)}, u32[]{:S(2)}) collective-permute-start(s32[1]{0:T(128)S(1)} %bitcast.150), channel_id=1, source_target_pairs={{1,0},{2,1},{3,2},{4,3},{5,4},{6,5},{7,6},{8,7},{9,8},{10,9},{11,1... | collective-permute-start | bytes 20 | tf_op jit(solution)/shard_map/ppermute | solution.py:342
  76.4 1.2 copy-start
  77.6 1.2 copy-start.1
  78.8 1.2 copy-start.2
  80.0 6.9 %copy-start.4 = (f32[8,2,128,128]{3,2,1,0:T(8,128)S(1)}, f32[8,2,128,128]{3,2,1,0:T(8,128)}, u32[]{:S(2)}) copy-start(f32[8,2,128,128]{3,2,1,0:T(8,128)} %copy-done.3) | copy-start | bytes 3145732
  80.0 6.9 %copy-start.9 = (f32[8,128,128]{2,1,0:T(8,128)S(1)}, f32[8,128,128]{2,1,0:T(8,128)}, u32[]{:S(2)}) copy-start(f32[8,128,128]{2,1,0:T(8,128)} %copy-done.8) | copy-start | bytes 1572868
  85.0 1.0 copy-start.6
  85.9 1.0 copy-start.7
  108.8 11.2 %collective-permute-start.5 = (bf16[3,512]{1,0:T(4,128)(2,1)S(1)}, bf16[3,512]{1,0:T(4,128)(2,1)S(1)}, u32[]{:S(2)}, u32[]{:S(2)}) collective-permute-start(bf16[3,512]{1,0:T(4,128)(2,1)S(1)} %slice.163), channel_id=1, source_target_pairs={{8,7},{24,23}} | collective-permute-start | bytes 9224 | tf_op jit(solution)/shard_map/ppermute | solution.py:447
  110.2 10.5 %collective-permute-start.6 = (bf16[3,512]{1,0:T(4,128)(2,1)S(1)}, bf16[3,512]{1,0:T(4,128)(2,1)S(1)}, u32[]{:S(2)}, u32[]{:S(2)}) collective-permute-start(bf16[3,512]{1,0:T(4,128)(2,1)S(1)} %slice.163), channel_id=1, source_target_pairs={{9,7},{25,23}} | collective-permute-start | bytes 9224 | tf_op jit(solution)/shard_map/ppermute | solution.py:447
  110.9 10.6 %collective-permute-start.7 = (bf16[3,512]{1,0:T(4,128)(2,1)S(1)}, bf16[3,512]{1,0:T(4,128)(2,1)S(1)}, u32[]{:S(2)}, u32[]{:S(2)}) collective-permute-start(bf16[3,512]{1,0:T(4,128)(2,1)S(1)} %slice.163), channel_id=1, source_target_pairs={{10,7},{26,23}} | collective-permute-start | bytes 9224 | tf_op jit(solution)/shard_map/ppermute | solution.py:447
  111.5 10.6 %collective-permute-start.8 = (bf16[3,512]{1,0:T(4,128)(2,1)S(1)}, bf16[3,512]{1,0:T(4,128)(2,1)S(1)}, u32[]{:S(2)}, u32[]{:S(2)}) collective-permute-start(bf16[3,512]{1,0:T(4,128)(2,1)S(1)} %slice.163), channel_id=1, source_target_pairs={{11,7},{27,23}} | collective-permute-start | bytes 9224 | tf_op jit(solution)/shard_map/ppermute | solution.py:447
  112.2 11.5 %collective-permute-start.9 = (bf16[3,512]{1,0:T(4,128)(2,1)S(1)}, bf16[3,512]{1,0:T(4,128)(2,1)S(1)}, u32[]{:S(2)}, u32[]{:S(2)}) collective-permute-start(bf16[3,512]{1,0:T(4,128)(2,1)S(1)} %slice.163), channel_id=1, source_target_pairs={{12,7},{28,23}} | collective-permute-start | bytes 9224 | tf_op jit(solution)/shard_map/ppermute | solution.py:447
  112.9 16.5 %all-to-all-start.4 = ((f32[8,4,128]{2,1,0:T(4,128)}), f32[8,4,128]{2,1,0:T(4,128)S(1)}, u32[]{:S(2)}, u32[]{:S(2)}) async-start(f32[8,4,128]{2,1,0:T(4,128)} %get-tuple-element.50), calls=%async_computation.4 | async-start | bytes 32768 | tf_op jit(solution)/shard_map/all_to_all | solution.py:356
  120.0 3.6 %collective-permute-start.10 = (bf16[3,512]{1,0:T(4,128)(2,1)S(1)}, bf16[3,512]{1,0:T(4,128)(2,1)S(1)}, u32[]{:S(2)}, u32[]{:S(2)}) collective-permute-start(bf16[3,512]{1,0:T(4,128)(2,1)S(1)} %slice.163), channel_id=1, source_target_pairs={{13,7},{29,23}} | collective-permute-start | bytes 9224 | tf_op jit(solution)/shard_map/ppermute | solution.py:447
  120.7 3.0 %collective-permute-start.11 = (bf16[3,512]{1,0:T(4,128)(2,1)S(1)}, bf16[3,512]{1,0:T(4,128)(2,1)S(1)}, u32[]{:S(2)}, u32[]{:S(2)}) collective-permute-start(bf16[3,512]{1,0:T(4,128)(2,1)S(1)} %slice.163), channel_id=1, source_target_pairs={{14,7},{30,23}} | collective-permute-start | bytes 9224 | tf_op jit(solution)/shard_map/ppermute | solution.py:447
  121.4 8.0 %collective-permute-start.12 = (bf16[3,512]{1,0:T(4,128)(2,1)S(1)}, bf16[3,512]{1,0:T(4,128)(2,1)S(1)}, u32[]{:S(2)}, u32[]{:S(2)}) collective-permute-start(bf16[3,512]{1,0:T(4,128)(2,1)S(1)} %slice.163), channel_id=1, source_target_pairs={{15,7},{31,23}} | collective-permute-start | bytes 9224 | tf_op jit(solution)/shard_map/ppermute | solution.py:447
  122.1 3.7 %collective-permute-start.13 = (f32[4,512]{1,0:T(4,128)S(1)}, f32[4,512]{1,0:T(4,128)S(1)}, u32[]{:S(2)}, u32[]{:S(2)}) collective-permute-start(f32[4,512]{1,0:T(4,128)S(1)} %get-tuple-element.49), channel_id=1, source_target_pairs={{0,16},{16,0},{1,17},{17,1},{2,18},{18,2},{3,19},{19,3},{4,20},{20... | collective-permute-start | bytes 24584 | tf_op jit(solution)/shard_map/ppermute | solution.py:455
  125.8 8.8 %collective-permute-start.14 = (f32[4,512]{1,0:T(4,128)S(1)}, f32[4,512]{1,0:T(4,128)S(1)}, u32[]{:S(2)}, u32[]{:S(2)}) collective-permute-start(f32[4,512]{1,0:T(4,128)S(1)} %add.52), channel_id=1, source_target_pairs={{0,8},{1,9},{2,10},{3,11},{4,12},{5,13},{6,14},{7,15},{8,0},{9,1},... | collective-permute-start | bytes 24584 | tf_op jit(solution)/shard_map/ppermute | solution.py:459
  129.4 15.2 %all-to-all-start.2 = ((bf16[8,128,256]{2,1,0:T(8,128)(2,1)}), bf16[8,128,256]{2,1,0:T(8,128)(2,1)S(1)}, u32[]{:S(2)}, u32[]{:S(2)}) async-start(bf16[8,128,256]{2,1,0:T(8,128)(2,1)} %get-tuple-element.35), calls=%async_computation.2 | async-start | bytes 1048576 | tf_op jit(solution)/shard_map/all_to_all | solution.py:356
  134.7 4.2 %collective-permute-start.15 = (f32[4,512]{1,0:T(4,128)S(1)}, f32[4,512]{1,0:T(4,128)S(1)}, u32[]{:S(2)}, u32[]{:S(2)}) collective-permute-start(f32[4,512]{1,0:T(4,128)S(1)} %get-tuple-element.72), channel_id=1, source_target_pairs={{0,1},{1,0},{2,3},{3,2},{4,5},{5,4},{6,7},{7,6},{8,9},{9,8},{10,11... | collective-permute-start | bytes 24584 | tf_op jit(solution)/shard_map/ppermute | solution.py:463
  135.3 8.5 %collective-permute-start.16 = (f32[4,512]{1,0:T(4,128)S(1)}, f32[4,512]{1,0:T(4,128)S(1)}, u32[]{:S(2)}, u32[]{:S(2)}) collective-permute-start(f32[4,512]{1,0:T(4,128)S(1)} %get-tuple-element.72), channel_id=1, source_target_pairs={{0,2},{1,3},{2,0},{3,1},{4,6},{5,7},{6,4},{7,5},{8,10},{9,11},{10,... | collective-permute-start | bytes 24584 | tf_op jit(solution)/shard_map/ppermute | solution.py:463
  137.0 7.5 %collective-permute-start.17 = (f32[4,512]{1,0:T(4,128)S(1)}, f32[4,512]{1,0:T(4,128)S(1)}, u32[]{:S(2)}, u32[]{:S(2)}) collective-permute-start(f32[4,512]{1,0:T(4,128)S(1)} %get-tuple-element.72), channel_id=1, source_target_pairs={{0,3},{1,2},{2,1},{3,0},{4,7},{5,6},{6,5},{7,4},{8,11},{9,10},{10,... | collective-permute-start | bytes 24584 | tf_op jit(solution)/shard_map/ppermute | solution.py:463
  137.0 11.1 %collective-permute-start.18 = (f32[4,512]{1,0:T(4,128)S(1)}, f32[4,512]{1,0:T(4,128)S(1)}, u32[]{:S(2)}, u32[]{:S(2)}) collective-permute-start(f32[4,512]{1,0:T(4,128)S(1)} %get-tuple-element.72), channel_id=1, source_target_pairs={{0,4},{1,5},{2,6},{3,7},{4,0},{5,1},{6,2},{7,3},{8,12},{9,13},{10,... | collective-permute-start | bytes 24584 | tf_op jit(solution)/shard_map/ppermute | solution.py:463
  138.7 9.5 %collective-permute-start.19 = (f32[4,512]{1,0:T(4,128)S(1)}, f32[4,512]{1,0:T(4,128)S(1)}, u32[]{:S(2)}, u32[]{:S(2)}) collective-permute-start(f32[4,512]{1,0:T(4,128)S(1)} %get-tuple-element.72), channel_id=1, source_target_pairs={{0,5},{1,4},{2,7},{3,6},{4,1},{5,0},{6,3},{7,2},{8,13},{9,12},{10,... | collective-permute-start | bytes 24584 | tf_op jit(solution)/shard_map/ppermute | solution.py:463
  138.8 9.4 %collective-permute-start.20 = (f32[4,512]{1,0:T(4,128)S(1)}, f32[4,512]{1,0:T(4,128)S(1)}, u32[]{:S(2)}, u32[]{:S(2)}) collective-permute-start(f32[4,512]{1,0:T(4,128)S(1)} %get-tuple-element.72), channel_id=1, source_target_pairs={{0,6},{1,7},{2,4},{3,5},{4,2},{5,3},{6,0},{7,1},{8,14},{9,15},{10,... | collective-permute-start | bytes 24584 | tf_op jit(solution)/shard_map/ppermute | solution.py:463
  143.7 4.5 %collective-permute-start.21 = (f32[4,512]{1,0:T(4,128)S(1)}, f32[4,512]{1,0:T(4,128)S(1)}, u32[]{:S(2)}, u32[]{:S(2)}) collective-permute-start(f32[4,512]{1,0:T(4,128)S(1)} %get-tuple-element.72), channel_id=1, source_target_pairs={{0,7},{1,6},{2,5},{3,4},{4,3},{5,2},{6,1},{7,0},{8,15},{9,14},{10,... | collective-permute-start | bytes 24584 | tf_op jit(solution)/shard_map/ppermute | solution.py:463
  144.6 18.1 %all-to-all-start.3 = ((bf16[8,128,512]{2,1,0:T(8,128)(2,1)}), bf16[8,128,512]{2,1,0:T(8,128)(2,1)S(1)}, u32[]{:S(2)}, u32[]{:S(2)}) async-start(bf16[8,128,512]{2,1,0:T(8,128)(2,1)} %get-tuple-element.47), calls=%async_computation.3 | async-start | bytes 2097152 | tf_op jit(solution)/shard_map/all_to_all | solution.py:356

commit v2 on v1

v2 whole, which is shorter than its diff:
```python
import functools

import jax
import jax.numpy as jnp
from jax import lax
from jax.experimental import pallas as pl
from jax.experimental.pallas import tpu as pltpu
from jax.sharding import PartitionSpec as P

DK = 128
DOC_MOST = 1024
EPS = 1e-6
CODE = 16
COUNTS = (2, 2, 2, 2)
VMEM = 56 << 20
RIM = 16
f32 = jnp.float32
bf16 = jnp.bfloat16


def dg(a, b, ca, cb):
    return lax.dot_general(a, b, (((ca,), (cb,)), ((), ())), preferred_element_type=f32)


def split(x):
    hi = x.astype(bf16)
    return (hi, (x - hi.astype(f32)).astype(bf16))


def cat(parts, axis):
    return tuple(jnp.concatenate(leaves, axis) for leaves in zip(*parts))


def mm(a, b, ca, cb):
    out = dg(a[0], b[0], ca, cb)
    if len(b) > 1:
        out = out + dg(a[0], b[1], ca, cb)
    if len(a) > 1:
        out = out + dg(a[1], b[0], ca, cb)
    return out


def iota2(shape, dim):
    return lax.broadcasted_iota(jnp.int32, shape, dim)


def conv_inputs(x_ref, n, width, shift_ref, docs):
    length = docs.shape[0]
    shift_ref[5:8, :width] = x_ref[n, length : length + 3, :width].astype(f32)
    rows = x_ref[n, :length, :width].astype(f32)
    shift_ref[8 : 8 + length, :width] = rows
    at = iota2((length, DK), 0)
    first = docs[0:1, :]
    taps = [rows]
    for off in (1, 2, 3):
        earlier = jnp.where(at >= off, pltpu.roll(docs, off, 0), first)
        ok = earlier == docs
        moved = shift_ref[8 - off : 8 - off + length, :width]
        taps.append(jnp.where(wide(ok, width), moved, 0.0))
    return taps


def wide(x, width):
    return jnp.concatenate([x] * (width // DK), 1)


def conv_out(taps, w):
    return sum(w[3 - off : 4 - off, :] * taps[off] for off in range(4))


def conv_back(dz, taps, w, code, plain, dz_ref, doc_next, dw_ref, rim_ref):
    length, width = dz.shape
    dz_ref[8 + length :, :] = dz_ref[8:16, :]
    dz_ref[8 : 8 + length, :] = dz
    docs_after = doc_next[...]
    at = iota2((length, DK), 0)
    dx = w[3:4, :] * dz
    for off in (1, 2, 3):
        ahead = pltpu.roll(plain, length - off, 0)
        for r in range(off):
            ahead = jnp.where(at == length - off + r, docs_after[r : r + 1, :], ahead)
        moved = dz_ref[8 + off : 8 + off + length, :]
        dx = dx + w[3 - off : 4 - off, :] * jnp.where(wide(ahead == plain, width), moved, 0.0)
    doc_next[...] = plain[0:8, :]
    for off in range(4):
        dw_ref[3 - off : 4 - off, :] += jnp.sum(dz * taps[off], 0, keepdims=True)
    head = jnp.where(wide(code[0:8, :] == code[0:1, :], width), dz[0:8, :], 0.0)
    held = wide(code[0:1, :], width)
    for r in range(3):
        total = 0.0
        for off in range(3 - r, 4):
            total = total + w[3 - off : 4 - off, :] * head[r + off - 3 : r + off - 2, :]
        rim_ref[r : r + 1, :] = jnp.where(held >= CODE * (3 - r), total, 0.0)
    return dx


def unit(x):
    inv = lax.rsqrt(jnp.sum(x * x, -1, keepdims=True) + EPS)
    return x * inv, inv


def unit_back(grad, hat, inv):
    return inv * (grad - hat * jnp.sum(grad * hat, -1, keepdims=True))


def sigmoid(z):
    return 1.0 / (1.0 + jnp.exp(-z))


class Meta:
    def __init__(self, numbers, per_key):
        length = numbers.shape[1]
        rows = numbers.astype(f32)
        row_at = iota2((RIM, DK), 0)
        i, j = iota2((length, length), 0), iota2((length, length), 1)
        self.lower, self.strict = i >= j, i > j

        def column(first, count):
            pick = ((row_at >= first) & (row_at < first + count)).astype(f32).astype(bf16)
            return dg(numbers, pick, 0, 0)

        self.code = column(3, 1)
        self.plain = self.code - CODE * jnp.floor(self.code * (1.0 / CODE))
        code_row = rows[3:4]
        self.same = (self.code == code_row) & self.lower
        carry = (self.code >= CODE) & (self.code == code_row[:, 0:1])
        ending = self.code == code_row[:, length - 1 : length]
        until = (i <= j).astype(f32).astype(bf16)
        row_sums = dg(numbers, until, 1, 0)
        ones = jnp.ones((length, DK), bf16)
        self.c_row, self.c_col, self.beta, self.beta_row = [], [], [], []
        self.entry, self.tail, self.keep = [], [], []
        for h in range(per_key):
            at = 4 + 3 * h
            self.c_row.append(row_sums[at : at + 1] + row_sums[at + 1 : at + 2] + row_sums[at + 2 : at + 3])
            c_col = 0.0
            for part in (2, 1, 0):
                c_col = c_col + dg(jnp.where(self.lower, rows[at + part : at + part + 1], 0.0).astype(bf16), ones, 1, 0)
            self.c_col.append(c_col)
            at = 4 + 3 * per_key + 3 * h
            self.beta.append(column(at, 3))
            self.beta_row.append(rows[at : at + 1] + rows[at + 1 : at + 2] + rows[at + 2 : at + 3])
            self.entry.append(jnp.where(carry, jnp.exp(c_col), 0.0))
            last = self.c_row[h][:, length - 1 : length]
            self.tail.append(jnp.where(ending, jnp.exp(jnp.minimum(last - c_col, 0.0)), 0.0))
            self.keep.append(self.entry[h][length - 1 : length, :])

    def fading(self, h):
        gap = jnp.minimum(self.c_col[h] - self.c_row[h], 0.0)
        return jnp.where(self.same, jnp.exp(gap), 0.0)


def inverse(mats):
    length = mats[0].shape[0]
    i, j = iota2((length, length), 0), iota2((length, length), 1)
    eye = (i == j).astype(f32)
    inner = [jnp.where((i // 8) == (j // 8), n, 0.0) for n in mats]
    s1 = [split(n) for n in inner]
    s2 = [split(mm(a, a, 1, 0)) for a in s1]
    low = [eye - n + (a[0].astype(f32) + a[1].astype(f32)) - mm(b, a, 1, 0) for n, a, b in zip(inner, s2, s1)]
    s4 = [split(mm(a, a, 1, 0)) for a in s2]
    inv = [t + mm(split(t), a, 1, 0) for t, a in zip(low, s4)]
    width = 8
    while width < length:
        cross = ((i // (2 * width)) == (j // (2 * width))) & ((i // width) > (j // width))
        st = [split(t) for t in inv]
        half = [mm(split(jnp.where(cross, n, 0.0)), t, 1, 0) for n, t in zip(mats, st)]
        inv = [t - mm(s, split(x), 1, 0) for t, s, x in zip(inv, st, half)]
        width *= 2
    return inv


def rows_from(x):
    ones = jnp.ones((8, x.shape[1]), bf16)
    return mm((ones,), split(x), 1, 1)[0:1]


def three_rows(x):
    hi = x.astype(bf16).astype(f32)
    mid = (x - hi).astype(bf16).astype(f32)
    return jnp.concatenate([hi, mid, x - hi - mid], 0)


def key_kernel(per_key, count, x_ref, w_ref, k_ref, f_ref, n_ref, t_ref, w_out, u_ref, a_ref, m_ref, s_ref, end_ref,
               chain, shift_ref):
    step = pl.program_id(0)
    length = k_ref.shape[1]
    own = w_ref.shape[1]
    eye = (iota2((DK, DK), 0) == iota2((DK, DK), 1)).astype(f32)

    @pl.when(step == 0)
    def _():
        for h in range(per_key):
            chain[h] = jnp.concatenate([eye, jnp.zeros((DK, DK), f32)], 1)

    w = w_ref[...]
    pairs = [(n, h) for n in range(count) for h in range(per_key)]
    metas, ks, vs = [], [], []
    for n in range(count):
        meta = Meta(x_ref[n, length:, :DK], per_key)
        z = conv_out(conv_inputs(x_ref, n, own, shift_ref.at[n], meta.code), w)
        act = z * sigmoid(z)
        k, _ = unit(act[:, :DK])
        k_ref[n] = k
        metas.append(meta)
        ks.append(k)
        vs.append(act[:, DK:])
    sk = [split(k) for k in ks]
    kk = [mm(s, s, 1, 1) for s in sk]
    fs = [metas[n].fading(h) for n, h in pairs]
    ns = [jnp.where(metas[n].strict, metas[n].beta[h] * kk[n] * f, 0.0) for (n, h), f in zip(pairs, fs)]
    ts = inverse(ns)
    rhs = [
        jnp.concatenate([metas[n].beta[h] * metas[n].entry[h] * ks[n], metas[n].beta[h] * vs[n][:, h * DK : (h + 1) * DK]], 1)
        for n, h in pairs
    ]
    wu = [mm(split(t), split(r), 1, 0) for t, r in zip(ts, rhs)]
    kwu = [mm(split(metas[n].tail[h] * ks[n]), split(x), 0, 0) for (n, h), x in zip(pairs, wu)]
    for m, (n, h) in enumerate(pairs):
        f_ref[n, h], n_ref[n, h], t_ref[n, h] = fs[m], ns[m], ts[m]
        w_out[n, h], u_ref[n, h] = wu[m][:, :DK], wu[m][:, DK:]
        a = metas[n].keep[h] * eye - kwu[m][:, :DK]
        a_ref[n, h] = a
        now = chain[h]
        m_ref[n, h], s_ref[n, h] = now[:, :DK], now[:, DK:]
        later = mm(split(a), split(now), 1, 0)
        chain[h] = jnp.concatenate([later[:, :DK], later[:, DK:] + kwu[m][:, DK:]], 1)
    for h in range(per_key):
        end_ref[h] = chain[h, :, DK:]


def query_kernel(per_key, count, x_ref, y_ref, w_ref, k_ref, f_ref, w_in, u_ref, a_ref, p_ref, y_out, pu_ref, r_ref,
                 m_ref, g_ref, start_ref, chain, shift_ref):
    step = pl.program_id(0)
    length = k_ref.shape[1]
    eye = (iota2((DK, DK), 0) == iota2((DK, DK), 1)).astype(f32)

    @pl.when(step == 0)
    def _():
        for h in range(per_key):
            chain[h] = jnp.concatenate([eye, jnp.zeros((DK, DK), f32)], 1)

    w = w_ref[...]
    pairs = [(n, h) for n in reversed(range(count)) for h in range(per_key)]
    metas, qs, qk = {}, {}, {}
    for n in range(count):
        metas[n] = Meta(x_ref[n, length:, :DK], per_key)
        z = conv_out(conv_inputs(y_ref, n, DK, shift_ref.at[n], metas[n].code), w)
        q, _ = unit(z * sigmoid(z))
        qs[n] = q * DK**-0.5
        qk[n] = mm(split(qs[n]), split(k_ref[n]), 1, 1)
    ps = [qk[n] * f_ref[n, h] for n, h in pairs]
    sp = [split(p) for p in ps]
    swu = [cat([split(w_in[n, h]), split(u_ref[n, h])], 1) for n, h in pairs]
    pwu = [mm(p, s, 1, 0) for p, s in zip(sp, swu)]
    ys = [metas[n].entry[h] * qs[n] - x[:, :DK] for (n, h), x in zip(pairs, pwu)]
    dos = [(y_ref[n, :length, (h + 1) * DK : (h + 2) * DK],) for n, h in pairs]
    gs = [mm(split(y), d, 0, 0) for y, d in zip(ys, dos)]
    rs = [mm(p, d, 0, 0) for p, d in zip(sp, dos)]
    for m, (n, h) in enumerate(pairs):
        p_ref[n, h], y_out[n, h], pu_ref[n, h], r_ref[n, h] = ps[m], ys[m], pwu[m][:, DK:], rs[m]
        now = chain[h]
        m_ref[n, h], g_ref[n, h] = now[:, :DK], now[:, DK:]
        later = mm(split(a_ref[n, h]), split(now), 0, 0)
        chain[h] = jnp.concatenate([later[:, :DK], later[:, DK:] + gs[m]], 1)
    for h in range(per_key):
        start_ref[h] = chain[h, :, DK:]


def read_kernel(per_key, count, in_ref, x_ref, y_ref, w_ref, k_ref, f_ref, p_ref, w_in, u_ref, y_in, pu_ref, m_ref,
                sl_ref, out_ref, d_ref, s_ref, dk_ref, dc_ref, rim_ref, dw_ref, shift_ref, dz_ref, doc_next):
    length = k_ref.shape[1]

    @pl.when(pl.program_id(0) == 0)
    def _():
        dw_ref[...] = jnp.zeros_like(dw_ref)
        dz_ref[...] = jnp.zeros_like(dz_ref)
        doc_next[...] = jnp.zeros_like(doc_next)

    w = w_ref[...]
    s_in = [split(in_ref[h]) for h in range(per_key)]
    pairs = [(n, h) for n in reversed(range(count)) for h in range(per_key)]
    metas, taps, sig, zs, hats, inv, qs, sq, sk = {}, {}, {}, {}, {}, {}, {}, {}, {}
    for n in range(count):
        metas[n] = Meta(x_ref[n, length:, :DK], per_key)
        taps[n] = conv_inputs(y_ref, n, DK, shift_ref.at[n], metas[n].code)
        zs[n] = conv_out(taps[n], w)
        sig[n] = sigmoid(zs[n])
        hats[n], inv[n] = unit(zs[n] * sig[n])
        qs[n] = hats[n] * DK**-0.5
        sq[n], sk[n] = split(qs[n]), split(k_ref[n])
    states = [sl_ref[n, h] + mm(split(m_ref[n, h]), s_in[h], 1, 0) for n, h in pairs]
    ss = [split(s) for s in states]
    both = [mm(cat([split(w_in[n, h]), split(y_in[n, h])], 0), s, 1, 0) for (n, h), s in zip(pairs, ss)]
    ds = [u_ref[n, h] - x[:length] for (n, h), x in zip(pairs, both)]
    dos = [(y_ref[n, :length, (h + 1) * DK : (h + 2) * DK],) for n, h in pairs]
    dps = [mm(do, split(d), 1, 1) for do, d in zip(dos, ds)]
    enters = [metas[n].entry[h] * mm(do, s, 1, 1) for (n, h), do, s in zip(pairs, dos, ss)]
    dpf = [split(dp * f_ref[n, h]) for (n, h), dp in zip(pairs, dps)]
    dqs = [e + mm(x, sk[n], 1, 0) for (n, h), e, x in zip(pairs, enters, dpf)]
    dks = [mm(x, sq[n], 0, 0) for (n, h), x in zip(pairs, dpf)]
    dq, dk = {}, {}
    for m, (n, h) in enumerate(pairs):
        s_ref[n, h], d_ref[n, h] = states[m], ds[m]
        out_ref[n, :, (h + 1) * DK : (h + 2) * DK] = (both[m][length:] + pu_ref[n, h]).astype(bf16)
        gaps = dps[m] * p_ref[n, h]
        dc_ref[n, h : h + 1, :] = rows_from(gaps + enters[m] * qs[n]) - jnp.sum(gaps, 0, keepdims=True)
        dq[n] = dq[n] + dqs[m] if h else dqs[m]
        dk[n] = dk[n] + dks[m] if h else dks[m]
    for n in reversed(range(count)):
        dk_ref[n] = dk[n]
        grad = unit_back(DK**-0.5 * dq[n], hats[n], inv[n])
        dz = grad * (sig[n] + zs[n] * sig[n] * (1.0 - sig[n]))
        dx = conv_back(dz, taps[n], w, metas[n].code, metas[n].plain, dz_ref, doc_next, dw_ref, rim_ref)
        out_ref[n, :, :DK] = dx.astype(bf16)


def write_kernel(per_key, count, in_ref, x_ref, w_ref, k_ref, f_ref, n_ref, t_ref, r_ref, m_ref, gl_ref, d_ref, s_ref,
                 dk_ref, dc_ref, dx_ref, rim_ref, dw_ref, shift_ref, dz_ref, doc_next):
    length = k_ref.shape[1]
    own = w_ref.shape[1]

    @pl.when(pl.program_id(0) == 0)
    def _():
        dw_ref[...] = jnp.zeros_like(dw_ref)
        dz_ref[...] = jnp.zeros_like(dz_ref)
        doc_next[...] = jnp.zeros_like(doc_next)

    w = w_ref[...]
    i, j = iota2((length, length), 0), iota2((length, length), 1)
    from_here = (i >= j).astype(f32).astype(bf16)
    g_in = [split(in_ref[h]) for h in range(per_key)]
    pairs = [(n, h) for n in reversed(range(count)) for h in range(per_key)]
    metas, taps, sig, zs, hats, inv, vs, sk = {}, {}, {}, {}, {}, {}, {}, {}
    for n in range(count):
        metas[n] = Meta(x_ref[n, length:, :DK], per_key)
        taps[n] = conv_inputs(x_ref, n, own, shift_ref.at[n], metas[n].code)
        zs[n] = conv_out(taps[n], w)
        sig[n] = sigmoid(zs[n])
        act = zs[n] * sig[n]
        hats[n], inv[n] = unit(act[:, :DK])
        vs[n] = act[:, DK:]
        sk[n] = split(k_ref[n])
    later = [gl_ref[n, h] + mm(split(m_ref[n, h]), g_in[h], 1, 0) for n, h in pairs]
    s_later = [split(x) for x in later]
    s_d = [split(d_ref[n, h]) for n, h in pairs]
    s_s = [split(s_ref[n, h]) for n, h in pairs]
    x1 = [mm(split(metas[n].tail[h] * k_ref[n]), s, 1, 0) for (n, h), s in zip(pairs, s_later)]
    es = [mm(split(t_ref[n, h]), split(r_ref[n, h] + x), 0, 0) for (n, h), x in zip(pairs, x1)]
    se = [split(e) for e in es]
    ends = [metas[n].tail[h] * mm(d, s, 1, 1) for (n, h), d, s in zip(pairs, s_d, s_later)]
    dns = [-mm(e, d, 1, 1) for e, d in zip(se, s_d)]
    ess = [mm(e, s, 1, 1) for e, s in zip(se, s_s)]
    dkk = [
        split(jnp.where(metas[n].strict, dn * metas[n].beta[h] * f_ref[n, h], 0.0)) for (n, h), dn in zip(pairs, dns)
    ]
    dks = [mm(x, sk[n], 1, 0) + mm(x, sk[n], 0, 0) for (n, h), x in zip(pairs, dkk)]
    dk, dv, rows = {n: dk_ref[n] for n in range(count)}, {}, {}
    for m, (n, h) in enumerate(pairs):
        meta, k = metas[n], k_ref[n]
        bes = meta.beta[h] * meta.entry[h] * ess[m]
        dk[n] = dk[n] + dks[m] - bes + ends[m]
        dv[n, h] = meta.beta[h] * es[m]
        nn = dns[m] * n_ref[n, h]
        ek = ends[m] * k
        dc = dc_ref[n, h : h + 1, :] + rows_from(nn - bes * k - ek) - jnp.sum(nn, 0, keepdims=True)
        last = jnp.sum(ek + later[m] * s_ref[n, h] * meta.keep[h], 0, keepdims=True)
        at_end = jnp.sum(last, 1, keepdims=True)
        rows[n, h] = mm(split(jnp.broadcast_to(dc, (8, length))), (from_here,), 1, 0)[0:1] + at_end
        own_v = vs[n][:, h * DK : (h + 1) * DK]
        rows[n, per_key + h] = (
            rows_from(es[m] * own_v - meta.entry[h] * ess[m] * k) + rows_from(nn) / meta.beta_row[h]
        )
    for n in reversed(range(count)):
        dk_act = unit_back(dk[n], hats[n], inv[n])
        d_act = jnp.concatenate([dk_act] + [dv[n, h] for h in range(per_key)], 1)
        dz = d_act * (sig[n] + zs[n] * sig[n] * (1.0 - sig[n]))
        dx = conv_back(dz, taps[n], w, metas[n].code, metas[n].plain, dz_ref, doc_next, dw_ref, rim_ref)
        dx_ref[n, :length, :] = dx.astype(bf16)
        gates = three_rows(jnp.concatenate([rows[n, m] for m in range(2 * per_key)], 0))
        gates = jnp.concatenate([gates, jnp.zeros((RIM - gates.shape[0], length), f32)], 0)
        dx_ref[n, length:, :] = jnp.concatenate([gates, jnp.zeros((RIM, own - DK), f32)], 1).astype(bf16)


def three(x):
    hi = lax.reduce_precision(x, 8, 7)
    mid = lax.reduce_precision(x - hi, 8, 7)
    return jnp.stack([hi, mid, x - hi - mid], -2).astype(bf16)


def local(mixed, conv_weight, log_decay, beta, doc_ids, out_grad):
    n_seq, n_dp = lax.axis_size("seq"), lax.axis_size("dp")
    rows, docs, og = mixed[0], doc_ids[0], out_grad[0]
    length, channels = rows.shape
    heads = log_decay.shape[1]
    key_heads = (channels - heads * DK) // (2 * DK)
    per_key = heads // key_heads
    G = key_heads
    assert n_seq % G == 0 and G * length >= DOC_MOST
    member = lax.axis_index("seq") % G
    team = [list(range(s, s + G)) for s in range(0, n_seq, G)]
    own = DK + per_key * DK

    def shifted(x, by):
        return lax.ppermute(x, "seq", [(s, s + by) for s in range(n_seq) if 0 <= s + by < n_seq])

    def by_member(x):
        return jnp.moveaxis(x.reshape(x.shape[:-1] + (G, -1)), -2, 0)

    def of_members(x):
        return jnp.moveaxis(x, 0, -2).reshape(x.shape[1:-1] + (-1,))

    def keys_values(x):
        return jnp.concatenate([by_member(x[..., G * DK : 2 * G * DK]), by_member(x[..., 2 * G * DK :])], -1)

    def swap(x):
        return lax.all_to_all(x, "seq", 0, 0, axis_index_groups=team)

    doc_row = jnp.pad((docs[-3:] + 1).astype(bf16), (0, channels - 3))
    rim = shifted(jnp.concatenate([rows[-3:], doc_row[None]], 0), 1)
    held = rim[3, :3] == (docs[0] + 1).astype(bf16)
    rim_rows = jnp.where(held[:, None], rim[:3], 0)
    code = (docs + 1 + CODE * jnp.sum(held.astype(jnp.int32))).astype(bf16)
    numbers = jnp.concatenate(
        [
            jnp.broadcast_to(code, (G, 1, length)),
            three(log_decay[0].reshape(G, per_key, length)).reshape(G, -1, length),
            three(beta[0].reshape(G, per_key, length)).reshape(G, -1, length),
        ],
        1,
    )
    numbers = jnp.pad(numbers, ((0, 0), (0, 0), (0, own - DK)))
    x = swap(jnp.concatenate([keys_values(rows), keys_values(rim_rows), numbers], 1))
    queries = jnp.concatenate([by_member(rows[:, : G * DK]), by_member(rim_rows[:, : G * DK])], 1)
    queries = jnp.pad(queries, ((0, 0), (0, RIM - 3), (0, 0)))
    asked = jnp.pad(by_member(og), ((0, 0), (0, RIM), (0, 0)))
    later_part = jnp.concatenate([queries, asked], 2)
    later_part, x = lax.optimization_barrier((later_part, x))
    y = swap(later_part)
    taps = conv_weight.astype(f32)
    w_kv = lax.dynamic_index_in_dim(keys_values(taps), member, 0, keepdims=False)
    w_q = lax.dynamic_index_in_dim(by_member(taps[:, : G * DK]), member, 0, keepdims=False)

    pair = (per_key, DK, DK)
    block = (length, DK)

    def call(kernel, count, name, back, fulls, ins, out_shapes, out_fulls, scratch, flops):
        steps = G // count
        order = (lambda s: steps - 1 - s) if back else (lambda s: s)

        def spec(shape):
            return pl.BlockSpec((count,) + shape, lambda s: (order(s),) + (0,) * len(shape))

        def full(shape):
            return pl.BlockSpec(shape, lambda s: (0,) * len(shape))

        in_specs = [full(a.shape) if m in fulls else spec(a.shape[1:]) for m, a in enumerate(ins)]
        return pl.pallas_call(
            functools.partial(kernel, per_key, count),
            grid=(steps,),
            in_specs=in_specs,
            out_specs=[spec(s) for s, _ in out_shapes] + [full(s) for s in out_fulls],
            out_shape=[jax.ShapeDtypeStruct((G,) + s, t) for s, t in out_shapes]
            + [jax.ShapeDtypeStruct(s, f32) for s in out_fulls],
            scratch_shapes=scratch(count),
            compiler_params=pltpu.CompilerParams(vmem_limit_bytes=VMEM),
            cost_estimate=pl.CostEstimate(flops=flops, bytes_accessed=8 << 20, transcendentals=0),
            name=name,
        )(*ins)

    def conv_scratch(width):
        return lambda count: [
            pltpu.VMEM((count, 8 + length, width), f32),
            pltpu.VMEM((16 + length, width), f32),
            pltpu.VMEM((8, DK), f32),
        ]

    def chain_scratch(width):
        return lambda count: [pltpu.VMEM((per_key, DK, 2 * DK), f32), pltpu.VMEM((count, 8 + length, width), f32)]

    k, f, n, t, w_out, u, a, m_fwd, s_local, end = call(
        key_kernel, COUNTS[0], "keys", False, (1,), (x, w_kv), [(block, f32)] + [(pair, f32)] * 8, [pair],
        chain_scratch(own), 15 * 10**9,
    )
    state_in = shifted(end, G)
    p, y_read, pu, r, m_bwd, g_local, start = call(
        query_kernel, COUNTS[1], "queries", True, (2,), (x, y, w_q, k, f, w_out, u, a), [(pair, f32)] * 6, [pair],
        chain_scratch(DK), 8 * 10**9,
    )
    back_in = shifted(start, -G)
    o, d, s, dk, dc, rim_q, dw_q = call(
        read_kernel, COUNTS[2], "reads", True, (0, 3), (state_in, x, y, w_q, k, f, p, w_out, u, y_read, pu, m_fwd, s_local),
        [((length, own), bf16), (pair, f32), (pair, f32), (block, f32), ((per_key, length), f32)],
        [(3, DK), (4, DK)], conv_scratch(DK), 8 * 10**9,
    )
    o = swap(o)
    dx, rim_kv, dw_kv = call(
        write_kernel, COUNTS[3], "writes", True, (0, 2), (back_in, x, w_kv, k, f, n, t, r, m_bwd, g_local, d, s, dk, dc),
        [((length + RIM, own), bf16)], [(3, own), (4, own)], conv_scratch(own), 15 * 10**9,
    )
    dx = swap(dx)

    small = jnp.concatenate([jnp.concatenate([dw_q, dw_kv], 1), jnp.concatenate([rim_q, rim_kv], 1)], 0)
    gathered = small[None]
    step = 1
    while step < G:
        other = lax.ppermute(gathered, "seq", [(s, s ^ step) for s in range(n_seq)])
        upper = (member & step) > 0
        gathered = jnp.where(upper, jnp.concatenate([other, gathered], 0), jnp.concatenate([gathered, other], 0))
        step *= 2
    total = of_members(gathered[:, :, :DK]), of_members(gathered[:, :, DK : 2 * DK]), of_members(gathered[:, :, 2 * DK :])
    total = jnp.concatenate(total, -1)
    d_weight, rim_grad = total[:4], total[4:]
    step = G
    while step < n_seq:
        d_weight = d_weight + lax.ppermute(d_weight, "seq", [(s, s ^ step) for s in range(n_seq)])
        step *= 2
    step = 1
    while step < n_dp:
        d_weight = d_weight + lax.ppermute(d_weight, "dp", [(s, s ^ step) for s in range(n_dp)])
        step *= 2
    incoming = lax.ppermute(rim_grad.astype(bf16), "seq", [(s, s - 1) for s in range(G, n_seq, G)])

    output = of_members(o[:, :, DK:])
    d_rows = jnp.concatenate(
        [of_members(o[:, :, :DK]), of_members(dx[:, :length, :DK]), of_members(dx[:, :length, DK:])], -1
    )
    d_tail = (d_rows[-3:].astype(f32) + incoming.astype(f32)).astype(bf16)
    d_rows = jnp.concatenate([d_rows[:-3], d_tail], 0)
    gates = dx[:, length : length + 6 * per_key, :DK].astype(f32).reshape(G, 3, 2, per_key, length)
    gates = gates[:, 0] + (gates[:, 1] + gates[:, 2])
    d_decay, d_beta = gates[:, 0].reshape(heads, length), gates[:, 1].reshape(heads, length)
    return (output[None], d_rows[None], d_weight, d_decay[None], d_beta[None])


def solution(mesh):
    in_specs = (
        P("dp", "seq", None),
        P(),
        P("dp", None, "seq"),
        P("dp", None, "seq"),
        P("dp", "seq"),
        P("dp", "seq", None),
    )
    out_specs = (
        P("dp", "seq", None),
        P("dp", "seq", None),
        P(),
        P("dp", None, "seq"),
        P("dp", None, "seq"),
    )
    return jax.shard_map(
        local, mesh=mesh, in_specs=in_specs, out_specs=out_specs, check_vma=False
    )
```

time: 166 us -> 140 us (0.84)
  the two profiles are of different devices: /device:TPU:0 before, /device:TPU:8 now
where the time goes in v2:
time: 140 us
  Pallas kernels  51.7 us (37%)
  waiting for transfers between devices  33.3 us (24%)
  starting transfers between devices  32.1 us (23%)
  local copies, waits for them, and re-layouts  13.5 us (10%)
  other arithmetic  7.14 us (5%)
  between operations  1.81 us (1%)
    pallas_call x4, Pallas kernels, call(): pl.pallas_call(functools.partial(kernel, per_key, count), grid=(steps,),...  51.7 us
    all_to_all x4, starting transfers between devices, swap(): return lax.all_to_all(x, 'seq', 0, 0, axis_index_groups=team)  16.7 us
    ppermute x1, waiting for transfers between devices, local(): lax.ppermute(d_weight, 'seq', [(s, s ^ step) for s in range(n_seq)])  12 us
    all_to_all x4, waiting for transfers between devices, swap(): return lax.all_to_all(x, 'seq', 0, 0, axis_index_groups=team)  10.4 us
    ppermute x3, waiting for transfers between devices, local(): other = lax.ppermute(gathered, 'seq', [(s, s ^ step) for s in range(n_seq)])  7.59 us
    unnamed x28, local copies, waits for them, and re-layouts  7.58 us
    ppermute x3, starting transfers between devices, shifted(): lax.ppermute(x, 'seq', [(s, s + by) for s in range(n_seq) if 0 <= s + by...  7.56 us
    ppermute x1, starting transfers between devices, local(): lax.ppermute(d_weight, 'seq', [(s, s ^ step) for s in range(n_seq)])  3.6 us
  transfers between devices with their start and end apart: 13, of which 7 were waited for; matrix products, arithmetic and copies ran while one was open for 7% of the time, Pallas kernels for 37%

profile of v2, /device:TPU:8, one launch (start us, length us, event | category | flops | bytes accessed | tf_op | source)
XLA Modules:
  0.0 139.6 jit_solution(4010471854631862358)
XLA Ops:
  0.6 0.9 slice_bitcast_fusion.6
  1.5 0.7 convert_bitcast_fusion.1
  2.3 1.9 %collective-permute-start = (bf16[4,4096]{1,0:T(4,128)(2,1)S(1)}, bf16[4,4096]{1,0:T(4,128)(2,1)S(1)}, u32[]{:S(2)}, u32[]{:S(2)}) collective-permute-start(bf16[4,4096]{1,0:T(4,128)(2,1)S(1)} %pad_maximum_fusion.3), channel_id=1, source_target_pairs={{0,1},{1,2},{2,3},{3,4},{4,5},{5,6},{6,7},{7,8},{8,9},{9,10},{10,1... | collective-permute-start | bytes 98312 | tf_op jit(solution)/shard_map/ppermute | solution.py:405
  4.3 1.6 %copy.87 = bf16[1,128,4096]{1,2,0:T(8,128)(2,1)S(1)} copy(bf16[1,128,4096]{2,1,0:T(8,128)(2,1)} %param.6) | data formatting | bytes 2097152 | tf_op args[0]
  6.1 0.5 copy-done.11
  7.0 1.4 %collective-permute-done = bf16[4,4096]{1,0:T(4,128)(2,1)S(1)} collective-permute-done((bf16[4,4096]{1,0:T(4,128)(2,1)S(1)}, bf16[4,4096]{1,0:T(4,128)(2,1)S(1)}, u32[]{:S(2)}, u32[]{:S(2)}) %collective-permute-start) | collective-permute-done | bytes 32800 | tf_op jit(solution)/shard_map/ppermute | solution.py:405
  8.5 0.6 convert_reduce_fusion
  9.9 1.0 pad_maximum_fusion.1
  11.0 4.2 %all-to-all-start = ((bf16[8,144,384]{2,1,0:T(8,128)(2,1)}), bf16[8,144,384]{2,1,0:T(8,128)(2,1)S(1)}, u32[]{:S(2)}, u32[]{:S(2)}) async-start(bf16[8,144,384]{2,1,0:T(8,128)(2,1)} %pad_maximum_fusion.1), calls=%async_computation | async-start | bytes 1769472 | tf_op jit(solution)/shard_map/all_to_all | solution.py:417
  15.9 1.0 fusion.1
  17.0 10.4 %all-to-all-done.x_ref = bf16[8,144,384]{2,1,0:T(8,128)(2,1)S(1)} async-done(((bf16[8,144,384]{2,1,0:T(8,128)(2,1)}), bf16[8,144,384]{2,1,0:T(8,128)(2,1)S(1)}, u32[]{:S(2)}, u32[]{:S(2)}) %all-to-all-start) | async-done | bytes 884768 | tf_op jit(solution)/shard_map/all_to_all | solution.py:417
  27.3 4.0 %all-to-all-start.1 = ((bf16[8,144,384]{2,1,0:T(8,128)(2,1)}), bf16[8,144,384]{2,1,0:T(8,128)(2,1)S(1)}, u32[]{:S(2)}, u32[]{:S(2)}) async-start(bf16[8,144,384]{2,1,0:T(8,128)(2,1)} %fusion.1), calls=%async_computation.1 | async-start | bytes 1769472 | tf_op jit(solution)/shard_map/all_to_all | solution.py:417
  31.4 0.6 dynamic-slice_bitcast_fusion.w_ref
  32.0 0.6 fusion.15.w_ref
  32.6 17.8 %keys.1 = (f32[8,128,128]{2,1,0:T(8,128)}, f32[8,2,128,128]{3,2,1,0:T(8,128)}, f32[8,2,128,128]{3,2,1,0:T(8,128)}, f32[8,2,128,128]{3,2,1,0:T(8,128)}, f32[8,2,1...) custom-call(bf16[8,144,384]{2,1,0:T(8,128)(2,1)} %copy-done.1, ...), custom_call_target="tpu_custom_call" | custom-call | flops 15000000512 | bytes 8388608 | tf_op jit(solution)/shard_map/keys/pallas_call | solution.py:458
  50.3 4.4 %collective-permute-start.1 = (f32[2,128,128]{2,1,0:T(8,128)}, f32[2,128,128]{2,1,0:T(8,128)S(1)}, u32[]{:S(2)}, u32[]{:S(2)}) collective-permute-start(f32[2,128,128]{2,1,0:T(8,128)} %get-tuple-element.35), channel_id=1, source_target_pairs={{0,8},{1,9},{2,10},{3,11},{4,12},{5,13},{6,14},{7,15},{16,24},{17,... | collective-permute-start | bytes 393224 | tf_op jit(solution)/shard_map/ppermute | solution.py:405
  54.7 0.9 copy-done.2
  55.7 8.9 %queries.1 = (f32[8,2,128,128]{3,2,1,0:T(8,128)}, f32[8,2,128,128]{3,2,1,0:T(8,128)}, f32[8,2,128,128]{3,2,1,0:T(8,128)}, f32[8,2,128,128]{3,2,1,0:T(8,128)}, f3...) custom-call(bf16[8,144,384]{2,1,0:T(8,128)(2,1)} %copy-done.1, ...), custom_call_target="tpu_custom_call" | custom-call | flops 8000000000 | bytes 8388608 | tf_op jit(solution)/shard_map/queries/pallas_call | solution.py:458
  64.6 1.3 collective-permute-start.2
  65.9 0.6 copy-done.10
  66.6 9.2 %reads.1 = (bf16[8,128,384]{2,1,0:T(8,128)(2,1)}, f32[8,2,128,128]{3,2,1,0:T(8,128)}, f32[8,2,128,128]{3,2,1,0:T(8,128)}, f32[8,128,128]{2,1,0:T(8,128)}, f32[8,...) custom-call(f32[2,128,128]{2,1,0:T(8,128)} %copy-done.10, bf16[8,144,384]{2,1,0:T(8,128)(2,1)} %copy-done.1, ...), custom_call_target="tpu_custom_call" | custom-call | flops 8000000000 | bytes 8388608 | tf_op jit(solution)/shard_map/reads/pallas_call | solution.py:458
  75.8 4.2 %all-to-all-start.2 = ((bf16[8,128,384]{2,1,0:T(8,128)(2,1)}), bf16[8,128,384]{2,1,0:T(8,128)(2,1)S(1)}, u32[]{:S(2)}, u32[]{:S(2)}) async-start(bf16[8,128,384]{2,1,0:T(8,128)(2,1)} %get-tuple-element.47), calls=%async_computation.2 | async-start | bytes 1572864 | tf_op jit(solution)/shard_map/all_to_all | solution.py:417
  80.0 0.6 copy-done.9
  80.7 15.7 %writes.1 = (bf16[8,144,384]{2,1,0:T(8,128)(2,1)}, f32[3,384]{1,0:T(4,128)}, f32[4,384]{1,0:T(4,128)}) custom-call(f32[2,128,128]{2,1,0:T(8,128)} %copy-done.9, bf16[8,144,384]{2,1,0:T(8,128)(2,1)} %copy-done.1, f32[4,384]{1,0:T(4,128)} %fusion.15.w_ref, f32[8,128,128]{2,1,0:T(8,128)} %get-tuple-element.37.k_ref, ...), custom_call_target="tpu_custom_call" | custom-call | flops 15000000512 | bytes 8388608 | tf_op jit(solution)/shard_map/writes/pallas_call | solution.py:458
  96.4 0.7 maximum_bitcast_fusion.1
  97.3 1.0 collective-permute-done.3
  98.4 1.5 %collective-permute-start.4 = (f32[2,7,512]{2,1,0:T(8,128)S(1)}, f32[2,7,512]{2,1,0:T(8,128)S(1)}, u32[]{:S(2)}, u32[]{:S(2)}) collective-permute-start(f32[2,7,512]{2,1,0:T(8,128)S(1)} %maximum_select_fusion.2), channel_id=1, source_target_pairs={{0,2},{1,3},{2,0},{3,1},{4,6},{5,7},{6,4},{7,5},{8,10},{9,11},{10,... | collective-permute-start | bytes 86024 | tf_op jit(solution)/shard_map/ppermute | solution.py:507
  99.8 2.5 %collective-permute-done.4 = f32[2,7,512]{2,1,0:T(8,128)S(1)} collective-permute-done((f32[2,7,512]{2,1,0:T(8,128)S(1)}, f32[2,7,512]{2,1,0:T(8,128)S(1)}, u32[]{:S(2)}, u32[]{:S(2)}) %collective-permute-start.4) | collective-permute-done | bytes 28704 | tf_op jit(solution)/shard_map/ppermute | solution.py:507
  102.5 4.1 %collective-permute-done.5 = f32[4,7,512]{2,1,0:T(8,128)S(1)} collective-permute-done((f32[4,7,512]{2,1,0:T(8,128)S(1)}, f32[4,7,512]{2,1,0:T(8,128)S(1)}, u32[]{:S(2)}, u32[]{:S(2)}) %collective-permute-start.5) | collective-permute-done | bytes 57376 | tf_op jit(solution)/shard_map/ppermute | solution.py:507
  106.7 4.2 %all-to-all-start.3 = ((bf16[8,144,384]{2,1,0:T(8,128)(2,1)}), bf16[8,144,384]{2,1,0:T(8,128)(2,1)S(1)}, u32[]{:S(2)}, u32[]{:S(2)}) async-start(bf16[8,144,384]{2,1,0:T(8,128)(2,1)} %get-tuple-element.58), calls=%async_computation.3 | async-start | bytes 1769472 | tf_op jit(solution)/shard_map/all_to_all | solution.py:417
  111.0 3.6 %collective-permute-start.7 = (f32[4,4096]{1,0:T(4,128)S(1)}, f32[4,4096]{1,0:T(4,128)S(1)}, u32[]{:S(2)}, u32[]{:S(2)}) collective-permute-start(f32[4,4096]{1,0:T(4,128)S(1)} %slice.152), channel_id=1, source_target_pairs={{0,8},{1,9},{2,10},{3,11},{4,12},{5,13},{6,14},{7,15},{8,0},{9,1},... | collective-permute-start | bytes 196616 | tf_op jit(solution)/shard_map/ppermute | solution.py:516
  114.5 12.0 %collective-permute-done.7 = f32[4,4096]{1,0:T(4,128)S(1)} collective-permute-done((f32[4,4096]{1,0:T(4,128)S(1)}, f32[4,4096]{1,0:T(4,128)S(1)}, u32[]{:S(2)}, u32[]{:S(2)}) %collective-permute-start.7) | collective-permute-done | bytes 65568 | tf_op jit(solution)/shard_map/ppermute | solution.py:516
  126.6 1.6 %collective-permute-start.8 = (f32[4,4096]{1,0:T(4,128)S(1)}, f32[4,4096]{1,0:T(4,128)S(1)}, u32[]{:S(2)}, u32[]{:S(2)}) collective-permute-start(f32[4,4096]{1,0:T(4,128)S(1)} %slice_add_fusion.1), channel_id=1, source_target_pairs={{0,16},{16,0},{1,17},{17,1},{2,18},{18,2},{3,19},{19,3},{4,20},{20... | collective-permute-start | bytes 196616 | tf_op jit(solution)/shard_map/ppermute | solution.py:520
  128.1 0.8 collective-permute-start.6
  129.0 1.9 %collective-permute-done.8 = f32[4,4096]{1,0:T(4,128)S(1)} collective-permute-done((f32[4,4096]{1,0:T(4,128)S(1)}, f32[4,4096]{1,0:T(4,128)S(1)}, u32[]{:S(2)}, u32[]{:S(2)}) %collective-permute-start.8) | collective-permute-done | bytes 65568 | tf_op jit(solution)/shard_map/ppermute | solution.py:520
  130.9 0.6 add.69
  131.8 0.3 copy.102
  132.1 1.0 copy.111
  133.1 0.3 copy.105
  133.4 0.6 copy-done
  134.4 0.4 slice.147
  134.7 0.4 copy.106
  135.1 0.5 copy.107
  135.6 0.6 maximum_bitcast_fusion
  136.2 1.3 copy.112
  137.5 0.8 slice_convert_fusion.1
  138.4 0.6 copy.109
  139.0 0.6 copy.110
  (73 shorter events, 2.7 us)
Async XLA Ops:
  2.3 3.6 %copy-start.5 = (f32[1,16,128]{2,1,0:T(8,128)S(1)}, f32[1,16,128]{2,1,0:T(8,128)}, u32[]{:S(2)}) copy-start(f32[1,16,128]{2,1,0:T(8,128)} %param.8) | copy-start | bytes 24580
  2.3 3.6 %copy-start.6 = (f32[1,16,128]{2,1,0:T(8,128)S(1)}, f32[1,16,128]{2,1,0:T(8,128)}, u32[]{:S(2)}) copy-start(f32[1,16,128]{2,1,0:T(8,128)} %param.9) | copy-start | bytes 24580
  2.3 6.1 %collective-permute-start = (bf16[4,4096]{1,0:T(4,128)(2,1)S(1)}, bf16[4,4096]{1,0:T(4,128)(2,1)S(1)}, u32[]{:S(2)}, u32[]{:S(2)}) collective-permute-start(bf16[4,4096]{1,0:T(4,128)(2,1)S(1)} %pad_maximum_fusion.3), channel_id=1, source_target_pairs={{0,1},{1,2},{2,3},{3,4},{4,5},{5,6},{6,7},{7,8},{8,9},{9,10},{10,1... | collective-permute-start | bytes 98312 | tf_op jit(solution)/shard_map/ppermute | solution.py:405
  5.9 0.7 copy-start.11
  11.0 4.2 %copy-start.4 = (bf16[4,4096]{1,0:T(4,128)(2,1)S(1)}, bf16[4,4096]{1,0:T(4,128)(2,1)}, u32[]{:S(2)}) copy-start(bf16[4,4096]{1,0:T(4,128)(2,1)} %param.7) | copy-start | bytes 98308
  11.0 4.4 %copy-start.3 = (bf16[1,128,2048]{2,1,0:T(8,128)(2,1)S(1)}, bf16[1,128,2048]{2,1,0:T(8,128)(2,1)}, u32[]{:S(2)}) copy-start(bf16[1,128,2048]{2,1,0:T(8,128)(2,1)} %param.11) | copy-start | bytes 1572868
  11.0 16.4 %all-to-all-start = ((bf16[8,144,384]{2,1,0:T(8,128)(2,1)}), bf16[8,144,384]{2,1,0:T(8,128)(2,1)S(1)}, u32[]{:S(2)}, u32[]{:S(2)}) async-start(bf16[8,144,384]{2,1,0:T(8,128)(2,1)} %pad_maximum_fusion.1), calls=%async_computation | async-start | bytes 1769472 | tf_op jit(solution)/shard_map/all_to_all | solution.py:417
  27.3 5.2 %copy-start.1 = (bf16[8,144,384]{2,1,0:T(8,128)(2,1)}, bf16[8,144,384]{2,1,0:T(8,128)(2,1)S(1)}, u32[]{:S(2)}) copy-start(bf16[8,144,384]{2,1,0:T(8,128)(2,1)S(1)} %all-to-all-done.x_ref) | copy-start | bytes 2654212
  27.3 27.4 %all-to-all-start.1 = ((bf16[8,144,384]{2,1,0:T(8,128)(2,1)}), bf16[8,144,384]{2,1,0:T(8,128)(2,1)S(1)}, u32[]{:S(2)}, u32[]{:S(2)}) async-start(bf16[8,144,384]{2,1,0:T(8,128)(2,1)} %fusion.1), calls=%async_computation.1 | async-start | bytes 1769472 | tf_op jit(solution)/shard_map/all_to_all | solution.py:417
  50.3 15.6 %collective-permute-start.1 = (f32[2,128,128]{2,1,0:T(8,128)}, f32[2,128,128]{2,1,0:T(8,128)S(1)}, u32[]{:S(2)}, u32[]{:S(2)}) collective-permute-start(f32[2,128,128]{2,1,0:T(8,128)} %get-tuple-element.35), channel_id=1, source_target_pairs={{0,8},{1,9},{2,10},{3,11},{4,12},{5,13},{6,14},{7,15},{16,24},{17,... | collective-permute-start | bytes 393224 | tf_op jit(solution)/shard_map/ppermute | solution.py:405
  54.7 0.9 copy-start.2
  64.6 15.4 %collective-permute-start.2 = (f32[2,128,128]{2,1,0:T(8,128)}, f32[2,128,128]{2,1,0:T(8,128)S(1)}, u32[]{:S(2)}, u32[]{:S(2)}) collective-permute-start(f32[2,128,128]{2,1,0:T(8,128)} %get-tuple-element.48), channel_id=1, source_target_pairs={{8,0},{9,1},{10,2},{11,3},{12,4},{13,5},{14,6},{15,7},{24,16},{25,... | collective-permute-start | bytes 393224 | tf_op jit(solution)/shard_map/ppermute | solution.py:405
  65.9 0.6 copy-start.10
  75.8 30.9 %all-to-all-start.2 = ((bf16[8,128,384]{2,1,0:T(8,128)(2,1)}), bf16[8,128,384]{2,1,0:T(8,128)(2,1)S(1)}, u32[]{:S(2)}, u32[]{:S(2)}) async-start(bf16[8,128,384]{2,1,0:T(8,128)(2,1)} %get-tuple-element.47), calls=%async_computation.2 | async-start | bytes 1572864 | tf_op jit(solution)/shard_map/all_to_all | solution.py:417
  80.0 0.6 copy-start.9
  80.6 15.8 %copy-start.7 = (f32[3,128]{1,0:T(4,128)S(1)}, f32[3,128]{1,0:T(4,128)}, u32[]{:S(2)}) copy-start(f32[3,128]{1,0:T(4,128)} %get-tuple-element.61) | copy-start | bytes 4612
  80.7 15.8 %copy-start.8 = (f32[4,128]{1,0:T(4,128)S(1)}, f32[4,128]{1,0:T(4,128)}, u32[]{:S(2)}) copy-start(f32[4,128]{1,0:T(4,128)} %get-tuple-element.59) | copy-start | bytes 6148
  97.1 1.2 collective-permute-start.3
  98.4 3.9 %collective-permute-start.4 = (f32[2,7,512]{2,1,0:T(8,128)S(1)}, f32[2,7,512]{2,1,0:T(8,128)S(1)}, u32[]{:S(2)}, u32[]{:S(2)}) collective-permute-start(f32[2,7,512]{2,1,0:T(8,128)S(1)} %maximum_select_fusion.2), channel_id=1, source_target_pairs={{0,2},{1,3},{2,0},{3,1},{4,6},{5,7},{6,4},{7,5},{8,10},{9,11},{10,... | collective-permute-start | bytes 86024 | tf_op jit(solution)/shard_map/ppermute | solution.py:507
  102.3 4.3 %collective-permute-start.5 = (f32[4,7,512]{2,1,0:T(8,128)S(1)}, f32[4,7,512]{2,1,0:T(8,128)S(1)}, u32[]{:S(2)}, u32[]{:S(2)}) collective-permute-start(f32[4,7,512]{2,1,0:T(8,128)S(1)} %maximum_select_fusion.1), channel_id=1, source_target_pairs={{0,4},{1,5},{2,6},{3,7},{4,0},{5,1},{6,2},{7,3},{8,12},{9,13},{10,... | collective-permute-start | bytes 172040 | tf_op jit(solution)/shard_map/ppermute | solution.py:507
  106.7 26.4 %all-to-all-start.3 = ((bf16[8,144,384]{2,1,0:T(8,128)(2,1)}), bf16[8,144,384]{2,1,0:T(8,128)(2,1)S(1)}, u32[]{:S(2)}, u32[]{:S(2)}) async-start(bf16[8,144,384]{2,1,0:T(8,128)(2,1)} %get-tuple-element.58), calls=%async_computation.3 | async-start | bytes 1769472 | tf_op jit(solution)/shard_map/all_to_all | solution.py:417
  111.0 15.6 %collective-permute-start.7 = (f32[4,4096]{1,0:T(4,128)S(1)}, f32[4,4096]{1,0:T(4,128)S(1)}, u32[]{:S(2)}, u32[]{:S(2)}) collective-permute-start(f32[4,4096]{1,0:T(4,128)S(1)} %slice.152), channel_id=1, source_target_pairs={{0,8},{1,9},{2,10},{3,11},{4,12},{5,13},{6,14},{7,15},{8,0},{9,1},... | collective-permute-start | bytes 196616 | tf_op jit(solution)/shard_map/ppermute | solution.py:516
  126.6 4.3 %collective-permute-start.8 = (f32[4,4096]{1,0:T(4,128)S(1)}, f32[4,4096]{1,0:T(4,128)S(1)}, u32[]{:S(2)}, u32[]{:S(2)}) collective-permute-start(f32[4,4096]{1,0:T(4,128)S(1)} %slice_add_fusion.1), channel_id=1, source_target_pairs={{0,16},{16,0},{1,17},{17,1},{2,18},{18,2},{3,19},{19,3},{4,20},{20... | collective-permute-start | bytes 196616 | tf_op jit(solution)/shard_map/ppermute | solution.py:520
  128.1 7.0 %collective-permute-start.6 = (bf16[3,4096]{1,0:T(4,128)(2,1)S(1)}, bf16[3,4096]{1,0:T(4,128)(2,1)S(1)}, u32[]{:S(2)}, u32[]{:S(2)}) collective-permute-start(bf16[3,4096]{1,0:T(4,128)(2,1)S(1)} %slice.183), channel_id=1, source_target_pairs={{8,7},{24,23}} | collective-permute-start | bytes 73736 | tf_op jit(solution)/shard_map/ppermute | solution.py:522
  133.1 0.9 copy-start

commit v3 on v2

--- a/solution.py
+++ b/solution.py
@@ -11,7 +11,7 @@
 DOC_MOST = 1024
 EPS = 1e-6
 CODE = 16
-COUNTS = (2, 2, 2, 2)
+COUNTS = (4, 4, 2, 4)
 VMEM = 56 << 20
 RIM = 16
 f32 = jnp.float32
@@ -44,18 +44,19 @@
     return lax.broadcasted_iota(jnp.int32, shape, dim)
 
 
-def conv_inputs(x_ref, n, width, shift_ref, docs):
+def conv_inputs(x_ref, n, width, shift_ref, docs, lane=0):
     length = docs.shape[0]
-    shift_ref[5:8, :width] = x_ref[n, length : length + 3, :width].astype(f32)
-    rows = x_ref[n, :length, :width].astype(f32)
-    shift_ref[8 : 8 + length, :width] = rows
+    to = slice(0, width)
+    shift_ref[5:8, to] = x_ref[n, length : length + 3, lane : lane + width].astype(f32)
+    rows = x_ref[n, :length, lane : lane + width].astype(f32)
+    shift_ref[8 : 8 + length, to] = rows
     at = iota2((length, DK), 0)
     first = docs[0:1, :]
     taps = [rows]
     for off in (1, 2, 3):
         earlier = jnp.where(at >= off, pltpu.roll(docs, off, 0), first)
         ok = earlier == docs
-        moved = shift_ref[8 - off : 8 - off + length, :width]
+        moved = shift_ref[8 - off : 8 - off + length, to]
         taps.append(jnp.where(wide(ok, width), moved, 0.0))
     return taps
 
@@ -129,7 +130,7 @@
         row_sums = dg(numbers, until, 1, 0)
         ones = jnp.ones((length, DK), bf16)
         self.c_row, self.c_col, self.beta, self.beta_row = [], [], [], []
-        self.entry, self.tail, self.keep = [], [], []
+        self.entry, self.tail, self.keep, self.both = [], [], [], []
         for h in range(per_key):
             at = 4 + 3 * h
             self.c_row.append(row_sums[at : at + 1] + row_sums[at + 1 : at + 2] + row_sums[at + 2 : at + 3])
@@ -144,6 +145,7 @@
             last = self.c_row[h][:, length - 1 : length]
             self.tail.append(jnp.where(ending, jnp.exp(jnp.minimum(last - c_col, 0.0)), 0.0))
             self.keep.append(self.entry[h][length - 1 : length, :])
+            self.both.append(self.beta[h] * self.entry[h])
 
     def fading(self, h):
         gap = jnp.minimum(self.c_col[h] - self.c_row[h], 0.0)
@@ -170,19 +172,14 @@
     return inv
 
 
-def rows_from(x):
-    ones = jnp.ones((8, x.shape[1]), bf16)
-    return mm((ones,), split(x), 1, 1)[0:1]
-
-
-def three_rows(x):
-    hi = x.astype(bf16).astype(f32)
-    mid = (x - hi).astype(bf16).astype(f32)
-    return jnp.concatenate([hi, mid, x - hi - mid], 0)
-
-
-def key_kernel(per_key, count, x_ref, w_ref, k_ref, f_ref, n_ref, t_ref, w_out, u_ref, a_ref, m_ref, s_ref, end_ref,
-               chain, shift_ref):
+def rows_from(xs):
+    wide_x = split(jnp.concatenate(xs, 1))
+    shape = (len(xs) * DK, DK)
+    pick = ((iota2(shape, 0) // DK) == iota2(shape, 1)).astype(f32).astype(bf16)
+    return mm(wide_x, (pick,), 1, 0).T
+
+
+def key_kernel(per_key, count, x_ref, w_ref, k_ref, t_ref, w_out, u_ref, a_ref, m_ref, s_ref, end_ref, chain, shift_ref):
     step = pl.program_id(0)
     length = k_ref.shape[1]
     own = w_ref.shape[1]
@@ -207,18 +204,18 @@
         vs.append(act[:, DK:])
     sk = [split(k) for k in ks]
     kk = [mm(s, s, 1, 1) for s in sk]
-    fs = [metas[n].fading(h) for n, h in pairs]
-    ns = [jnp.where(metas[n].strict, metas[n].beta[h] * kk[n] * f, 0.0) for (n, h), f in zip(pairs, fs)]
+    ns = [
+        jnp.where(metas[n].strict, metas[n].beta[h] * kk[n] * metas[n].fading(h), 0.0) for n, h in pairs
+    ]
     ts = inverse(ns)
     rhs = [
-        jnp.concatenate([metas[n].beta[h] * metas[n].entry[h] * ks[n], metas[n].beta[h] * vs[n][:, h * DK : (h + 1) * DK]], 1)
+        jnp.concatenate([metas[n].both[h] * ks[n], metas[n].beta[h] * vs[n][:, h * DK : (h + 1) * DK]], 1)
         for n, h in pairs
     ]
     wu = [mm(split(t), split(r), 1, 0) for t, r in zip(ts, rhs)]
     kwu = [mm(split(metas[n].tail[h] * ks[n]), split(x), 0, 0) for (n, h), x in zip(pairs, wu)]
     for m, (n, h) in enumerate(pairs):
-        f_ref[n, h], n_ref[n, h], t_ref[n, h] = fs[m], ns[m], ts[m]
-        w_out[n, h], u_ref[n, h] = wu[m][:, :DK], wu[m][:, DK:]
+        t_ref[n, h], w_out[n, h], u_ref[n, h] = ts[m], wu[m][:, :DK], wu[m][:, DK:]
         a = metas[n].keep[h] * eye - kwu[m][:, :DK]
         a_ref[n, h] = a
         now = chain[h]
@@ -229,8 +226,7 @@
         end_ref[h] = chain[h, :, DK:]
 
 
-def query_kernel(per_key, count, x_ref, y_ref, w_ref, k_ref, f_ref, w_in, u_ref, a_ref, p_ref, y_out, pu_ref, r_ref,
-                 m_ref, g_ref, start_ref, chain, shift_ref):
+def query_kernel(per_key, count, x_ref, y_ref, w_ref, k_ref, t_ref, a_ref, e_ref, m_ref, g_ref, start_ref, chain, shift_ref):
     step = pl.program_id(0)
     length = k_ref.shape[1]
     eye = (iota2((DK, DK), 0) == iota2((DK, DK), 1)).astype(f32)
@@ -242,23 +238,25 @@
 
     w = w_ref[...]
     pairs = [(n, h) for n in reversed(range(count)) for h in range(per_key)]
-    metas, qs, qk = {}, {}, {}
+    metas, sq, sk, qk = {}, {}, {}, {}
     for n in range(count):
         metas[n] = Meta(x_ref[n, length:, :DK], per_key)
         z = conv_out(conv_inputs(y_ref, n, DK, shift_ref.at[n], metas[n].code), w)
         q, _ = unit(z * sigmoid(z))
-        qs[n] = q * DK**-0.5
-        qk[n] = mm(split(qs[n]), split(k_ref[n]), 1, 1)
-    ps = [qk[n] * f_ref[n, h] for n, h in pairs]
-    sp = [split(p) for p in ps]
-    swu = [cat([split(w_in[n, h]), split(u_ref[n, h])], 1) for n, h in pairs]
-    pwu = [mm(p, s, 1, 0) for p, s in zip(sp, swu)]
-    ys = [metas[n].entry[h] * qs[n] - x[:, :DK] for (n, h), x in zip(pairs, pwu)]
+        sq[n], sk[n] = split(q * DK**-0.5), split(k_ref[n])
+        qk[n] = mm(sq[n], sk[n], 1, 1)
     dos = [(y_ref[n, :length, (h + 1) * DK : (h + 2) * DK],) for n, h in pairs]
-    gs = [mm(split(y), d, 0, 0) for y, d in zip(ys, dos)]
-    rs = [mm(p, d, 0, 0) for p, d in zip(sp, dos)]
+    rs = [mm(split(qk[n] * metas[n].fading(h)), d, 0, 0) for (n, h), d in zip(pairs, dos)]
+    es = [mm(split(t_ref[n, h]), split(r), 0, 0) for (n, h), r in zip(pairs, rs)]
+    gs = []
+    for at in range(0, len(pairs), per_key):
+        n = pairs[at][0]
+        asked = jnp.concatenate([metas[n].entry[h] * dos[at + h][0].astype(f32) for h in range(per_key)], 1)
+        undone = jnp.concatenate([-metas[n].both[h] * es[at + h] for h in range(per_key)], 1)
+        b = mm(cat([sq[n], sk[n]], 0), cat([split(asked), split(undone)], 0), 0, 0)
+        gs += [b[:, h * DK : (h + 1) * DK] for h in range(per_key)]
     for m, (n, h) in enumerate(pairs):
-        p_ref[n, h], y_out[n, h], pu_ref[n, h], r_ref[n, h] = ps[m], ys[m], pwu[m][:, DK:], rs[m]
+        e_ref[n, h] = es[m]
         now = chain[h]
         m_ref[n, h], g_ref[n, h] = now[:, :DK], now[:, DK:]
         later = mm(split(a_ref[n, h]), split(now), 0, 0)
@@ -267,8 +265,8 @@
         start_ref[h] = chain[h, :, DK:]
 
 
-def read_kernel(per_key, count, in_ref, x_ref, y_ref, w_ref, k_ref, f_ref, p_ref, w_in, u_ref, y_in, pu_ref, m_ref,
-                sl_ref, out_ref, d_ref, s_ref, dk_ref, dc_ref, rim_ref, dw_ref, shift_ref, dz_ref, doc_next):
+def read_kernel(per_key, count, in_ref, x_ref, y_ref, w_ref, k_ref, w_in, u_ref, m_ref, sl_ref, out_ref, d_ref, s_ref,
+                dk_ref, dc_ref, rim_ref, dw_ref, shift_ref, dz_ref, doc_next):
     length = k_ref.shape[1]
 
     @pl.when(pl.program_id(0) == 0)
@@ -280,7 +278,7 @@
     w = w_ref[...]
     s_in = [split(in_ref[h]) for h in range(per_key)]
     pairs = [(n, h) for n in reversed(range(count)) for h in range(per_key)]
-    metas, taps, sig, zs, hats, inv, qs, sq, sk = {}, {}, {}, {}, {}, {}, {}, {}, {}
+    metas, taps, sig, zs, hats, inv, qs, sq, sk, qk = {}, {}, {}, {}, {}, {}, {}, {}, {}, {}
     for n in range(count):
         metas[n] = Meta(x_ref[n, length:, :DK], per_key)
         taps[n] = conv_inputs(y_ref, n, DK, shift_ref.at[n], metas[n].code)
@@ -289,24 +287,33 @@
         hats[n], inv[n] = unit(zs[n] * sig[n])
         qs[n] = hats[n] * DK**-0.5
         sq[n], sk[n] = split(qs[n]), split(k_ref[n])
+        qk[n] = mm(sq[n], sk[n], 1, 1)
     states = [sl_ref[n, h] + mm(split(m_ref[n, h]), s_in[h], 1, 0) for n, h in pairs]
     ss = [split(s) for s in states]
-    both = [mm(cat([split(w_in[n, h]), split(y_in[n, h])], 0), s, 1, 0) for (n, h), s in zip(pairs, ss)]
-    ds = [u_ref[n, h] - x[:length] for (n, h), x in zip(pairs, both)]
+    fs = [metas[n].fading(h) for n, h in pairs]
+    ds = [u_ref[n, h] - mm(split(w_in[n, h]), s, 1, 0) for (n, h), s in zip(pairs, ss)]
+    sd = [split(d) for d in ds]
+    qss = {n: mm(sq[n], cat([ss[m] for m in range(len(pairs)) if pairs[m][0] == n], 1), 1, 0) for n in range(count)}
+    outs = [
+        metas[n].entry[h] * qss[n][:, h * DK : (h + 1) * DK] + mm(split(qk[n] * f), d, 1, 0)
+        for (n, h), f, d in zip(pairs, fs, sd)
+    ]
     dos = [(y_ref[n, :length, (h + 1) * DK : (h + 2) * DK],) for n, h in pairs]
-    dps = [mm(do, split(d), 1, 1) for do, d in zip(dos, ds)]
-    enters = [metas[n].entry[h] * mm(do, s, 1, 1) for (n, h), do, s in zip(pairs, dos, ss)]
-    dpf = [split(dp * f_ref[n, h]) for (n, h), dp in zip(pairs, dps)]
-    dqs = [e + mm(x, sk[n], 1, 0) for (n, h), e, x in zip(pairs, enters, dpf)]
-    dks = [mm(x, sq[n], 0, 0) for (n, h), x in zip(pairs, dpf)]
+    back = [mm(do, cat([d, s], 0), 1, 1) for do, d, s in zip(dos, sd, ss)]
+    dps = [x[:, :length] * f for x, f in zip(back, fs)]
+    enters = [metas[n].entry[h] * x[:, length:] for (n, h), x in zip(pairs, back)]
     dq, dk = {}, {}
-    for m, (n, h) in enumerate(pairs):
-        s_ref[n, h], d_ref[n, h] = states[m], ds[m]
-        out_ref[n, :, (h + 1) * DK : (h + 2) * DK] = (both[m][length:] + pu_ref[n, h]).astype(bf16)
-        gaps = dps[m] * p_ref[n, h]
-        dc_ref[n, h : h + 1, :] = rows_from(gaps + enters[m] * qs[n]) - jnp.sum(gaps, 0, keepdims=True)
-        dq[n] = dq[n] + dqs[m] if h else dqs[m]
-        dk[n] = dk[n] + dks[m] if h else dks[m]
+    for n in range(count):
+        mine = [m for m in range(len(pairs)) if pairs[m][0] == n]
+        s_dp = split(sum(dps[m] for m in mine))
+        dq[n] = mm(s_dp, sk[n], 1, 0) + sum(enters[m] for m in mine)
+        dk[n] = mm(s_dp, sq[n], 0, 0)
+        gaps = [dps[m] * qk[n] for m in mine]
+        sums = rows_from([g + enters[m] * qs[n] for g, m in zip(gaps, mine)])
+        for h, m in enumerate(mine):
+            s_ref[n, h], d_ref[n, h] = states[m], ds[m]
+            out_ref[n, :, (h + 1) * DK : (h + 2) * DK] = outs[m].astype(bf16)
+            dc_ref[n, h : h + 1, :] = sums[h : h + 1] - jnp.sum(gaps[h], 0, keepdims=True)
     for n in reversed(range(count)):
         dk_ref[n] = dk[n]
         grad = unit_back(DK**-0.5 * dq[n], hats[n], inv[n])
@@ -315,12 +322,13 @@
         out_ref[n, :, :DK] = dx.astype(bf16)
 
 
-def write_kernel(per_key, count, in_ref, x_ref, w_ref, k_ref, f_ref, n_ref, t_ref, r_ref, m_ref, gl_ref, d_ref, s_ref,
-                 dk_ref, dc_ref, dx_ref, rim_ref, dw_ref, shift_ref, dz_ref, doc_next):
+def write_kernel(per_key, count, in_ref, x_ref, w_ref, k_ref, t_ref, e_ref, m_ref, gl_ref, d_ref, s_ref, dk_ref, dc_ref,
+                 dwq_ref, rimq_ref, dx_ref, gates_ref, small_ref, shift_ref, dz_ref, doc_next, dw_ref, rim_ref):
+    step, steps = pl.program_id(0), pl.num_programs(0)
     length = k_ref.shape[1]
     own = w_ref.shape[1]
 
-    @pl.when(pl.program_id(0) == 0)
+    @pl.when(step == 0)
     def _():
         dw_ref[...] = jnp.zeros_like(dw_ref)
         dz_ref[...] = jnp.zeros_like(dz_ref)
@@ -331,7 +339,7 @@
     from_here = (i >= j).astype(f32).astype(bf16)
     g_in = [split(in_ref[h]) for h in range(per_key)]
     pairs = [(n, h) for n in reversed(range(count)) for h in range(per_key)]
-    metas, taps, sig, zs, hats, inv, vs, sk = {}, {}, {}, {}, {}, {}, {}, {}
+    metas, taps, sig, zs, hats, inv, vs, sk, kk = {}, {}, {}, {}, {}, {}, {}, {}, {}
     for n in range(count):
         metas[n] = Meta(x_ref[n, length:, :DK], per_key)
         taps[n] = conv_inputs(x_ref, n, own, shift_ref.at[n], metas[n].code)
@@ -341,45 +349,107 @@
         hats[n], inv[n] = unit(act[:, :DK])
         vs[n] = act[:, DK:]
         sk[n] = split(k_ref[n])
+        kk[n] = mm(sk[n], sk[n], 1, 1)
     later = [gl_ref[n, h] + mm(split(m_ref[n, h]), g_in[h], 1, 0) for n, h in pairs]
     s_later = [split(x) for x in later]
     s_d = [split(d_ref[n, h]) for n, h in pairs]
     s_s = [split(s_ref[n, h]) for n, h in pairs]
-    x1 = [mm(split(metas[n].tail[h] * k_ref[n]), s, 1, 0) for (n, h), s in zip(pairs, s_later)]
-    es = [mm(split(t_ref[n, h]), split(r_ref[n, h] + x), 0, 0) for (n, h), x in zip(pairs, x1)]
+    kg = {n: mm(sk[n], cat([s_later[m] for m in range(len(pairs)) if pairs[m][0] == n], 1), 1, 0) for n in range(count)}
+    x1 = [metas[n].tail[h] * kg[n][:, h * DK : (h + 1) * DK] for n, h in pairs]
+    es = [e_ref[n, h] + mm(split(t_ref[n, h]), split(x), 0, 0) for (n, h), x in zip(pairs, x1)]
     se = [split(e) for e in es]
     ends = [metas[n].tail[h] * mm(d, s, 1, 1) for (n, h), d, s in zip(pairs, s_d, s_later)]
-    dns = [-mm(e, d, 1, 1) for e, d in zip(se, s_d)]
-    ess = [mm(e, s, 1, 1) for e, s in zip(se, s_s)]
+    back = [mm(e, cat([d, s], 0), 1, 1) for e, d, s in zip(se, s_d, s_s)]
+    ess = [x[:, length:] for x in back]
     dkk = [
-        split(jnp.where(metas[n].strict, dn * metas[n].beta[h] * f_ref[n, h], 0.0)) for (n, h), dn in zip(pairs, dns)
+        jnp.where(metas[n].strict, x[:, :length] * (-metas[n].beta[h] * metas[n].fading(h)), 0.0)
+        for (n, h), x in zip(pairs, back)
     ]
-    dks = [mm(x, sk[n], 1, 0) + mm(x, sk[n], 0, 0) for (n, h), x in zip(pairs, dkk)]
-    dk, dv, rows = {n: dk_ref[n] for n in range(count)}, {}, {}
-    for m, (n, h) in enumerate(pairs):
+    dk, dv, rows = {}, {}, {}
+    for n in range(count):
+        mine = [m for m in range(len(pairs)) if pairs[m][0] == n]
         meta, k = metas[n], k_ref[n]
-        bes = meta.beta[h] * meta.entry[h] * ess[m]
-        dk[n] = dk[n] + dks[m] - bes + ends[m]
-        dv[n, h] = meta.beta[h] * es[m]
-        nn = dns[m] * n_ref[n, h]
-        ek = ends[m] * k
-        dc = dc_ref[n, h : h + 1, :] + rows_from(nn - bes * k - ek) - jnp.sum(nn, 0, keepdims=True)
-        last = jnp.sum(ek + later[m] * s_ref[n, h] * meta.keep[h], 0, keepdims=True)
-        at_end = jnp.sum(last, 1, keepdims=True)
-        rows[n, h] = mm(split(jnp.broadcast_to(dc, (8, length))), (from_here,), 1, 0)[0:1] + at_end
-        own_v = vs[n][:, h * DK : (h + 1) * DK]
-        rows[n, per_key + h] = (
-            rows_from(es[m] * own_v - meta.entry[h] * ess[m] * k) + rows_from(nn) / meta.beta_row[h]
-        )
+        s_dkk = split(sum(dkk[m] for m in mine))
+        bes = [meta.both[h] * ess[m] for h, m in enumerate(mine)]
+        dk[n] = dk_ref[n] + mm(s_dkk, sk[n], 1, 0) + mm(s_dkk, sk[n], 0, 0) + sum(ends[m] - b for b, m in zip(bes, mine))
+        nn = [dkk[m] * kk[n] for m in mine]
+        ek = [ends[m] * k for m in mine]
+        mats = [x - b * k - y for x, b, y in zip(nn, bes, ek)] + nn
+        mats += [
+            es[m] * vs[n][:, h * DK : (h + 1) * DK] - meta.entry[h] * ess[m] * k for h, m in enumerate(mine)
+        ]
+        sums = rows_from(mats)
+        dc = [
+            dc_ref[n, h : h + 1, :] + sums[h : h + 1] - jnp.sum(nn[h], 0, keepdims=True) for h in range(per_key)
+        ]
+        dc = jnp.concatenate(dc + [jnp.zeros((8 - per_key, length), f32)], 0)
+        decays = mm(split(dc), (from_here,), 1, 0)
+        for h, m in enumerate(mine):
+            dv[n, h] = meta.beta[h] * es[m]
+            last = jnp.sum(ek[h] + later[m] * s_ref[n, h] * meta.keep[h], 0, keepdims=True)
+            rows[n, h] = decays[h : h + 1] + jnp.sum(last, 1, keepdims=True)
+            rows[n, per_key + h] = (
+                sums[2 * per_key + h : 2 * per_key + h + 1] + sums[per_key + h : per_key + h + 1] / meta.beta_row[h]
+            )
     for n in reversed(range(count)):
         dk_act = unit_back(dk[n], hats[n], inv[n])
         d_act = jnp.concatenate([dk_act] + [dv[n, h] for h in range(per_key)], 1)
         dz = d_act * (sig[n] + zs[n] * sig[n] * (1.0 - sig[n]))
         dx = conv_back(dz, taps[n], w, metas[n].code, metas[n].plain, dz_ref, doc_next, dw_ref, rim_ref)
-        dx_ref[n, :length, :] = dx.astype(bf16)
-        gates = three_rows(jnp.concatenate([rows[n, m] for m in range(2 * per_key)], 0))
-        gates = jnp.concatenate([gates, jnp.zeros((RIM - gates.shape[0], length), f32)], 0)
-        dx_ref[n, length:, :] = jnp.concatenate([gates, jnp.zeros((RIM, own - DK), f32)], 1).astype(bf16)
+        dx_ref[n] = dx.astype(bf16)
+        gates_ref[n] = jnp.concatenate([rows[n, m] for m in range(2 * per_key)], 0)
+
+    @pl.when(step == steps - 1)
+    def _():
+        small_ref[0:4, :DK], small_ref[0:4, DK:] = dwq_ref[...], dw_ref[...]
+        small_ref[4:7, :DK], small_ref[4:7, DK:] = rimq_ref[...], rim_ref[...]
+        small_ref[7:8, :] = jnp.zeros((1, small_ref.shape[1]), f32)
+
+
+def places(G, per_key):
+    starts = [lambda m: m * DK, lambda m: (G + m) * DK]
+    starts += [lambda m, h=h: (2 * G + m * per_key + h) * DK for h in range(per_key)]
+    return starts
+
+
+def tail_kernel(groups, next_ref, gates_ref, dx_ref, *refs):
+    refs, out_ref = refs[:-1], refs[-1]
+    taps = [ref[0:4, :] for ref in refs]
+    while len(taps) > 1:
+        taps = [i + j for i, j in zip(taps[::2], taps[1::2])]
+    rims = sum(next_ref[q] * refs[q][4:7, :] for q in range(groups))
+    parts = range(refs[0].shape[1] // DK)
+    shared = [taps[0][:, m * DK : (m + 1) * DK] for m in parts] + [rims[:, m * DK : (m + 1) * DK] for m in parts]
+    for m in range(out_ref.shape[0]):
+        x = jnp.concatenate([gates_ref[m]] + shared, 0)
+        hi = x.astype(bf16)
+        mid = (x - hi.astype(f32)).astype(bf16)
+        low = (x - hi.astype(f32) - mid.astype(f32)).astype(bf16)
+        out_ref[m] = jnp.concatenate([hi, mid, low], 1)
+
+
+def reads_kernel(G, width, o_ref, out_ref):
+    for m in range(G):
+        out_ref[:, m * width : (m + 1) * width] = o_ref[m, :, DK:]
+
+
+def unpack_kernel(G, per_key, last_ref, o_ref, dx_ref, rows_ref, dw_ref, decay_ref, beta_ref):
+    length = rows_ref.shape[0]
+    early = length - RIM
+    gates, taps = 2 * per_key, 4 * (2 + per_key)
+    for m in range(G):
+        x = dx_ref[m, length:, :].astype(f32)
+        x = x[:, :DK] + (x[:, DK : 2 * DK] + x[:, 2 * DK : 3 * DK])
+        decay_ref[m * per_key : (m + 1) * per_key, :] = x[:per_key]
+        beta_ref[m * per_key : (m + 1) * per_key, :] = x[per_key:gates]
+        for part, start in enumerate(places(G, per_key)):
+            to = slice(start(m), start(m) + DK)
+            ref, lane = (o_ref, 0) if part == 0 else (dx_ref, (part - 1) * DK)
+            rows_ref[:early, to] = ref[m, :early, lane : lane + DK]
+            rim = x[gates + taps + 3 * part : gates + taps + 3 * part + 3] * last_ref[0]
+            rim = jnp.concatenate([jnp.zeros((RIM - 3, DK), f32), rim], 0)
+            rows_ref[early:, to] = (ref[m, early:length, lane : lane + DK].astype(f32) + rim).astype(bf16)
+            dw_ref[:, to] = x[gates + 4 * part : gates + 4 * part + 4]
 
 
 def three(x):
@@ -434,18 +504,22 @@
     queries = jnp.concatenate([by_member(rows[:, : G * DK]), by_member(rim_rows[:, : G * DK])], 1)
     queries = jnp.pad(queries, ((0, 0), (0, RIM - 3), (0, 0)))
     asked = jnp.pad(by_member(og), ((0, 0), (0, RIM), (0, 0)))
-    later_part = jnp.concatenate([queries, asked], 2)
-    later_part, x = lax.optimization_barrier((later_part, x))
-    y = swap(later_part)
+    y = jnp.concatenate([queries, asked], 2)
+    y, x = lax.optimization_barrier((y, x))
+    y = swap(y)
     taps = conv_weight.astype(f32)
-    w_kv = lax.dynamic_index_in_dim(keys_values(taps), member, 0, keepdims=False)
-    w_q = lax.dynamic_index_in_dim(by_member(taps[:, : G * DK]), member, 0, keepdims=False)
+    w_q, w_k, w_v = [
+        lax.dynamic_index_in_dim(by_member(part), member, 0, keepdims=False)
+        for part in (taps[:, : G * DK], taps[:, G * DK : 2 * G * DK], taps[:, 2 * G * DK :])
+    ]
+    w_kv = jnp.concatenate([w_k, w_v], 1)
 
     pair = (per_key, DK, DK)
     block = (length, DK)
 
-    def call(kernel, count, name, back, fulls, ins, out_shapes, out_fulls, scratch, flops):
+    def call(kernel, count, name, back, fulls, ins, out_shapes, out_fulls, scratch, flops, behind=0):
         steps = G // count
+        out_fulls = [s if isinstance(s[0], tuple) else (s, f32) for s in out_fulls]
         order = (lambda s: steps - 1 - s) if back else (lambda s: s)
 
         def spec(shape):
@@ -459,9 +533,11 @@
             functools.partial(kernel, per_key, count),
             grid=(steps,),
             in_specs=in_specs,
-            out_specs=[spec(s) for s, _ in out_shapes] + [full(s) for s in out_fulls],
-            out_shape=[jax.ShapeDtypeStruct((G,) + s, t) for s, t in out_shapes]
-            + [jax.ShapeDtypeStruct(s, f32) for s in out_fulls],
+            out_specs=[spec(s) for s, _ in out_shapes] + [full(s) for s, _ in out_fulls],
+            out_shape=[
+                jax.ShapeDtypeStruct((G, s[0] + (0 if m else behind)) + s[1:], t) for m, (s, t) in enumerate(out_shapes)
+            ]
+            + [jax.ShapeDtypeStruct(s, t) for s, t in out_fulls],
             scratch_shapes=scratch(count),
             compiler_params=pltpu.CompilerParams(vmem_limit_bytes=VMEM),
             cost_estimate=pl.CostEstimate(flops=flops, bytes_accessed=8 << 20, transcendentals=0),
@@ -478,58 +554,71 @@
     def chain_scratch(width):
         return lambda count: [pltpu.VMEM((per_key, DK, 2 * DK), f32), pltpu.VMEM((count, 8 + length, width), f32)]
 
-    k, f, n, t, w_out, u, a, m_fwd, s_local, end = call(
-        key_kernel, COUNTS[0], "keys", False, (1,), (x, w_kv), [(block, f32)] + [(pair, f32)] * 8, [pair],
+    k, t, w_out, u, a, m_fwd, s_local, end = call(
+        key_kernel, COUNTS[0], "keys", False, (1,), (x, w_kv), [(block, f32)] + [(pair, f32)] * 6, [pair],
         chain_scratch(own), 15 * 10**9,
     )
     state_in = shifted(end, G)
-    p, y_read, pu, r, m_bwd, g_local, start = call(
-        query_kernel, COUNTS[1], "queries", True, (2,), (x, y, w_q, k, f, w_out, u, a), [(pair, f32)] * 6, [pair],
+    e, m_bwd, g_local, start = call(
+        query_kernel, COUNTS[1], "queries", True, (2,), (x, y, w_q, k, t, a), [(pair, f32)] * 3, [pair],
         chain_scratch(DK), 8 * 10**9,
     )
     back_in = shifted(start, -G)
     o, d, s, dk, dc, rim_q, dw_q = call(
-        read_kernel, COUNTS[2], "reads", True, (0, 3), (state_in, x, y, w_q, k, f, p, w_out, u, y_read, pu, m_fwd, s_local),
+        read_kernel, COUNTS[2], "reads", True, (0, 3), (state_in, x, y, w_q, k, w_out, u, m_fwd, s_local),
         [((length, own), bf16), (pair, f32), (pair, f32), (block, f32), ((per_key, length), f32)],
         [(3, DK), (4, DK)], conv_scratch(DK), 8 * 10**9,
     )
     o = swap(o)
-    dx, rim_kv, dw_kv = call(
-        write_kernel, COUNTS[3], "writes", True, (0, 2), (back_in, x, w_kv, k, f, n, t, r, m_bwd, g_local, d, s, dk, dc),
-        [((length + RIM, own), bf16)], [(3, own), (4, own)], conv_scratch(own), 15 * 10**9,
-    )
+    behind = 2 * per_key + 7 * (2 + per_key)
+    assert behind == 2 * RIM
+    dx, gates, small = call(
+        write_kernel, COUNTS[3], "writes", True, (0, 2, 12, 13),
+        (back_in, x, w_kv, k, t, e, m_bwd, g_local, d, s, dk, dc, dw_q, rim_q),
+        [((length, own), bf16), ((2 * per_key, length), f32)], [(8, DK + own)],
+        lambda count: conv_scratch(own)(count) + [pltpu.VMEM((4, own), f32), pltpu.VMEM((3, own), f32)],
+        15 * 10**9, behind,
+    )
+    me = lax.axis_index("seq")
+    terms, nexts = [], []
+    for p in range(n_dp):
+        for q in range(0, n_seq, G):
+            perm = [(i * n_seq + j, (i ^ p) * n_seq + (j ^ q)) for i in range(n_dp) for j in range(n_seq)]
+            terms.append(lax.ppermute(small, ("dp", "seq"), perm) if p or q else small)
+            if p == 0:
+                nexts.append((me ^ q) == me + G)
+    tail = pl.BlockSpec((G, behind, own), lambda s: (0, length // behind, 0))
+    dx = pl.pallas_call(
+        functools.partial(tail_kernel, n_seq // G),
+        grid=(1,),
+        in_specs=[pl.BlockSpec(memory_space=pltpu.SMEM), pl.BlockSpec(gates.shape, lambda s: (0, 0, 0)), tail]
+        + [pl.BlockSpec(small.shape, lambda s: (0, 0))] * len(terms),
+        out_specs=tail,
+        out_shape=jax.ShapeDtypeStruct(dx.shape, bf16),
+        input_output_aliases={2: 0},
+        name="tails",
+    )(jnp.stack(nexts).astype(f32), gates, dx, *terms)
+    dx, o = lax.optimization_barrier((dx, o))
     dx = swap(dx)
-
-    small = jnp.concatenate([jnp.concatenate([dw_q, dw_kv], 1), jnp.concatenate([rim_q, rim_kv], 1)], 0)
-    gathered = small[None]
-    step = 1
-    while step < G:
-        other = lax.ppermute(gathered, "seq", [(s, s ^ step) for s in range(n_seq)])
-        upper = (member & step) > 0
-        gathered = jnp.where(upper, jnp.concatenate([other, gathered], 0), jnp.concatenate([gathered, other], 0))
-        step *= 2
-    total = of_members(gathered[:, :, :DK]), of_members(gathered[:, :, DK : 2 * DK]), of_members(gathered[:, :, 2 * DK :])
-    total = jnp.concatenate(total, -1)
-    d_weight, rim_grad = total[:4], total[4:]
-    step = G
-    while step < n_seq:
-        d_weight = d_weight + lax.ppermute(d_weight, "seq", [(s, s ^ step) for s in range(n_seq)])
-        step *= 2
-    step = 1
-    while step < n_dp:
-        d_weight = d_weight + lax.ppermute(d_weight, "dp", [(s, s ^ step) for s in range(n_dp)])
-        step *= 2
-    incoming = lax.ppermute(rim_grad.astype(bf16), "seq", [(s, s - 1) for s in range(G, n_seq, G)])
-
-    output = of_members(o[:, :, DK:])
-    d_rows = jnp.concatenate(
-        [of_members(o[:, :, :DK]), of_members(dx[:, :length, :DK]), of_members(dx[:, :length, DK:])], -1
-    )
-    d_tail = (d_rows[-3:].astype(f32) + incoming.astype(f32)).astype(bf16)
-    d_rows = jnp.concatenate([d_rows[:-3], d_tail], 0)
-    gates = dx[:, length : length + 6 * per_key, :DK].astype(f32).reshape(G, 3, 2, per_key, length)
-    gates = gates[:, 0] + (gates[:, 1] + gates[:, 2])
-    d_decay, d_beta = gates[:, 0].reshape(heads, length), gates[:, 1].reshape(heads, length)
+    output = pl.pallas_call(
+        functools.partial(reads_kernel, G, per_key * DK),
+        out_shape=jax.ShapeDtypeStruct((length, heads * DK), bf16),
+        cost_estimate=pl.CostEstimate(flops=0, bytes_accessed=3 << 20, transcendentals=0),
+        name="outputs",
+    )(o)
+    dx, output = lax.optimization_barrier((dx, output))
+    d_rows, d_weight, d_decay, d_beta = pl.pallas_call(
+        functools.partial(unpack_kernel, G, per_key),
+        in_specs=[pl.BlockSpec(memory_space=pltpu.SMEM)] + [pl.BlockSpec(memory_space=pltpu.VMEM)] * 2,
+        out_shape=[
+            jax.ShapeDtypeStruct((length, channels), bf16),
+            jax.ShapeDtypeStruct((4, channels), f32),
+            jax.ShapeDtypeStruct((heads, length), f32),
+            jax.ShapeDtypeStruct((heads, length), f32),
+        ],
+        compiler_params=pltpu.CompilerParams(vmem_limit_bytes=VMEM),
+        name="unpack",
+    )((member == G - 1).astype(f32)[None], o, dx)
     return (output[None], d_rows[None], d_weight, d_decay[None], d_beta[None])
 
 

time: 140 us -> 126 us (0.900)
  the two profiles are of different devices: /device:TPU:8 before, /device:TPU:0 now
where the time goes in v3:
time: 126 us; the launch traced here: 125 us
  Pallas kernels  51.9 us (41%)
  starting transfers between devices  31.4 us (25%)
  waiting for transfers between devices  26.8 us (21%)
  local copies, waits for them, and re-layouts  8.63 us (7%)
  other arithmetic  4.88 us (4%)
  between operations  1.71 us (1%)
    pallas_call x4, Pallas kernels, call(): pl.pallas_call(functools.partial(kernel, per_key, count), grid=(steps,),...  45.7 us
    all_to_all x4, waiting for transfers between devices, swap(): return lax.all_to_all(x, 'seq', 0, 0, axis_index_groups=team)  22.6 us
    all_to_all x4, starting transfers between devices, swap(): return lax.all_to_all(x, 'seq', 0, 0, axis_index_groups=team)  18.1 us
    ppermute x3, starting transfers between devices, shifted(): lax.ppermute(x, 'seq', [(s, s + by) for s in range(n_seq) if 0 <= s + by...  8.16 us
    unnamed x30, local copies, waits for them, and re-layouts  6.23 us
    ppermute x3, starting transfers between devices, local(): terms.append(lax.ppermute(small, ('dp', 'seq'), perm) if p or q else small)  5.17 us
    ppermute x3, waiting for transfers between devices, local(): terms.append(lax.ppermute(small, ('dp', 'seq'), perm) if p or q else small)  4.16 us
    pallas_call x1, Pallas kernels, local(): pl.pallas_call(functools.partial(unpack_kernel, G, per_key), in_specs=[pl...  2.62 us
  transfers between devices with their start and end apart: 10, of which 5 were waited for; matrix products, arithmetic and copies ran while one was open for 5% of the time, Pallas kernels for 39%

profile of v3, /device:TPU:0, one launch (start us, length us, event | category | flops | bytes accessed | tf_op | source)
XLA Modules:
  0.0 125.3 jit_solution(7006103865395505468)
XLA Ops:
  0.6 0.7 convert_bitcast_fusion.1
  1.4 0.9 slice_bitcast_fusion
  2.3 0.0 copy-start.9
  2.3 0.0 copy-start.10
  2.3 2.4 %collective-permute-start = (bf16[4,4096]{1,0:T(4,128)(2,1)S(1)}, bf16[4,4096]{1,0:T(4,128)(2,1)S(1)}, u32[]{:S(2)}, u32[]{:S(2)}) collective-permute-start(bf16[4,4096]{1,0:T(4,128)(2,1)S(1)} %pad_maximum_fusion.1), channel_id=1, source_target_pairs={{0,1},{1,2},{2,3},{3,4},{4,5},{5,6},{6,7},{7,8},{8,9},{9,10},{10,1... | collective-permute-start | bytes 98312 | tf_op jit(solution)/shard_map/ppermute | solution.py:475
  4.7 1.6 %copy.43 = bf16[1,128,4096]{1,2,0:T(8,128)(2,1)S(1)} copy(bf16[1,128,4096]{2,1,0:T(8,128)(2,1)} %param.6) | data formatting | bytes 2097152 | tf_op args[0]
  6.4 0.0 copy-start.13
  6.5 0.5 copy-done.13
  7.1 0.2 copy.47
  7.3 0.2 copy.48
  7.5 0.0 collective-permute-done
  7.5 0.6 convert_reduce_fusion
  8.1 0.1 slice_select_fusion
  9.0 1.0 pad_maximum_fusion
  10.0 6.2 %all-to-all-start = ((bf16[8,144,384]{2,1,0:T(8,128)(2,1)}), bf16[8,144,384]{2,1,0:T(8,128)(2,1)S(1)}, u32[]{:S(2)}, u32[]{:S(2)}) async-start(bf16[8,144,384]{2,1,0:T(8,128)(2,1)} %pad_maximum_fusion), calls=%async_computation | async-start | bytes 1769472 | tf_op jit(solution)/shard_map/all_to_all | solution.py:487
  16.3 0.3 copy.45
  16.5 0.2 copy.46
  16.8 0.2 copy.44
  17.0 1.1 fusion.1
  18.1 10.8 %all-to-all-done.x_ref = bf16[8,144,384]{2,1,0:T(8,128)(2,1)S(1)} async-done(((bf16[8,144,384]{2,1,0:T(8,128)(2,1)}), bf16[8,144,384]{2,1,0:T(8,128)(2,1)S(1)}, u32[]{:S(2)}, u32[]{:S(2)}) %all-to-all-start) | async-done | bytes 884768 | tf_op jit(solution)/shard_map/all_to_all | solution.py:487
  28.9 3.6 %all-to-all-start.1 = ((bf16[8,144,384]{2,1,0:T(8,128)(2,1)}), bf16[8,144,384]{2,1,0:T(8,128)(2,1)S(1)}, u32[]{:S(2)}, u32[]{:S(2)}) async-start(bf16[8,144,384]{2,1,0:T(8,128)(2,1)} %fusion.1), calls=%async_computation.1 | async-start | bytes 1769472 | tf_op jit(solution)/shard_map/all_to_all | solution.py:487
  32.5 0.6 dynamic-slice_bitcast_fusion.2.w_ref
  33.1 0.6 pad_maximum_fusion.4.w_ref
  33.7 13.7 %keys.1 = (f32[8,128,128]{2,1,0:T(8,128)}, f32[8,2,128,128]{3,2,1,0:T(8,128)}, f32[8,2,128,128]{3,2,1,0:T(8,128)}, f32[8,2,128,128]{3,2,1,0:T(8,128)}, f32[8,2,1...) custom-call(bf16[8,144,384]{2,1,0:T(8,128)(2,1)} %copy-done.2, ...), custom_call_target="tpu_custom_call" | custom-call | flops 15000000512 | bytes 8388608 | tf_op jit(solution)/shard_map/keys/pallas_call | solution.py:532
  47.4 4.3 %collective-permute-start.2 = (f32[2,128,128]{2,1,0:T(8,128)}, f32[2,128,128]{2,1,0:T(8,128)S(1)}, u32[]{:S(2)}, u32[]{:S(2)}) collective-permute-start(f32[2,128,128]{2,1,0:T(8,128)} %get-tuple-element.46), channel_id=1, source_target_pairs={{0,8},{1,9},{2,10},{3,11},{4,12},{5,13},{6,14},{7,15},{16,24},{17,... | collective-permute-start | bytes 393224 | tf_op jit(solution)/shard_map/ppermute | solution.py:475
  51.7 0.0 all-to-all-done.1.y_ref
  51.7 0.9 copy-done.3
  52.7 8.3 %queries.1 = (f32[8,2,128,128]{3,2,1,0:T(8,128)}, f32[8,2,128,128]{3,2,1,0:T(8,128)}, f32[8,2,128,128]{3,2,1,0:T(8,128)}, f32[2,128,128]{2,1,0:T(8,128)}) custom-call(bf16[8,144,384]{2,1,0:T(8,128)(2,1)} %copy-done.2, bf16[8,144,384]{2,1,0:T(8,128)(2,1)} %copy-done.3, f32[4,128]{1,0:T(4,128)} %dynamic-slice_bitcast_fusion.2.w_ref, ...), custom_call_target="tpu_custom_call" | custom-call | flops 8000000000 | bytes 8388608 | tf_op jit(solution)/shard_map/queries/pallas_call | solution.py:532
  60.9 1.5 %collective-permute-start.1 = (f32[2,128,128]{2,1,0:T(8,128)}, f32[2,128,128]{2,1,0:T(8,128)S(1)}, u32[]{:S(2)}, u32[]{:S(2)}) collective-permute-start(f32[2,128,128]{2,1,0:T(8,128)} %get-tuple-element.42), channel_id=1, source_target_pairs={{8,0},{9,1},{10,2},{11,3},{12,4},{13,5},{14,6},{15,7},{24,16},{25,... | collective-permute-start | bytes 393224 | tf_op jit(solution)/shard_map/ppermute | solution.py:475
  62.4 0.6 copy-done.12
  63.1 10.0 %reads.1 = (bf16[8,128,384]{2,1,0:T(8,128)(2,1)}, f32[8,2,128,128]{3,2,1,0:T(8,128)}, f32[8,2,128,128]{3,2,1,0:T(8,128)}, f32[8,128,128]{2,1,0:T(8,128)}, f32[8,...) custom-call(f32[2,128,128]{2,1,0:T(8,128)} %copy-done.12, bf16[8,144,384]{2,1,0:T(8,128)(2,1)} %copy-done.2, ...), custom_call_target="tpu_custom_call" | custom-call | flops 8000000000 | bytes 8388608 | tf_op jit(solution)/shard_map/reads/pallas_call | solution.py:532
  73.1 4.1 %all-to-all-start.2 = ((bf16[8,128,384]{2,1,0:T(8,128)(2,1)}), bf16[8,128,384]{2,1,0:T(8,128)(2,1)S(1)}, u32[]{:S(2)}, u32[]{:S(2)}) async-start(bf16[8,128,384]{2,1,0:T(8,128)(2,1)} %get-tuple-element.60), calls=%async_computation.2 | async-start | bytes 1572864 | tf_op jit(solution)/shard_map/all_to_all | solution.py:487
  77.2 0.6 copy-done.11
  77.9 13.7 %writes.1 = (bf16[8,160,384]{2,1,0:T(8,128)(2,1)}, f32[8,4,128]{2,1,0:T(4,128)}, f32[8,512]{1,0:T(8,128)}) custom-call(f32[2,128,128]{2,1,0:T(8,128)} %copy-done.11, bf16[8,144,384]{2,1,0:T(8,128)(2,1)} %copy-done.2, f32[4,384]{1,0:T(4,128)} %pad_maximum_fusion.4.w_ref, f32[8,128,128]{2,1,0:T(8,128)} %get-tuple-element.39.k_ref, ...), custom_call_target="tpu_custom_call" | custom-call | flops 15000000512 | bytes 8388608 | tf_op jit(solution)/shard_map/writes/pallas_call | solution.py:532
  91.6 4.5 %collective-permute-start.5 = (f32[8,512]{1,0:T(8,128)}, f32[8,512]{1,0:T(8,128)S(1)}, u32[]{:S(2)}, u32[]{:S(2)}) collective-permute-start(f32[8,512]{1,0:T(8,128)} %get-tuple-element.59.refs_0_), channel_id=1, source_target_pairs={{0,24},{1,25},{2,26},{3,27},{4,28},{5,29},{6,30},{7,31},{8,16},{9,... | collective-permute-start | bytes 49160 | tf_op jit(solution)/shard_map/ppermute | solution.py:587
  96.1 0.5 collective-permute-start.4
  96.6 0.1 collective-permute-start.3
  96.7 0.6 add_convert_fusion.next_ref
  97.3 0.7 collective-permute-done.5.refs_3_
  98.0 2.0 %collective-permute-done.4.refs_2_ = f32[8,512]{1,0:T(8,128)S(1)} collective-permute-done((f32[8,512]{1,0:T(8,128)}, f32[8,512]{1,0:T(8,128)S(1)}, u32[]{:S(2)}, u32[]{:S(2)}) %collective-permute-start.4) | collective-permute-done | bytes 16416 | tf_op jit(solution)/shard_map/ppermute | solution.py:587
  100.1 1.4 %collective-permute-done.3.refs_1_ = f32[8,512]{1,0:T(8,128)S(1)} collective-permute-done((f32[8,512]{1,0:T(8,128)}, f32[8,512]{1,0:T(8,128)S(1)}, u32[]{:S(2)}, u32[]{:S(2)}) %collective-permute-start.3) | collective-permute-done | bytes 16416 | tf_op jit(solution)/shard_map/ppermute | solution.py:587
  101.5 0.6 copy-done.8
  102.1 1.7 %tails.1 = bf16[8,160,384]{2,1,0:T(8,128)(2,1)} custom-call(f32[2]{0:T(128)} %add_convert_fusion.next_ref, f32[8,4,128]{2,1,0:T(4,128)} %get-tuple-element.57.gates_ref, bf16[8,160,384]{2,1,0:T(8,128)(2,1)} %get-tuple-element.58.dx_ref, f32[8,512]{1,0:T(8,128)} %get-tuple-element.59.refs_0_, f32[8,512]{1,0:T(8,128)} %copy-done.8, ...), custom_call_target="tpu_custom_call", output_to_operand_aliasing={{}: (2, {})} | custom-call | tf_op jit(solution)/shard_map/tails/pallas_call | solution.py:591
  103.8 4.2 %all-to-all-start.3 = ((bf16[8,160,384]{2,1,0:T(8,128)(2,1)}), bf16[8,160,384]{2,1,0:T(8,128)(2,1)S(1)}, u32[]{:S(2)}, u32[]{:S(2)}) async-start(bf16[8,160,384]{2,1,0:T(8,128)(2,1)} %tails.1), calls=%async_computation.3 | async-start | bytes 1966080 | tf_op jit(solution)/shard_map/all_to_all | solution.py:487
  108.0 2.0 %outputs.1 = bf16[128,2048]{1,0:T(8,128)(2,1)} custom-call(bf16[8,128,384]{2,1,0:T(8,128)(2,1)} %copy-done), custom_call_target="tpu_custom_call" | custom-call | bytes 3145728 | tf_op jit(solution)/shard_map/outputs/pallas_call | solution.py:603
  110.0 11.8 %all-to-all-done.3.dx_ref = bf16[8,160,384]{2,1,0:T(8,128)(2,1)S(1)} async-done(((bf16[8,160,384]{2,1,0:T(8,128)(2,1)}), bf16[8,160,384]{2,1,0:T(8,128)(2,1)S(1)}, u32[]{:S(2)}, u32[]{:S(2)}) %all-to-all-start.3) | async-done | bytes 983072 | tf_op jit(solution)/shard_map/all_to_all | solution.py:487
  121.7 1.0 copy-done.1
  122.7 2.6 %unpack.1 = (bf16[128,4096]{1,0:T(8,128)(2,1)}, f32[4,4096]{1,0:T(4,128)}, f32[16,128]{1,0:T(8,128)}, f32[16,128]{1,0:T(8,128)}) custom-call(f32[1]{0:T(128)} %bitcast.33.last_ref, bf16[8,128,384]{2,1,0:T(8,128)(2,1)} %copy-done, bf16[8,160,384]{2,1,0:T(8,128)(2,1)} %copy-done.1), custom_call_target="tpu_custom_call" | custom-call | tf_op jit(solution)/shard_map/unpack/pallas_call | solution.py:610
  (44 shorter events, 0.3 us)
Async XLA Ops:
  2.3 4.0 %copy-start.9 = (f32[1,16,128]{2,1,0:T(8,128)S(1)}, f32[1,16,128]{2,1,0:T(8,128)}, u32[]{:S(2)}) copy-start(f32[1,16,128]{2,1,0:T(8,128)} %param.8) | copy-start | bytes 24580
  2.3 4.0 %copy-start.10 = (f32[1,16,128]{2,1,0:T(8,128)S(1)}, f32[1,16,128]{2,1,0:T(8,128)}, u32[]{:S(2)}) copy-start(f32[1,16,128]{2,1,0:T(8,128)} %param.9) | copy-start | bytes 24580
  2.3 5.2 %collective-permute-start = (bf16[4,4096]{1,0:T(4,128)(2,1)S(1)}, bf16[4,4096]{1,0:T(4,128)(2,1)S(1)}, u32[]{:S(2)}, u32[]{:S(2)}) collective-permute-start(bf16[4,4096]{1,0:T(4,128)(2,1)S(1)} %pad_maximum_fusion.1), channel_id=1, source_target_pairs={{0,1},{1,2},{2,3},{3,4},{4,5},{5,6},{6,7},{7,8},{8,9},{9,10},{10,1... | collective-permute-start | bytes 98312 | tf_op jit(solution)/shard_map/ppermute | solution.py:475
  6.4 0.7 copy-start.13
  10.0 6.2 %copy-start.5 = (bf16[4,4096]{1,0:T(4,128)(2,1)S(1)}, bf16[4,4096]{1,0:T(4,128)(2,1)}, u32[]{:S(2)}) copy-start(bf16[4,4096]{1,0:T(4,128)(2,1)} %param.7) | copy-start | bytes 98308
  10.0 6.2 %copy-start.4 = (bf16[1,128,2048]{2,1,0:T(8,128)(2,1)S(1)}, bf16[1,128,2048]{2,1,0:T(8,128)(2,1)}, u32[]{:S(2)}) copy-start(bf16[1,128,2048]{2,1,0:T(8,128)(2,1)} %param.11) | copy-start | bytes 1572868
  10.0 18.9 %all-to-all-start = ((bf16[8,144,384]{2,1,0:T(8,128)(2,1)}), bf16[8,144,384]{2,1,0:T(8,128)(2,1)S(1)}, u32[]{:S(2)}, u32[]{:S(2)}) async-start(bf16[8,144,384]{2,1,0:T(8,128)(2,1)} %pad_maximum_fusion), calls=%async_computation | async-start | bytes 1769472 | tf_op jit(solution)/shard_map/all_to_all | solution.py:487
  28.9 4.7 %copy-start.2 = (bf16[8,144,384]{2,1,0:T(8,128)(2,1)}, bf16[8,144,384]{2,1,0:T(8,128)(2,1)S(1)}, u32[]{:S(2)}) copy-start(bf16[8,144,384]{2,1,0:T(8,128)(2,1)S(1)} %all-to-all-done.x_ref) | copy-start | bytes 2654212
  28.9 22.8 %all-to-all-start.1 = ((bf16[8,144,384]{2,1,0:T(8,128)(2,1)}), bf16[8,144,384]{2,1,0:T(8,128)(2,1)S(1)}, u32[]{:S(2)}, u32[]{:S(2)}) async-start(bf16[8,144,384]{2,1,0:T(8,128)(2,1)} %fusion.1), calls=%async_computation.1 | async-start | bytes 1769472 | tf_op jit(solution)/shard_map/all_to_all | solution.py:487
  47.4 15.0 %collective-permute-start.2 = (f32[2,128,128]{2,1,0:T(8,128)}, f32[2,128,128]{2,1,0:T(8,128)S(1)}, u32[]{:S(2)}, u32[]{:S(2)}) collective-permute-start(f32[2,128,128]{2,1,0:T(8,128)} %get-tuple-element.46), channel_id=1, source_target_pairs={{0,8},{1,9},{2,10},{3,11},{4,12},{5,13},{6,14},{7,15},{16,24},{17,... | collective-permute-start | bytes 393224 | tf_op jit(solution)/shard_map/ppermute | solution.py:475
  51.7 0.9 copy-start.3
  60.9 16.3 %collective-permute-start.1 = (f32[2,128,128]{2,1,0:T(8,128)}, f32[2,128,128]{2,1,0:T(8,128)S(1)}, u32[]{:S(2)}, u32[]{:S(2)}) collective-permute-start(f32[2,128,128]{2,1,0:T(8,128)} %get-tuple-element.42), channel_id=1, source_target_pairs={{8,0},{9,1},{10,2},{11,3},{12,4},{13,5},{14,6},{15,7},{24,16},{25,... | collective-permute-start | bytes 393224 | tf_op jit(solution)/shard_map/ppermute | solution.py:475
  62.4 0.7 copy-start.12
  73.1 30.7 %all-to-all-start.2 = ((bf16[8,128,384]{2,1,0:T(8,128)(2,1)}), bf16[8,128,384]{2,1,0:T(8,128)(2,1)S(1)}, u32[]{:S(2)}, u32[]{:S(2)}) async-start(bf16[8,128,384]{2,1,0:T(8,128)(2,1)} %get-tuple-element.60), calls=%async_computation.2 | async-start | bytes 1572864 | tf_op jit(solution)/shard_map/all_to_all | solution.py:487
  77.2 0.7 copy-start.11
  91.6 6.5 %collective-permute-start.5 = (f32[8,512]{1,0:T(8,128)}, f32[8,512]{1,0:T(8,128)S(1)}, u32[]{:S(2)}, u32[]{:S(2)}) collective-permute-start(f32[8,512]{1,0:T(8,128)} %get-tuple-element.59.refs_0_), channel_id=1, source_target_pairs={{0,24},{1,25},{2,26},{3,27},{4,28},{5,29},{6,30},{7,31},{8,16},{9,... | collective-permute-start | bytes 49160 | tf_op jit(solution)/shard_map/ppermute | solution.py:587
  96.1 3.9 %collective-permute-start.4 = (f32[8,512]{1,0:T(8,128)}, f32[8,512]{1,0:T(8,128)S(1)}, u32[]{:S(2)}, u32[]{:S(2)}) collective-permute-start(f32[8,512]{1,0:T(8,128)} %get-tuple-element.59.refs_0_), channel_id=1, source_target_pairs={{0,16},{1,17},{2,18},{3,19},{4,20},{5,21},{6,22},{7,23},{8,24},{9,... | collective-permute-start | bytes 49160 | tf_op jit(solution)/shard_map/ppermute | solution.py:587
  96.6 4.9 %collective-permute-start.3 = (f32[8,512]{1,0:T(8,128)}, f32[8,512]{1,0:T(8,128)S(1)}, u32[]{:S(2)}, u32[]{:S(2)}) collective-permute-start(f32[8,512]{1,0:T(8,128)} %get-tuple-element.59.refs_0_), channel_id=1, source_target_pairs={{0,8},{1,9},{2,10},{3,11},{4,12},{5,13},{6,14},{7,15},{8,0},{9,1},... | collective-permute-start | bytes 49160 | tf_op jit(solution)/shard_map/ppermute | solution.py:587
  98.0 3.5 %copy-start.6 = (f32[8,512]{1,0:T(8,128)}, f32[8,512]{1,0:T(8,128)S(1)}, u32[]{:S(2)}) copy-start(f32[8,512]{1,0:T(8,128)S(1)} %collective-permute-done.5.refs_3_) | copy-start | bytes 49156
  100.1 1.5 %copy-start.7 = (f32[8,512]{1,0:T(8,128)}, f32[8,512]{1,0:T(8,128)S(1)}, u32[]{:S(2)}) copy-start(f32[8,512]{1,0:T(8,128)S(1)} %collective-permute-done.4.refs_2_) | copy-start | bytes 49156
  101.5 0.6 copy-start.8
  103.8 4.2 %copy-start = (bf16[8,128,384]{2,1,0:T(8,128)(2,1)}, bf16[8,128,384]{2,1,0:T(8,128)(2,1)S(1)}, u32[]{:S(2)}) copy-start(bf16[8,128,384]{2,1,0:T(8,128)(2,1)S(1)} %all-to-all-done.2.o_ref) | copy-start | bytes 2359300
  103.8 18.0 %all-to-all-start.3 = ((bf16[8,160,384]{2,1,0:T(8,128)(2,1)}), bf16[8,160,384]{2,1,0:T(8,128)(2,1)S(1)}, u32[]{:S(2)}, u32[]{:S(2)}) async-start(bf16[8,160,384]{2,1,0:T(8,128)(2,1)} %tails.1), calls=%async_computation.3 | async-start | bytes 1966080 | tf_op jit(solution)/shard_map/all_to_all | solution.py:487
  121.7 1.0 copy-start.1

commit v4 on v3

--- a/solution.py
+++ b/solution.py
@@ -11,8 +11,8 @@
 DOC_MOST = 1024
 EPS = 1e-6
 CODE = 16
-COUNTS = (4, 4, 2, 4)
-VMEM = 56 << 20
+COUNTS = (4, 4, 4, 4)
+VMEM = 64 << 20
 RIM = 16
 f32 = jnp.float32
 bf16 = jnp.bfloat16
@@ -44,10 +44,12 @@
     return lax.broadcasted_iota(jnp.int32, shape, dim)
 
 
-def conv_inputs(x_ref, n, width, shift_ref, docs, lane=0):
-    length = docs.shape[0]
+def conv_inputs(x_ref, n, width, shift_ref, docs, rim=None):
+    length, lane = docs.shape[0], 0
     to = slice(0, width)
-    shift_ref[5:8, to] = x_ref[n, length : length + 3, lane : lane + width].astype(f32)
+    if rim is None:
+        rim = x_ref[n, length : length + RIM, :width].astype(f32)[:3]
+    shift_ref[5:8, to] = rim
     rows = x_ref[n, :length, lane : lane + width].astype(f32)
     shift_ref[8 : 8 + length, to] = rows
     at = iota2((length, DK), 0)
@@ -59,6 +61,10 @@
         moved = shift_ref[8 - off : 8 - off + length, to]
         taps.append(jnp.where(wide(ok, width), moved, 0.0))
     return taps
+
+
+def query_rim(x_ref, n, length):
+    return x_ref[n, length : length + RIM, DK : 2 * DK].astype(f32)[3:6]
 
 
 def wide(x, width):
@@ -241,7 +247,7 @@
     metas, sq, sk, qk = {}, {}, {}, {}
     for n in range(count):
         metas[n] = Meta(x_ref[n, length:, :DK], per_key)
-        z = conv_out(conv_inputs(y_ref, n, DK, shift_ref.at[n], metas[n].code), w)
+        z = conv_out(conv_inputs(y_ref, n, DK, shift_ref.at[n], metas[n].code, query_rim(x_ref, n, length)), w)
         q, _ = unit(z * sigmoid(z))
         sq[n], sk[n] = split(q * DK**-0.5), split(k_ref[n])
         qk[n] = mm(sq[n], sk[n], 1, 1)
@@ -281,7 +287,7 @@
     metas, taps, sig, zs, hats, inv, qs, sq, sk, qk = {}, {}, {}, {}, {}, {}, {}, {}, {}, {}
     for n in range(count):
         metas[n] = Meta(x_ref[n, length:, :DK], per_key)
-        taps[n] = conv_inputs(y_ref, n, DK, shift_ref.at[n], metas[n].code)
+        taps[n] = conv_inputs(y_ref, n, DK, shift_ref.at[n], metas[n].code, query_rim(x_ref, n, length))
         zs[n] = conv_out(taps[n], w)
         sig[n] = sigmoid(zs[n])
         hats[n], inv[n] = unit(zs[n] * sig[n])
@@ -412,7 +418,7 @@
     return starts
 
 
-def tail_kernel(groups, next_ref, gates_ref, dx_ref, *refs):
+def tail_kernel(groups, next_ref, gates_ref, *refs):
     refs, out_ref = refs[:-1], refs[-1]
     taps = [ref[0:4, :] for ref in refs]
     while len(taps) > 1:
@@ -433,22 +439,25 @@
         out_ref[:, m * width : (m + 1) * width] = o_ref[m, :, DK:]
 
 
-def unpack_kernel(G, per_key, last_ref, o_ref, dx_ref, rows_ref, dw_ref, decay_ref, beta_ref):
-    length = rows_ref.shape[0]
-    early = length - RIM
+def unpack_kernel(G, per_key, o_ref, dx_ref, rows_ref):
+    for m in range(G):
+        for part, start in enumerate(places(G, per_key)):
+            ref, lane = (o_ref, 0) if part == 0 else (dx_ref, (part - 1) * DK)
+            rows_ref[:, start(m) : start(m) + DK] = ref[m, :, lane : lane + DK]
+
+
+def final_kernel(G, per_key, last_ref, tail_ref, rows_in, rows_ref, dw_ref, decay_ref, beta_ref):
     gates, taps = 2 * per_key, 4 * (2 + per_key)
     for m in range(G):
-        x = dx_ref[m, length:, :].astype(f32)
+        x = tail_ref[m].astype(f32)
         x = x[:, :DK] + (x[:, DK : 2 * DK] + x[:, 2 * DK : 3 * DK])
         decay_ref[m * per_key : (m + 1) * per_key, :] = x[:per_key]
         beta_ref[m * per_key : (m + 1) * per_key, :] = x[per_key:gates]
         for part, start in enumerate(places(G, per_key)):
             to = slice(start(m), start(m) + DK)
-            ref, lane = (o_ref, 0) if part == 0 else (dx_ref, (part - 1) * DK)
-            rows_ref[:early, to] = ref[m, :early, lane : lane + DK]
             rim = x[gates + taps + 3 * part : gates + taps + 3 * part + 3] * last_ref[0]
             rim = jnp.concatenate([jnp.zeros((RIM - 3, DK), f32), rim], 0)
-            rows_ref[early:, to] = (ref[m, early:length, lane : lane + DK].astype(f32) + rim).astype(bf16)
+            rows_ref[:, to] = (rows_in[:, to].astype(f32) + rim).astype(bf16)
             dw_ref[:, to] = x[gates + 4 * part : gates + 4 * part + 4]
 
 
@@ -486,11 +495,14 @@
     def swap(x):
         return lax.all_to_all(x, "seq", 0, 0, axis_index_groups=team)
 
-    doc_row = jnp.pad((docs[-3:] + 1).astype(bf16), (0, channels - 3))
-    rim = shifted(jnp.concatenate([rows[-3:], doc_row[None]], 0), 1)
-    held = rim[3, :3] == (docs[0] + 1).astype(bf16)
-    rim_rows = jnp.where(held[:, None], rim[:3], 0)
-    code = (docs + 1 + CODE * jnp.sum(held.astype(jnp.int32))).astype(bf16)
+    marks = jnp.broadcast_to((docs[-3:] + 1).astype(bf16)[:, None], (3, DK)).reshape(-1)
+    marks = jnp.pad(marks, (0, channels - 3 * DK))
+    first = jnp.broadcast_to((docs[:1] + 1).astype(bf16), (DK,))
+    rim = shifted(jnp.concatenate([rows[-3:], marks[None]], 0), 1)
+    held = rim[3, : 3 * DK].reshape(3, DK) == first
+    rim_rows = jnp.where(held[:, None], rim[:3].reshape(3, -1, DK), 0).reshape(3, channels)
+    code = (docs + 1).reshape(-1, DK) + CODE * (held[0].astype(jnp.int32) + held[1] + held[2])
+    code = code.reshape(length).astype(bf16)
     numbers = jnp.concatenate(
         [
             jnp.broadcast_to(code, (G, 1, length)),
@@ -499,20 +511,24 @@
         ],
         1,
     )
-    numbers = jnp.pad(numbers, ((0, 0), (0, 0), (0, own - DK)))
-    x = swap(jnp.concatenate([keys_values(rows), keys_values(rim_rows), numbers], 1))
-    queries = jnp.concatenate([by_member(rows[:, : G * DK]), by_member(rim_rows[:, : G * DK])], 1)
-    queries = jnp.pad(queries, ((0, 0), (0, RIM - 3), (0, 0)))
-    asked = jnp.pad(by_member(og), ((0, 0), (0, RIM), (0, 0)))
-    y = jnp.concatenate([queries, asked], 2)
-    y, x = lax.optimization_barrier((y, x))
-    y = swap(y)
+    rim_q = jnp.pad(by_member(rim_rows[:, : G * DK]), ((0, 0), (0, RIM - 6), (0, own - 2 * DK)))
+    x = swap(
+        jnp.concatenate(
+            [keys_values(rows), keys_values(rim_rows), jnp.concatenate([numbers, rim_q], 2)], 1
+        )
+    )
+    y = jnp.concatenate([by_member(rows[:, : G * DK]), by_member(og)], 2)
     taps = conv_weight.astype(f32)
     w_q, w_k, w_v = [
         lax.dynamic_index_in_dim(by_member(part), member, 0, keepdims=False)
         for part in (taps[:, : G * DK], taps[:, G * DK : 2 * G * DK], taps[:, 2 * G * DK :])
     ]
     w_kv = jnp.concatenate([w_k, w_v], 1)
+    me = lax.axis_index("seq")
+    nexts = jnp.stack([(me ^ q) == me + G for q in range(0, n_seq, G)]).astype(f32)
+    last = (member == G - 1).astype(f32)[None]
+    y, x, w_q, w_kv, nexts, last = lax.optimization_barrier((y, x, w_q, w_kv, nexts, last))
+    y = swap(y)
 
     pair = (per_key, DK, DK)
     block = (length, DK)
@@ -577,27 +593,19 @@
         (back_in, x, w_kv, k, t, e, m_bwd, g_local, d, s, dk, dc, dw_q, rim_q),
         [((length, own), bf16), ((2 * per_key, length), f32)], [(8, DK + own)],
         lambda count: conv_scratch(own)(count) + [pltpu.VMEM((4, own), f32), pltpu.VMEM((3, own), f32)],
-        15 * 10**9, behind,
-    )
-    me = lax.axis_index("seq")
-    terms, nexts = [], []
+        15 * 10**9,
+    )
+    terms = []
     for p in range(n_dp):
         for q in range(0, n_seq, G):
             perm = [(i * n_seq + j, (i ^ p) * n_seq + (j ^ q)) for i in range(n_dp) for j in range(n_seq)]
             terms.append(lax.ppermute(small, ("dp", "seq"), perm) if p or q else small)
-            if p == 0:
-                nexts.append((me ^ q) == me + G)
-    tail = pl.BlockSpec((G, behind, own), lambda s: (0, length // behind, 0))
-    dx = pl.pallas_call(
+    tails = pl.pallas_call(
         functools.partial(tail_kernel, n_seq // G),
-        grid=(1,),
-        in_specs=[pl.BlockSpec(memory_space=pltpu.SMEM), pl.BlockSpec(gates.shape, lambda s: (0, 0, 0)), tail]
-        + [pl.BlockSpec(small.shape, lambda s: (0, 0))] * len(terms),
-        out_specs=tail,
-        out_shape=jax.ShapeDtypeStruct(dx.shape, bf16),
-        input_output_aliases={2: 0},
+        in_specs=[pl.BlockSpec(memory_space=pltpu.SMEM)] + [pl.BlockSpec(memory_space=pltpu.VMEM)] * (1 + len(terms)),
+        out_shape=jax.ShapeDtypeStruct((G, behind, own), bf16),
         name="tails",
-    )(jnp.stack(nexts).astype(f32), gates, dx, *terms)
+    )(nexts, gates, *terms)
     dx, o = lax.optimization_barrier((dx, o))
     dx = swap(dx)
     output = pl.pallas_call(
@@ -606,19 +614,35 @@
         cost_estimate=pl.CostEstimate(flops=0, bytes_accessed=3 << 20, transcendentals=0),
         name="outputs",
     )(o)
-    dx, output = lax.optimization_barrier((dx, output))
+    dx, tails = lax.optimization_barrier((dx, tails))
+    tails = swap(tails)
+    d_rows = pl.pallas_call(
+        functools.partial(unpack_kernel, G, per_key),
+        out_shape=jax.ShapeDtypeStruct((length, channels), bf16),
+        compiler_params=pltpu.CompilerParams(vmem_limit_bytes=VMEM),
+        name="unpack",
+    )(o, dx)
+    d_rows, tails, output = lax.optimization_barrier((d_rows, tails, output))
+    last_rows = pl.BlockSpec((RIM, channels), lambda s: (length // RIM - 1, 0))
     d_rows, d_weight, d_decay, d_beta = pl.pallas_call(
-        functools.partial(unpack_kernel, G, per_key),
-        in_specs=[pl.BlockSpec(memory_space=pltpu.SMEM)] + [pl.BlockSpec(memory_space=pltpu.VMEM)] * 2,
+        functools.partial(final_kernel, G, per_key),
+        grid=(1,),
+        in_specs=[
+            pl.BlockSpec(memory_space=pltpu.SMEM),
+            pl.BlockSpec(tails.shape, lambda s: (0, 0, 0)),
+            last_rows,
+        ],
+        out_specs=[last_rows]
+        + [pl.BlockSpec(shape, lambda s: (0, 0)) for shape in ((4, channels), (heads, length), (heads, length))],
         out_shape=[
             jax.ShapeDtypeStruct((length, channels), bf16),
             jax.ShapeDtypeStruct((4, channels), f32),
             jax.ShapeDtypeStruct((heads, length), f32),
             jax.ShapeDtypeStruct((heads, length), f32),
         ],
-        compiler_params=pltpu.CompilerParams(vmem_limit_bytes=VMEM),
-        name="unpack",
-    )((member == G - 1).astype(f32)[None], o, dx)
+        input_output_aliases={2: 0},
+        name="totals",
+    )(last, tails, d_rows)
     return (output[None], d_rows[None], d_weight, d_decay[None], d_beta[None])
 
 

time: 126 us -> 122 us (0.968)
  waiting for transfers between devices: 26.8 us -> 15.2 us
  starting transfers between devices: 31.4 us -> 42.7 us
  local copies, waits for them, and re-layouts: 8.63 us -> 5.56 us
    all_to_all x4 -> x5, waiting for transfers between devices: 22.6 us -> 10.6 us  [swap(): return lax.all_to_all(x, 'seq', 0, 0, axis_index_groups=team)]
    all_to_all x4 -> x5, starting transfers between devices: 18.1 us -> 27.8 us  [swap(): return lax.all_to_all(x, 'seq', 0, 0, axis_index_groups=team)]
    unnamed x30 -> x21, local copies, waits for them, and re-layouts: 6.23 us -> 3.09 us
    pallas_call x2 -> x3, Pallas kernels: 4.3 us -> 5.78 us  [the longest x1 2.54 us: local(): pl.pallas_call(functools.partial(unpack_kernel, G, per_key), out_shape=ja...]
  transfers between devices with their start and end apart: 10 -> 11, of which waited for: 5 -> 4; matrix products, arithmetic and copies ran while one was open for 5% -> 5% of each run, Pallas kernels for 39% -> 42%
where the time goes in v4:
time: 122 us; the launch traced here: 121 us
  Pallas kernels  52.5 us (43%)
  starting transfers between devices  42.7 us (35%)
  waiting for transfers between devices  15.2 us (12%)
  local copies, waits for them, and re-layouts  5.56 us (5%)
  other arithmetic  4.22 us (3%)
    pallas_call x4, Pallas kernels, call(): pl.pallas_call(functools.partial(kernel, per_key, count), grid=(steps,),...  44.7 us
    all_to_all x5, starting transfers between devices, swap(): return lax.all_to_all(x, 'seq', 0, 0, axis_index_groups=team)  27.8 us
    all_to_all x5, waiting for transfers between devices, swap(): return lax.all_to_all(x, 'seq', 0, 0, axis_index_groups=team)  10.6 us
    ppermute x3, starting transfers between devices, shifted(): lax.ppermute(x, 'seq', [(s, s + by) for s in range(n_seq) if 0 <= s + by...  9.29 us
    ppermute x3, starting transfers between devices, local(): terms.append(lax.ppermute(small, ('dp', 'seq'), perm) if p or q else small)  5.63 us
    ppermute x3, waiting for transfers between devices, local(): terms.append(lax.ppermute(small, ('dp', 'seq'), perm) if p or q else small)  4.63 us
    unnamed x21, local copies, waits for them, and re-layouts  3.09 us
    pallas_call x1, Pallas kernels, local(): pl.pallas_call(functools.partial(unpack_kernel, G, per_key), out_shape=ja...  2.54 us
  transfers between devices with their start and end apart: 11, of which 4 were waited for; matrix products, arithmetic and copies ran while one was open for 5% of the time, Pallas kernels for 42%

profile of v4, /device:TPU:0, one launch (start us, length us, event | category | flops | bytes accessed | tf_op | source)
XLA Modules:
  0.0 121.3 jit_solution(490994793072776709)
XLA Ops:
  0.6 0.7 convert_bitcast_fusion
  1.4 0.1 broadcast_bitcast_fusion.1
  1.5 0.9 slice_bitcast_fusion
  2.4 0.0 copy-start.6
  2.4 0.0 copy-start.7
  2.4 2.4 %collective-permute-start = (bf16[4,4096]{1,0:T(4,128)(2,1)S(1)}, bf16[4,4096]{1,0:T(4,128)(2,1)S(1)}, u32[]{:S(2)}, u32[]{:S(2)}) collective-permute-start(bf16[4,4096]{1,0:T(4,128)(2,1)S(1)} %pad_maximum_fusion.1), channel_id=1, source_target_pairs={{0,1},{1,2},{2,3},{3,4},{4,5},{5,6},{6,7},{7,8},{8,9},{9,10},{10,1... | collective-permute-start | bytes 98312 | tf_op jit(solution)/shard_map/ppermute | solution.py:484
  4.8 1.6 %copy.43 = bf16[1,128,4096]{1,2,0:T(8,128)(2,1)S(1)} copy(bf16[1,128,4096]{2,1,0:T(8,128)(2,1)} %param.6) | data formatting | bytes 2097152 | tf_op args[0]
  6.5 0.0 copy-start.8
  6.6 0.5 copy-done.8
  7.2 0.2 copy.47
  7.4 0.2 copy.48
  7.6 0.0 collective-permute-done
  7.8 1.1 fusion.4
  8.9 6.2 %all-to-all-start = ((bf16[8,144,384]{2,1,0:T(8,128)(2,1)}), bf16[8,144,384]{2,1,0:T(8,128)(2,1)}, u32[]{:S(2)}, u32[]{:S(2)}) async-start(bf16[8,144,384]{2,1,0:T(8,128)(2,1)} %fusion.4), calls=%async_computation | async-start | bytes 1769472 | tf_op jit(solution)/shard_map/all_to_all | solution.py:496
  15.2 0.3 copy.45
  15.4 0.2 copy.46
  15.7 0.2 copy.44
  15.8 0.6 add_convert_fusion.next_ref
  16.5 0.6 dynamic-slice_bitcast_fusion.1
  17.1 0.6 pad_maximum_fusion.4.w_ref
  17.7 1.0 pad_maximum_fusion
  18.6 9.4 %all-to-all-done.x_ref = bf16[8,144,384]{2,1,0:T(8,128)(2,1)} async-done(((bf16[8,144,384]{2,1,0:T(8,128)(2,1)}), bf16[8,144,384]{2,1,0:T(8,128)(2,1)}, u32[]{:S(2)}, u32[]{:S(2)}) %all-to-all-start) | async-done | bytes 884768 | tf_op jit(solution)/shard_map/all_to_all | solution.py:496
  28.0 4.2 %all-to-all-start.1 = ((bf16[8,128,384]{2,1,0:T(8,128)(2,1)}), bf16[8,128,384]{2,1,0:T(8,128)(2,1)}, u32[]{:S(2)}, u32[]{:S(2)}) async-start(bf16[8,128,384]{2,1,0:T(8,128)(2,1)} %pad_maximum_fusion), calls=%async_computation.1 | async-start | bytes 1572864 | tf_op jit(solution)/shard_map/all_to_all | solution.py:496
  32.3 13.7 %keys.1 = (f32[8,128,128]{2,1,0:T(8,128)}, f32[8,2,128,128]{3,2,1,0:T(8,128)}, f32[8,2,128,128]{3,2,1,0:T(8,128)}, f32[8,2,128,128]{3,2,1,0:T(8,128)}, f32[8,2,1...) custom-call(bf16[8,144,384]{2,1,0:T(8,128)(2,1)} %all-to-all-done.x_ref, ...), custom_call_target="tpu_custom_call" | custom-call | flops 15000000512 | bytes 8388608 | tf_op jit(solution)/shard_map/keys/pallas_call | solution.py:548
  46.0 5.5 %collective-permute-start.2 = (f32[2,128,128]{2,1,0:T(8,128)}, f32[2,128,128]{2,1,0:T(8,128)}, u32[]{:S(2)}, u32[]{:S(2)}) collective-permute-start(f32[2,128,128]{2,1,0:T(8,128)} %get-tuple-element.55), channel_id=1, source_target_pairs={{0,8},{1,9},{2,10},{3,11},{4,12},{5,13},{6,14},{7,15},{16,24},{17,... | collective-permute-start | bytes 393224 | tf_op jit(solution)/shard_map/ppermute | solution.py:484
  51.5 8.1 %queries.1 = (f32[8,2,128,128]{3,2,1,0:T(8,128)}, f32[8,2,128,128]{3,2,1,0:T(8,128)}, f32[8,2,128,128]{3,2,1,0:T(8,128)}, f32[2,128,128]{2,1,0:T(8,128)}) custom-call(bf16[8,144,384]{2,1,0:T(8,128)(2,1)} %all-to-all-done.x_ref, bf16[8,128,384]{2,1,0:T(8,128)(2,1)} %all-to-all-done.1.y_ref, f32[4,128]{1,0:T(4,128)} %get-tuple-element.46.w_ref, ...), custom_call_target="tpu_custom_call" | custom-call | flops 8000000000 | bytes 8388608 | tf_op jit(solution)/shard_map/queries/pallas_call | solution.py:548
  59.6 1.5 %collective-permute-start.1 = (f32[2,128,128]{2,1,0:T(8,128)}, f32[2,128,128]{2,1,0:T(8,128)}, u32[]{:S(2)}, u32[]{:S(2)}) collective-permute-start(f32[2,128,128]{2,1,0:T(8,128)} %get-tuple-element.51), channel_id=1, source_target_pairs={{8,0},{9,1},{10,2},{11,3},{12,4},{13,5},{14,6},{15,7},{24,16},{25,... | collective-permute-start | bytes 393224 | tf_op jit(solution)/shard_map/ppermute | solution.py:484
  61.0 0.0 collective-permute-done.2.in_ref
  61.1 9.2 %reads.1 = (bf16[8,128,384]{2,1,0:T(8,128)(2,1)}, f32[8,2,128,128]{3,2,1,0:T(8,128)}, f32[8,2,128,128]{3,2,1,0:T(8,128)}, f32[8,128,128]{2,1,0:T(8,128)}, f32[8,...) custom-call(f32[2,128,128]{2,1,0:T(8,128)} %collective-permute-done.2.in_ref, ...), custom_call_target="tpu_custom_call" | custom-call | flops 8000000000 | bytes 8388608 | tf_op jit(solution)/shard_map/reads/pallas_call | solution.py:548
  70.3 4.2 %all-to-all-start.2 = ((bf16[8,128,384]{2,1,0:T(8,128)(2,1)}), bf16[8,128,384]{2,1,0:T(8,128)(2,1)}, u32[]{:S(2)}, u32[]{:S(2)}) async-start(bf16[8,128,384]{2,1,0:T(8,128)(2,1)} %get-tuple-element.67), calls=%async_computation.2 | async-start | bytes 1572864 | tf_op jit(solution)/shard_map/all_to_all | solution.py:496
  74.6 13.7 %writes.1 = (bf16[8,128,384]{2,1,0:T(8,128)(2,1)}, f32[8,4,128]{2,1,0:T(4,128)}, f32[8,512]{1,0:T(8,128)}) custom-call(f32[2,128,128]{2,1,0:T(8,128)} %collective-permute-done.1.in_ref, bf16[8,144,384]{2,1,0:T(8,128)(2,1)} %all-to-all-done.x_ref, f32[4,384]{1,0:T(4,128)} %pad_maximum_fusion.4.w_ref, f32[8,128,128]{2,1,0:T(8,128)} %get-tuple-element.48.k_ref, ...), custom_call_target="tpu_custom_call" | custom-call | flops 15000000512 | bytes 8388608 | tf_op jit(solution)/shard_map/writes/pallas_call | solution.py:548
  88.2 0.0 all-to-all-done.2.o_ref
  88.2 4.2 %all-to-all-start.3 = ((bf16[8,128,384]{2,1,0:T(8,128)(2,1)}), bf16[8,128,384]{2,1,0:T(8,128)(2,1)}, u32[]{:S(2)}, u32[]{:S(2)}) async-start(bf16[8,128,384]{2,1,0:T(8,128)(2,1)} %get-tuple-element.69), calls=%async_computation.3 | async-start | bytes 1572864 | tf_op jit(solution)/shard_map/all_to_all | solution.py:496
  92.5 5.0 %collective-permute-start.5 = (f32[8,512]{1,0:T(8,128)S(1)}, f32[8,512]{1,0:T(8,128)S(1)}, u32[]{:S(2)}, u32[]{:S(2)}) collective-permute-start(f32[8,512]{1,0:T(8,128)S(1)} %copy-done.2), channel_id=1, source_target_pairs={{0,24},{1,25},{2,26},{3,27},{4,28},{5,29},{6,30},{7,31},{8,16},{9,... | collective-permute-start | bytes 49160 | tf_op jit(solution)/shard_map/ppermute | solution.py:602
  97.5 0.5 collective-permute-start.4
  98.0 0.1 collective-permute-start.3
  98.1 4.3 %collective-permute-done.5.refs_3_ = f32[8,512]{1,0:T(8,128)S(1)} collective-permute-done((f32[8,512]{1,0:T(8,128)S(1)}, f32[8,512]{1,0:T(8,128)S(1)}, u32[]{:S(2)}, u32[]{:S(2)}) %collective-permute-start.5) | collective-permute-done | bytes 16416 | tf_op jit(solution)/shard_map/ppermute | solution.py:602
  102.5 0.3 collective-permute-done.3.refs_1_
  102.8 0.3 copy-done.3
  103.1 0.0 copy-done.4
  103.1 0.3 copy-done.5
  103.4 1.5 %tails.1 = bf16[8,32,384]{2,1,0:T(8,128)(2,1)} custom-call(f32[2]{0:T(128)} %add_convert_fusion.next_ref, f32[8,4,128]{2,1,0:T(4,128)} %get-tuple-element.71.gates_ref, f32[8,512]{1,0:T(8,128)} %get-tuple-element.72.refs_0_, f32[8,512]{1,0:T(8,128)} %copy-done.5, f32[8,512]{1,0:T(8,128)} %copy-done.4, f32[8,512]{1,0:T(8,128)} %copy-done.3), custom_call_target="tpu_custom_call" | custom-call | tf_op jit(solution)/shard_map/tails/pallas_call | solution.py:603
  104.9 0.0 all-to-all-done.3.dx_ref
  104.9 8.9 %all-to-all-start.4 = ((bf16[8,32,384]{2,1,0:T(8,128)(2,1)}), bf16[8,32,384]{2,1,0:T(8,128)(2,1)}, u32[]{:S(2)}, u32[]{:S(2)}) async-start(bf16[8,32,384]{2,1,0:T(8,128)(2,1)} %tails.1), calls=%async_computation.4 | async-start | bytes 393216 | tf_op jit(solution)/shard_map/all_to_all | solution.py:496
  113.8 2.0 %outputs.1 = bf16[128,2048]{1,0:T(8,128)(2,1)} custom-call(bf16[8,128,384]{2,1,0:T(8,128)(2,1)} %all-to-all-done.2.o_ref), custom_call_target="tpu_custom_call" | custom-call | bytes 3145728 | tf_op jit(solution)/shard_map/outputs/pallas_call | solution.py:611
  115.8 2.5 %unpack.1.rows_in = bf16[128,4096]{1,0:T(8,128)(2,1)} custom-call(bf16[8,128,384]{2,1,0:T(8,128)(2,1)} %all-to-all-done.2.o_ref, bf16[8,128,384]{2,1,0:T(8,128)(2,1)} %all-to-all-done.3.dx_ref), custom_call_target="tpu_custom_call" | custom-call | tf_op jit(solution)/shard_map/unpack/pallas_call | solution.py:619
  118.3 1.2 %all-to-all-done.4.tail_ref = bf16[8,32,384]{2,1,0:T(8,128)(2,1)} async-done(((bf16[8,32,384]{2,1,0:T(8,128)(2,1)}), bf16[8,32,384]{2,1,0:T(8,128)(2,1)}, u32[]{:S(2)}, u32[]{:S(2)}) %all-to-all-start.4) | async-done | bytes 196640 | tf_op jit(solution)/shard_map/all_to_all | solution.py:496
  119.6 1.7 %totals.1 = (bf16[128,4096]{1,0:T(8,128)(2,1)}, f32[4,4096]{1,0:T(4,128)}, f32[16,128]{1,0:T(8,128)}, f32[16,128]{1,0:T(8,128)}) custom-call(f32[1]{0:T(128)} %bitcast.32.last_ref, bf16[8,32,384]{2,1,0:T(8,128)(2,1)} %all-to-all-done.4.tail_ref, bf16[128,4096]{1,0:T(8,128)(2,1)} %unpack.1.rows_in), custom_call_target="tpu_custom_call", output_to_operand_aliasing={{0}: (2, {})} | custom-call | tf_op jit(solution)/shard_map/totals/pallas_call | solution.py:627
  (36 shorter events, 0.3 us)
Async XLA Ops:
  2.4 4.1 %copy-start.6 = (f32[1,16,128]{2,1,0:T(8,128)S(1)}, f32[1,16,128]{2,1,0:T(8,128)}, u32[]{:S(2)}) copy-start(f32[1,16,128]{2,1,0:T(8,128)} %param.8) | copy-start | bytes 24580
  2.4 4.1 %copy-start.7 = (f32[1,16,128]{2,1,0:T(8,128)S(1)}, f32[1,16,128]{2,1,0:T(8,128)}, u32[]{:S(2)}) copy-start(f32[1,16,128]{2,1,0:T(8,128)} %param.9) | copy-start | bytes 24580
  2.4 5.2 %collective-permute-start = (bf16[4,4096]{1,0:T(4,128)(2,1)S(1)}, bf16[4,4096]{1,0:T(4,128)(2,1)S(1)}, u32[]{:S(2)}, u32[]{:S(2)}) collective-permute-start(bf16[4,4096]{1,0:T(4,128)(2,1)S(1)} %pad_maximum_fusion.1), channel_id=1, source_target_pairs={{0,1},{1,2},{2,3},{3,4},{4,5},{5,6},{6,7},{7,8},{8,9},{9,10},{10,1... | collective-permute-start | bytes 98312 | tf_op jit(solution)/shard_map/ppermute | solution.py:484
  6.5 0.7 copy-start.8
  8.9 6.2 %copy-start.1 = (bf16[4,4096]{1,0:T(4,128)(2,1)S(1)}, bf16[4,4096]{1,0:T(4,128)(2,1)}, u32[]{:S(2)}) copy-start(bf16[4,4096]{1,0:T(4,128)(2,1)} %param.7) | copy-start | bytes 98308
  8.9 6.2 %copy-start = (bf16[1,128,2048]{2,1,0:T(8,128)(2,1)S(1)}, bf16[1,128,2048]{2,1,0:T(8,128)(2,1)}, u32[]{:S(2)}) copy-start(bf16[1,128,2048]{2,1,0:T(8,128)(2,1)} %param.11) | copy-start | bytes 1572868
  8.9 19.1 %all-to-all-start = ((bf16[8,144,384]{2,1,0:T(8,128)(2,1)}), bf16[8,144,384]{2,1,0:T(8,128)(2,1)}, u32[]{:S(2)}, u32[]{:S(2)}) async-start(bf16[8,144,384]{2,1,0:T(8,128)(2,1)} %fusion.4), calls=%async_computation | async-start | bytes 1769472 | tf_op jit(solution)/shard_map/all_to_all | solution.py:496
  28.0 23.4 %all-to-all-start.1 = ((bf16[8,128,384]{2,1,0:T(8,128)(2,1)}), bf16[8,128,384]{2,1,0:T(8,128)(2,1)}, u32[]{:S(2)}, u32[]{:S(2)}) async-start(bf16[8,128,384]{2,1,0:T(8,128)(2,1)} %pad_maximum_fusion), calls=%async_computation.1 | async-start | bytes 1572864 | tf_op jit(solution)/shard_map/all_to_all | solution.py:496
  46.0 15.1 %collective-permute-start.2 = (f32[2,128,128]{2,1,0:T(8,128)}, f32[2,128,128]{2,1,0:T(8,128)}, u32[]{:S(2)}, u32[]{:S(2)}) collective-permute-start(f32[2,128,128]{2,1,0:T(8,128)} %get-tuple-element.55), channel_id=1, source_target_pairs={{0,8},{1,9},{2,10},{3,11},{4,12},{5,13},{6,14},{7,15},{16,24},{17,... | collective-permute-start | bytes 393224 | tf_op jit(solution)/shard_map/ppermute | solution.py:484
  59.6 15.0 %collective-permute-start.1 = (f32[2,128,128]{2,1,0:T(8,128)}, f32[2,128,128]{2,1,0:T(8,128)}, u32[]{:S(2)}, u32[]{:S(2)}) collective-permute-start(f32[2,128,128]{2,1,0:T(8,128)} %get-tuple-element.51), channel_id=1, source_target_pairs={{8,0},{9,1},{10,2},{11,3},{12,4},{13,5},{14,6},{15,7},{24,16},{25,... | collective-permute-start | bytes 393224 | tf_op jit(solution)/shard_map/ppermute | solution.py:484
  70.3 17.9 %all-to-all-start.2 = ((bf16[8,128,384]{2,1,0:T(8,128)(2,1)}), bf16[8,128,384]{2,1,0:T(8,128)(2,1)}, u32[]{:S(2)}, u32[]{:S(2)}) async-start(bf16[8,128,384]{2,1,0:T(8,128)(2,1)} %get-tuple-element.67), calls=%async_computation.2 | async-start | bytes 1572864 | tf_op jit(solution)/shard_map/all_to_all | solution.py:496
  88.2 4.3 %copy-start.2 = (f32[8,512]{1,0:T(8,128)S(1)}, f32[8,512]{1,0:T(8,128)}, u32[]{:S(2)}) copy-start(f32[8,512]{1,0:T(8,128)} %get-tuple-element.72.refs_0_) | copy-start | bytes 49156
  88.2 16.6 %all-to-all-start.3 = ((bf16[8,128,384]{2,1,0:T(8,128)(2,1)}), bf16[8,128,384]{2,1,0:T(8,128)(2,1)}, u32[]{:S(2)}, u32[]{:S(2)}) async-start(bf16[8,128,384]{2,1,0:T(8,128)(2,1)} %get-tuple-element.69), calls=%async_computation.3 | async-start | bytes 1572864 | tf_op jit(solution)/shard_map/all_to_all | solution.py:496
  92.5 10.0 %collective-permute-start.5 = (f32[8,512]{1,0:T(8,128)S(1)}, f32[8,512]{1,0:T(8,128)S(1)}, u32[]{:S(2)}, u32[]{:S(2)}) collective-permute-start(f32[8,512]{1,0:T(8,128)S(1)} %copy-done.2), channel_id=1, source_target_pairs={{0,24},{1,25},{2,26},{3,27},{4,28},{5,29},{6,30},{7,31},{8,16},{9,... | collective-permute-start | bytes 49160 | tf_op jit(solution)/shard_map/ppermute | solution.py:602
  97.5 5.0 %collective-permute-start.4 = (f32[8,512]{1,0:T(8,128)S(1)}, f32[8,512]{1,0:T(8,128)S(1)}, u32[]{:S(2)}, u32[]{:S(2)}) collective-permute-start(f32[8,512]{1,0:T(8,128)S(1)} %copy-done.2), channel_id=1, source_target_pairs={{0,16},{1,17},{2,18},{3,19},{4,20},{5,21},{6,22},{7,23},{8,24},{9,... | collective-permute-start | bytes 49160 | tf_op jit(solution)/shard_map/ppermute | solution.py:602
  98.0 4.7 %collective-permute-start.3 = (f32[8,512]{1,0:T(8,128)S(1)}, f32[8,512]{1,0:T(8,128)S(1)}, u32[]{:S(2)}, u32[]{:S(2)}) collective-permute-start(f32[8,512]{1,0:T(8,128)S(1)} %copy-done.2), channel_id=1, source_target_pairs={{0,8},{1,9},{2,10},{3,11},{4,12},{5,13},{6,14},{7,15},{8,0},{9,1},... | collective-permute-start | bytes 49160 | tf_op jit(solution)/shard_map/ppermute | solution.py:602
  102.5 0.6 copy-start.3
  102.5 0.6 copy-start.4
  102.8 0.6 copy-start.5
  104.9 14.7 %all-to-all-start.4 = ((bf16[8,32,384]{2,1,0:T(8,128)(2,1)}), bf16[8,32,384]{2,1,0:T(8,128)(2,1)}, u32[]{:S(2)}, u32[]{:S(2)}) async-start(bf16[8,32,384]{2,1,0:T(8,128)(2,1)} %tails.1), calls=%async_computation.4 | async-start | bytes 393216 | tf_op jit(solution)/shard_map/all_to_all | solution.py:496

commit v5 on v4

--- a/solution.py
+++ b/solution.py
@@ -38,6 +38,16 @@
     if len(a) > 1:
         out = out + dg(a[1], b[0], ca, cb)
     return out
+
+
+def joined(a, b, ca, cb):
+    if len(a) > 1 and len(b) > 1:
+        left, right = (a[0], a[0], a[1]), (b[0], b[1], b[0])
+    elif len(a) > 1:
+        left, right = a, b * 2
+    else:
+        left, right = a * len(b), b
+    return dg(jnp.concatenate(left, ca), jnp.concatenate(right, cb), ca, cb)
 
 
 def iota2(shape, dim):
@@ -164,16 +174,16 @@
     eye = (i == j).astype(f32)
     inner = [jnp.where((i // 8) == (j // 8), n, 0.0) for n in mats]
     s1 = [split(n) for n in inner]
-    s2 = [split(mm(a, a, 1, 0)) for a in s1]
-    low = [eye - n + (a[0].astype(f32) + a[1].astype(f32)) - mm(b, a, 1, 0) for n, a, b in zip(inner, s2, s1)]
-    s4 = [split(mm(a, a, 1, 0)) for a in s2]
-    inv = [t + mm(split(t), a, 1, 0) for t, a in zip(low, s4)]
+    s2 = [split(joined(a, a, 1, 0)) for a in s1]
+    low = [eye - n + (a[0].astype(f32) + a[1].astype(f32)) - joined(b, a, 1, 0) for n, a, b in zip(inner, s2, s1)]
+    s4 = [split(joined(a, a, 1, 0)) for a in s2]
+    inv = [t + joined(split(t), a, 1, 0) for t, a in zip(low, s4)]
     width = 8
     while width < length:
         cross = ((i // (2 * width)) == (j // (2 * width))) & ((i // width) > (j // width))
         st = [split(t) for t in inv]
-        half = [mm(split(jnp.where(cross, n, 0.0)), t, 1, 0) for n, t in zip(mats, st)]
-        inv = [t - mm(s, split(x), 1, 0) for t, s, x in zip(inv, st, half)]
+        half = [joined(split(jnp.where(cross, n, 0.0)), t, 1, 0) for n, t in zip(mats, st)]
+        inv = [t - joined(s, split(x), 1, 0) for t, s, x in zip(inv, st, half)]
         width *= 2
     return inv
 
@@ -209,7 +219,7 @@
         ks.append(k)
         vs.append(act[:, DK:])
     sk = [split(k) for k in ks]
-    kk = [mm(s, s, 1, 1) for s in sk]
+    kk = [joined(s, s, 1, 1) for s in sk]
     ns = [
         jnp.where(metas[n].strict, metas[n].beta[h] * kk[n] * metas[n].fading(h), 0.0) for n, h in pairs
     ]
@@ -218,15 +228,15 @@
         jnp.concatenate([metas[n].both[h] * ks[n], metas[n].beta[h] * vs[n][:, h * DK : (h + 1) * DK]], 1)
         for n, h in pairs
     ]
-    wu = [mm(split(t), split(r), 1, 0) for t, r in zip(ts, rhs)]
-    kwu = [mm(split(metas[n].tail[h] * ks[n]), split(x), 0, 0) for (n, h), x in zip(pairs, wu)]
+    wu = [joined(split(t), split(r), 1, 0) for t, r in zip(ts, rhs)]
+    kwu = [joined(split(metas[n].tail[h] * ks[n]), split(x), 0, 0) for (n, h), x in zip(pairs, wu)]
     for m, (n, h) in enumerate(pairs):
         t_ref[n, h], w_out[n, h], u_ref[n, h] = ts[m], wu[m][:, :DK], wu[m][:, DK:]
         a = metas[n].keep[h] * eye - kwu[m][:, :DK]
         a_ref[n, h] = a
         now = chain[h]
         m_ref[n, h], s_ref[n, h] = now[:, :DK], now[:, DK:]
-        later = mm(split(a), split(now), 1, 0)
+        later = joined(split(a), split(now), 1, 0)
         chain[h] = jnp.concatenate([later[:, :DK], later[:, DK:] + kwu[m][:, DK:]], 1)
     for h in range(per_key):
         end_ref[h] = chain[h, :, DK:]
@@ -355,17 +365,17 @@
         hats[n], inv[n] = unit(act[:, :DK])
         vs[n] = act[:, DK:]
         sk[n] = split(k_ref[n])
-        kk[n] = mm(sk[n], sk[n], 1, 1)
-    later = [gl_ref[n, h] + mm(split(m_ref[n, h]), g_in[h], 1, 0) for n, h in pairs]
+        kk[n] = joined(sk[n], sk[n], 1, 1)
+    later = [gl_ref[n, h] + joined(split(m_ref[n, h]), g_in[h], 1, 0) for n, h in pairs]
     s_later = [split(x) for x in later]
     s_d = [split(d_ref[n, h]) for n, h in pairs]
     s_s = [split(s_ref[n, h]) for n, h in pairs]
-    kg = {n: mm(sk[n], cat([s_later[m] for m in range(len(pairs)) if pairs[m][0] == n], 1), 1, 0) for n in range(count)}
+    kg = {n: joined(sk[n], cat([s_later[m] for m in range(len(pairs)) if pairs[m][0] == n], 1), 1, 0) for n in range(count)}
     x1 = [metas[n].tail[h] * kg[n][:, h * DK : (h + 1) * DK] for n, h in pairs]
-    es = [e_ref[n, h] + mm(split(t_ref[n, h]), split(x), 0, 0) for (n, h), x in zip(pairs, x1)]
+    es = [e_ref[n, h] + joined(split(t_ref[n, h]), split(x), 0, 0) for (n, h), x in zip(pairs, x1)]
     se = [split(e) for e in es]
-    ends = [metas[n].tail[h] * mm(d, s, 1, 1) for (n, h), d, s in zip(pairs, s_d, s_later)]
-    back = [mm(e, cat([d, s], 0), 1, 1) for e, d, s in zip(se, s_d, s_s)]
+    ends = [metas[n].tail[h] * joined(d, s, 1, 1) for (n, h), d, s in zip(pairs, s_d, s_later)]
+    back = [joined(e, cat([d, s], 0), 1, 1) for e, d, s in zip(se, s_d, s_s)]
     ess = [x[:, length:] for x in back]
     dkk = [
         jnp.where(metas[n].strict, x[:, :length] * (-metas[n].beta[h] * metas[n].fading(h)), 0.0)
@@ -377,7 +387,7 @@
         meta, k = metas[n], k_ref[n]
         s_dkk = split(sum(dkk[m] for m in mine))
         bes = [meta.both[h] * ess[m] for h, m in enumerate(mine)]
-        dk[n] = dk_ref[n] + mm(s_dkk, sk[n], 1, 0) + mm(s_dkk, sk[n], 0, 0) + sum(ends[m] - b for b, m in zip(bes, mine))
+        dk[n] = dk_ref[n] + joined(s_dkk, sk[n], 1, 0) + joined(s_dkk, sk[n], 0, 0) + sum(ends[m] - b for b, m in zip(bes, mine))
         nn = [dkk[m] * kk[n] for m in mine]
         ek = [ends[m] * k for m in mine]
         mats = [x - b * k - y for x, b, y in zip(nn, bes, ek)] + nn
@@ -389,7 +399,7 @@
             dc_ref[n, h : h + 1, :] + sums[h : h + 1] - jnp.sum(nn[h], 0, keepdims=True) for h in range(per_key)
         ]
         dc = jnp.concatenate(dc + [jnp.zeros((8 - per_key, length), f32)], 0)
-        decays = mm(split(dc), (from_here,), 1, 0)
+        decays = joined(split(dc), (from_here,), 1, 0)
         for h, m in enumerate(mine):
             dv[n, h] = meta.beta[h] * es[m]
             last = jnp.sum(ek[h] + later[m] * s_ref[n, h] * meta.keep[h], 0, keepdims=True)

time: 122 us -> 121 us (level)
  transfers between devices with their start and end apart: 11 -> 11, of which waited for: 4 -> 4; matrix products, arithmetic and copies ran while one was open for 5% -> 5% of each run, Pallas kernels for 42% -> 41%
where the time goes in v5:
time: 121 us; the launch traced here: 120 us
  Pallas kernels  51.5 us (43%)
  starting transfers between devices  42.8 us (35%)
  waiting for transfers between devices  15.2 us (13%)
  local copies, waits for them, and re-layouts  5.56 us (5%)
  other arithmetic  4.22 us (3%)
    pallas_call x4, Pallas kernels, call(): pl.pallas_call(functools.partial(kernel, per_key, count), grid=(steps,),...  43.8 us
    all_to_all x5, starting transfers between devices, swap(): return lax.all_to_all(x, 'seq', 0, 0, axis_index_groups=team)  27.8 us
    all_to_all x5, waiting for transfers between devices, swap(): return lax.all_to_all(x, 'seq', 0, 0, axis_index_groups=team)  10.6 us
    ppermute x3, starting transfers between devices, shifted(): lax.ppermute(x, 'seq', [(s, s + by) for s in range(n_seq) if 0 <= s + by...  9.29 us
    ppermute x3, starting transfers between devices, local(): terms.append(lax.ppermute(small, ('dp', 'seq'), perm) if p or q else small)  5.66 us
    ppermute x3, waiting for transfers between devices, local(): terms.append(lax.ppermute(small, ('dp', 'seq'), perm) if p or q else small)  4.61 us
    unnamed x21, local copies, waits for them, and re-layouts  3.09 us
    pallas_call x1, Pallas kernels, local(): pl.pallas_call(functools.partial(unpack_kernel, G, per_key), out_shape=ja...  2.54 us
  transfers between devices with their start and end apart: 11, of which 4 were waited for; matrix products, arithmetic and copies ran while one was open for 5% of the time, Pallas kernels for 41%

profile of v5, /device:TPU:0, one launch (start us, length us, event | category | flops | bytes accessed | tf_op | source)
XLA Modules:
  0.0 120.4 jit_solution(12934330904849874478)
XLA Ops:
  0.6 0.7 convert_bitcast_fusion
  1.4 0.1 broadcast_bitcast_fusion.1
  1.5 0.9 slice_bitcast_fusion
  2.4 0.0 copy-start.6
  2.4 0.0 copy-start.7
  2.4 2.4 %collective-permute-start = (bf16[4,4096]{1,0:T(4,128)(2,1)S(1)}, bf16[4,4096]{1,0:T(4,128)(2,1)S(1)}, u32[]{:S(2)}, u32[]{:S(2)}) collective-permute-start(bf16[4,4096]{1,0:T(4,128)(2,1)S(1)} %pad_maximum_fusion.1), channel_id=1, source_target_pairs={{0,1},{1,2},{2,3},{3,4},{4,5},{5,6},{6,7},{7,8},{8,9},{9,10},{10,1... | collective-permute-start | bytes 98312 | tf_op jit(solution)/shard_map/ppermute | solution.py:494
  4.8 1.6 %copy.43 = bf16[1,128,4096]{1,2,0:T(8,128)(2,1)S(1)} copy(bf16[1,128,4096]{2,1,0:T(8,128)(2,1)} %param.6) | data formatting | bytes 2097152 | tf_op args[0]
  6.5 0.0 copy-start.8
  6.6 0.5 copy-done.8
  7.2 0.2 copy.47
  7.4 0.2 copy.48
  7.6 0.0 collective-permute-done
  7.8 1.1 fusion.4
  8.9 6.2 %all-to-all-start = ((bf16[8,144,384]{2,1,0:T(8,128)(2,1)}), bf16[8,144,384]{2,1,0:T(8,128)(2,1)}, u32[]{:S(2)}, u32[]{:S(2)}) async-start(bf16[8,144,384]{2,1,0:T(8,128)(2,1)} %fusion.4), calls=%async_computation | async-start | bytes 1769472 | tf_op jit(solution)/shard_map/all_to_all | solution.py:506
  15.2 0.3 copy.45
  15.4 0.2 copy.46
  15.7 0.2 copy.44
  15.8 0.6 add_convert_fusion.next_ref
  16.5 0.6 dynamic-slice_bitcast_fusion.1
  17.1 0.6 pad_maximum_fusion.4.w_ref
  17.7 1.0 pad_maximum_fusion
  18.6 9.4 %all-to-all-done.x_ref = bf16[8,144,384]{2,1,0:T(8,128)(2,1)} async-done(((bf16[8,144,384]{2,1,0:T(8,128)(2,1)}), bf16[8,144,384]{2,1,0:T(8,128)(2,1)}, u32[]{:S(2)}, u32[]{:S(2)}) %all-to-all-start) | async-done | bytes 884768 | tf_op jit(solution)/shard_map/all_to_all | solution.py:506
  28.0 4.2 %all-to-all-start.1 = ((bf16[8,128,384]{2,1,0:T(8,128)(2,1)}), bf16[8,128,384]{2,1,0:T(8,128)(2,1)}, u32[]{:S(2)}, u32[]{:S(2)}) async-start(bf16[8,128,384]{2,1,0:T(8,128)(2,1)} %pad_maximum_fusion), calls=%async_computation.1 | async-start | bytes 1572864 | tf_op jit(solution)/shard_map/all_to_all | solution.py:506
  32.3 13.3 %keys.1 = (f32[8,128,128]{2,1,0:T(8,128)}, f32[8,2,128,128]{3,2,1,0:T(8,128)}, f32[8,2,128,128]{3,2,1,0:T(8,128)}, f32[8,2,128,128]{3,2,1,0:T(8,128)}, f32[8,2,1...) custom-call(bf16[8,144,384]{2,1,0:T(8,128)(2,1)} %all-to-all-done.x_ref, ...), custom_call_target="tpu_custom_call" | custom-call | flops 15000000512 | bytes 8388608 | tf_op jit(solution)/shard_map/keys/pallas_call | solution.py:558
  45.5 5.5 %collective-permute-start.2 = (f32[2,128,128]{2,1,0:T(8,128)}, f32[2,128,128]{2,1,0:T(8,128)}, u32[]{:S(2)}, u32[]{:S(2)}) collective-permute-start(f32[2,128,128]{2,1,0:T(8,128)} %get-tuple-element.55), channel_id=1, source_target_pairs={{0,8},{1,9},{2,10},{3,11},{4,12},{5,13},{6,14},{7,15},{16,24},{17,... | collective-permute-start | bytes 393224 | tf_op jit(solution)/shard_map/ppermute | solution.py:494
  51.0 0.0 all-to-all-done.1.y_ref
  51.0 8.1 %queries.1 = (f32[8,2,128,128]{3,2,1,0:T(8,128)}, f32[8,2,128,128]{3,2,1,0:T(8,128)}, f32[8,2,128,128]{3,2,1,0:T(8,128)}, f32[2,128,128]{2,1,0:T(8,128)}) custom-call(bf16[8,144,384]{2,1,0:T(8,128)(2,1)} %all-to-all-done.x_ref, bf16[8,128,384]{2,1,0:T(8,128)(2,1)} %all-to-all-done.1.y_ref, f32[4,128]{1,0:T(4,128)} %get-tuple-element.46.w_ref, ...), custom_call_target="tpu_custom_call" | custom-call | flops 8000000000 | bytes 8388608 | tf_op jit(solution)/shard_map/queries/pallas_call | solution.py:558
  59.1 1.5 %collective-permute-start.1 = (f32[2,128,128]{2,1,0:T(8,128)}, f32[2,128,128]{2,1,0:T(8,128)}, u32[]{:S(2)}, u32[]{:S(2)}) collective-permute-start(f32[2,128,128]{2,1,0:T(8,128)} %get-tuple-element.51), channel_id=1, source_target_pairs={{8,0},{9,1},{10,2},{11,3},{12,4},{13,5},{14,6},{15,7},{24,16},{25,... | collective-permute-start | bytes 393224 | tf_op jit(solution)/shard_map/ppermute | solution.py:494
  60.6 0.0 collective-permute-done.2.in_ref
  60.6 9.2 %reads.1 = (bf16[8,128,384]{2,1,0:T(8,128)(2,1)}, f32[8,2,128,128]{3,2,1,0:T(8,128)}, f32[8,2,128,128]{3,2,1,0:T(8,128)}, f32[8,128,128]{2,1,0:T(8,128)}, f32[8,...) custom-call(f32[2,128,128]{2,1,0:T(8,128)} %collective-permute-done.2.in_ref, ...), custom_call_target="tpu_custom_call" | custom-call | flops 8000000000 | bytes 8388608 | tf_op jit(solution)/shard_map/reads/pallas_call | solution.py:558
  69.8 4.2 %all-to-all-start.2 = ((bf16[8,128,384]{2,1,0:T(8,128)(2,1)}), bf16[8,128,384]{2,1,0:T(8,128)(2,1)}, u32[]{:S(2)}, u32[]{:S(2)}) async-start(bf16[8,128,384]{2,1,0:T(8,128)(2,1)} %get-tuple-element.67), calls=%async_computation.2 | async-start | bytes 1572864 | tf_op jit(solution)/shard_map/all_to_all | solution.py:506
  74.1 13.2 %writes.1 = (bf16[8,128,384]{2,1,0:T(8,128)(2,1)}, f32[8,4,128]{2,1,0:T(4,128)}, f32[8,512]{1,0:T(8,128)}) custom-call(f32[2,128,128]{2,1,0:T(8,128)} %collective-permute-done.1.in_ref, bf16[8,144,384]{2,1,0:T(8,128)(2,1)} %all-to-all-done.x_ref, f32[4,384]{1,0:T(4,128)} %pad_maximum_fusion.4.w_ref, f32[8,128,128]{2,1,0:T(8,128)} %get-tuple-element.48.k_ref, ...), custom_call_target="tpu_custom_call" | custom-call | flops 15000000512 | bytes 8388608 | tf_op jit(solution)/shard_map/writes/pallas_call | solution.py:558
  87.3 0.0 all-to-all-done.2.o_ref
  87.3 4.2 %all-to-all-start.3 = ((bf16[8,128,384]{2,1,0:T(8,128)(2,1)}), bf16[8,128,384]{2,1,0:T(8,128)(2,1)}, u32[]{:S(2)}, u32[]{:S(2)}) async-start(bf16[8,128,384]{2,1,0:T(8,128)(2,1)} %get-tuple-element.69), calls=%async_computation.3 | async-start | bytes 1572864 | tf_op jit(solution)/shard_map/all_to_all | solution.py:506
  91.5 5.0 %collective-permute-start.5 = (f32[8,512]{1,0:T(8,128)S(1)}, f32[8,512]{1,0:T(8,128)S(1)}, u32[]{:S(2)}, u32[]{:S(2)}) collective-permute-start(f32[8,512]{1,0:T(8,128)S(1)} %copy-done.2), channel_id=1, source_target_pairs={{0,24},{1,25},{2,26},{3,27},{4,28},{5,29},{6,30},{7,31},{8,16},{9,... | collective-permute-start | bytes 49160 | tf_op jit(solution)/shard_map/ppermute | solution.py:612
  96.6 0.5 collective-permute-start.4
  97.1 0.1 collective-permute-start.3
  97.2 4.3 %collective-permute-done.5.refs_3_ = f32[8,512]{1,0:T(8,128)S(1)} collective-permute-done((f32[8,512]{1,0:T(8,128)S(1)}, f32[8,512]{1,0:T(8,128)S(1)}, u32[]{:S(2)}, u32[]{:S(2)}) %collective-permute-start.5) | collective-permute-done | bytes 16416 | tf_op jit(solution)/shard_map/ppermute | solution.py:612
  101.5 0.3 collective-permute-done.3.refs_1_
  101.8 0.3 copy-done.3
  102.1 0.0 copy-done.4
  102.1 0.3 copy-done.5
  102.4 1.5 %tails.1 = bf16[8,32,384]{2,1,0:T(8,128)(2,1)} custom-call(f32[2]{0:T(128)} %add_convert_fusion.next_ref, f32[8,4,128]{2,1,0:T(4,128)} %get-tuple-element.71.gates_ref, f32[8,512]{1,0:T(8,128)} %get-tuple-element.72.refs_0_, f32[8,512]{1,0:T(8,128)} %copy-done.5, f32[8,512]{1,0:T(8,128)} %copy-done.4, f32[8,512]{1,0:T(8,128)} %copy-done.3), custom_call_target="tpu_custom_call" | custom-call | tf_op jit(solution)/shard_map/tails/pallas_call | solution.py:613
  103.9 8.9 %all-to-all-start.4 = ((bf16[8,32,384]{2,1,0:T(8,128)(2,1)}), bf16[8,32,384]{2,1,0:T(8,128)(2,1)}, u32[]{:S(2)}, u32[]{:S(2)}) async-start(bf16[8,32,384]{2,1,0:T(8,128)(2,1)} %tails.1), calls=%async_computation.4 | async-start | bytes 393216 | tf_op jit(solution)/shard_map/all_to_all | solution.py:506
  112.9 2.0 %outputs.1 = bf16[128,2048]{1,0:T(8,128)(2,1)} custom-call(bf16[8,128,384]{2,1,0:T(8,128)(2,1)} %all-to-all-done.2.o_ref), custom_call_target="tpu_custom_call" | custom-call | bytes 3145728 | tf_op jit(solution)/shard_map/outputs/pallas_call | solution.py:621
  114.9 2.5 %unpack.1.rows_in = bf16[128,4096]{1,0:T(8,128)(2,1)} custom-call(bf16[8,128,384]{2,1,0:T(8,128)(2,1)} %all-to-all-done.2.o_ref, bf16[8,128,384]{2,1,0:T(8,128)(2,1)} %all-to-all-done.3.dx_ref), custom_call_target="tpu_custom_call" | custom-call | tf_op jit(solution)/shard_map/unpack/pallas_call | solution.py:629
  117.4 1.2 %all-to-all-done.4.tail_ref = bf16[8,32,384]{2,1,0:T(8,128)(2,1)} async-done(((bf16[8,32,384]{2,1,0:T(8,128)(2,1)}), bf16[8,32,384]{2,1,0:T(8,128)(2,1)}, u32[]{:S(2)}, u32[]{:S(2)}) %all-to-all-start.4) | async-done | bytes 196640 | tf_op jit(solution)/shard_map/all_to_all | solution.py:506
  118.7 1.7 %totals.1 = (bf16[128,4096]{1,0:T(8,128)(2,1)}, f32[4,4096]{1,0:T(4,128)}, f32[16,128]{1,0:T(8,128)}, f32[16,128]{1,0:T(8,128)}) custom-call(f32[1]{0:T(128)} %bitcast.32.last_ref, bf16[8,32,384]{2,1,0:T(8,128)(2,1)} %all-to-all-done.4.tail_ref, bf16[128,4096]{1,0:T(8,128)(2,1)} %unpack.1.rows_in), custom_call_target="tpu_custom_call", output_to_operand_aliasing={{0}: (2, {})} | custom-call | tf_op jit(solution)/shard_map/totals/pallas_call | solution.py:637
  (36 shorter events, 0.3 us)
Async XLA Ops:
  2.4 4.1 %copy-start.6 = (f32[1,16,128]{2,1,0:T(8,128)S(1)}, f32[1,16,128]{2,1,0:T(8,128)}, u32[]{:S(2)}) copy-start(f32[1,16,128]{2,1,0:T(8,128)} %param.8) | copy-start | bytes 24580
  2.4 4.1 %copy-start.7 = (f32[1,16,128]{2,1,0:T(8,128)S(1)}, f32[1,16,128]{2,1,0:T(8,128)}, u32[]{:S(2)}) copy-start(f32[1,16,128]{2,1,0:T(8,128)} %param.9) | copy-start | bytes 24580
  2.4 5.2 %collective-permute-start = (bf16[4,4096]{1,0:T(4,128)(2,1)S(1)}, bf16[4,4096]{1,0:T(4,128)(2,1)S(1)}, u32[]{:S(2)}, u32[]{:S(2)}) collective-permute-start(bf16[4,4096]{1,0:T(4,128)(2,1)S(1)} %pad_maximum_fusion.1), channel_id=1, source_target_pairs={{0,1},{1,2},{2,3},{3,4},{4,5},{5,6},{6,7},{7,8},{8,9},{9,10},{10,1... | collective-permute-start | bytes 98312 | tf_op jit(solution)/shard_map/ppermute | solution.py:494
  6.5 0.7 copy-start.8
  8.9 6.2 %copy-start.1 = (bf16[4,4096]{1,0:T(4,128)(2,1)S(1)}, bf16[4,4096]{1,0:T(4,128)(2,1)}, u32[]{:S(2)}) copy-start(bf16[4,4096]{1,0:T(4,128)(2,1)} %param.7) | copy-start | bytes 98308
  8.9 6.2 %copy-start = (bf16[1,128,2048]{2,1,0:T(8,128)(2,1)S(1)}, bf16[1,128,2048]{2,1,0:T(8,128)(2,1)}, u32[]{:S(2)}) copy-start(bf16[1,128,2048]{2,1,0:T(8,128)(2,1)} %param.11) | copy-start | bytes 1572868
  8.9 19.1 %all-to-all-start = ((bf16[8,144,384]{2,1,0:T(8,128)(2,1)}), bf16[8,144,384]{2,1,0:T(8,128)(2,1)}, u32[]{:S(2)}, u32[]{:S(2)}) async-start(bf16[8,144,384]{2,1,0:T(8,128)(2,1)} %fusion.4), calls=%async_computation | async-start | bytes 1769472 | tf_op jit(solution)/shard_map/all_to_all | solution.py:506
  28.0 23.0 %all-to-all-start.1 = ((bf16[8,128,384]{2,1,0:T(8,128)(2,1)}), bf16[8,128,384]{2,1,0:T(8,128)(2,1)}, u32[]{:S(2)}, u32[]{:S(2)}) async-start(bf16[8,128,384]{2,1,0:T(8,128)(2,1)} %pad_maximum_fusion), calls=%async_computation.1 | async-start | bytes 1572864 | tf_op jit(solution)/shard_map/all_to_all | solution.py:506
  45.5 15.0 %collective-permute-start.2 = (f32[2,128,128]{2,1,0:T(8,128)}, f32[2,128,128]{2,1,0:T(8,128)}, u32[]{:S(2)}, u32[]{:S(2)}) collective-permute-start(f32[2,128,128]{2,1,0:T(8,128)} %get-tuple-element.55), channel_id=1, source_target_pairs={{0,8},{1,9},{2,10},{3,11},{4,12},{5,13},{6,14},{7,15},{16,24},{17,... | collective-permute-start | bytes 393224 | tf_op jit(solution)/shard_map/ppermute | solution.py:494
  59.1 15.0 %collective-permute-start.1 = (f32[2,128,128]{2,1,0:T(8,128)}, f32[2,128,128]{2,1,0:T(8,128)}, u32[]{:S(2)}, u32[]{:S(2)}) collective-permute-start(f32[2,128,128]{2,1,0:T(8,128)} %get-tuple-element.51), channel_id=1, source_target_pairs={{8,0},{9,1},{10,2},{11,3},{12,4},{13,5},{14,6},{15,7},{24,16},{25,... | collective-permute-start | bytes 393224 | tf_op jit(solution)/shard_map/ppermute | solution.py:494
  69.8 17.5 %all-to-all-start.2 = ((bf16[8,128,384]{2,1,0:T(8,128)(2,1)}), bf16[8,128,384]{2,1,0:T(8,128)(2,1)}, u32[]{:S(2)}, u32[]{:S(2)}) async-start(bf16[8,128,384]{2,1,0:T(8,128)(2,1)} %get-tuple-element.67), calls=%async_computation.2 | async-start | bytes 1572864 | tf_op jit(solution)/shard_map/all_to_all | solution.py:506
  87.3 4.3 %copy-start.2 = (f32[8,512]{1,0:T(8,128)S(1)}, f32[8,512]{1,0:T(8,128)}, u32[]{:S(2)}) copy-start(f32[8,512]{1,0:T(8,128)} %get-tuple-element.72.refs_0_) | copy-start | bytes 49156
  87.3 16.6 %all-to-all-start.3 = ((bf16[8,128,384]{2,1,0:T(8,128)(2,1)}), bf16[8,128,384]{2,1,0:T(8,128)(2,1)}, u32[]{:S(2)}, u32[]{:S(2)}) async-start(bf16[8,128,384]{2,1,0:T(8,128)(2,1)} %get-tuple-element.69), calls=%async_computation.3 | async-start | bytes 1572864 | tf_op jit(solution)/shard_map/all_to_all | solution.py:506
  91.5 10.0 %collective-permute-start.5 = (f32[8,512]{1,0:T(8,128)S(1)}, f32[8,512]{1,0:T(8,128)S(1)}, u32[]{:S(2)}, u32[]{:S(2)}) collective-permute-start(f32[8,512]{1,0:T(8,128)S(1)} %copy-done.2), channel_id=1, source_target_pairs={{0,24},{1,25},{2,26},{3,27},{4,28},{5,29},{6,30},{7,31},{8,16},{9,... | collective-permute-start | bytes 49160 | tf_op jit(solution)/shard_map/ppermute | solution.py:612
  96.6 5.0 %collective-permute-start.4 = (f32[8,512]{1,0:T(8,128)S(1)}, f32[8,512]{1,0:T(8,128)S(1)}, u32[]{:S(2)}, u32[]{:S(2)}) collective-permute-start(f32[8,512]{1,0:T(8,128)S(1)} %copy-done.2), channel_id=1, source_target_pairs={{0,16},{1,17},{2,18},{3,19},{4,20},{5,21},{6,22},{7,23},{8,24},{9,... | collective-permute-start | bytes 49160 | tf_op jit(solution)/shard_map/ppermute | solution.py:612
  97.1 4.7 %collective-permute-start.3 = (f32[8,512]{1,0:T(8,128)S(1)}, f32[8,512]{1,0:T(8,128)S(1)}, u32[]{:S(2)}, u32[]{:S(2)}) collective-permute-start(f32[8,512]{1,0:T(8,128)S(1)} %copy-done.2), channel_id=1, source_target_pairs={{0,8},{1,9},{2,10},{3,11},{4,12},{5,13},{6,14},{7,15},{8,0},{9,1},... | collective-permute-start | bytes 49160 | tf_op jit(solution)/shard_map/ppermute | solution.py:612
  101.5 0.6 copy-start.3
  101.5 0.6 copy-start.4
  101.8 0.6 copy-start.5
  103.9 14.7 %all-to-all-start.4 = ((bf16[8,32,384]{2,1,0:T(8,128)(2,1)}), bf16[8,32,384]{2,1,0:T(8,128)(2,1)}, u32[]{:S(2)}, u32[]{:S(2)}) async-start(bf16[8,32,384]{2,1,0:T(8,128)(2,1)} %tails.1), calls=%async_computation.4 | async-start | bytes 393216 | tf_op jit(solution)/shard_map/all_to_all | solution.py:506

commit v6 on v5

--- a/solution.py
+++ b/solution.py
@@ -179,11 +179,28 @@
     s4 = [split(joined(a, a, 1, 0)) for a in s2]
     inv = [t + joined(split(t), a, 1, 0) for t, a in zip(low, s4)]
     width = 8
-    while width < length:
+    while width < min(16, length):
         cross = ((i // (2 * width)) == (j // (2 * width))) & ((i // width) > (j // width))
         st = [split(t) for t in inv]
         half = [joined(split(jnp.where(cross, n, 0.0)), t, 1, 0) for n, t in zip(mats, st)]
         inv = [t - joined(s, split(x), 1, 0) for t, s, x in zip(inv, st, half)]
+        width *= 2
+    while width < length:
+        starts = range(width, length, 2 * width)
+
+        def seconds(x):
+            return jnp.concatenate([x[at : at + width] for at in starts], 0)
+
+        def back(x):
+            gap = jnp.zeros((width, length), x.dtype)
+            return jnp.concatenate([y for m in range(len(starts)) for y in (gap, x[m * width : (m + 1) * width])], 0)
+
+        shape = (length // 2, length)
+        cross = (iota2(shape, 1) // width) == 2 * (iota2(shape, 0) // width)
+        st = [split(t) for t in inv]
+        half = [joined(split(jnp.where(cross, seconds(n), 0.0)), t, 1, 0) for n, t in zip(mats, st)]
+        half = [tuple(back(leaf) for leaf in split(x)) for x in half]
+        inv = [t - back(joined(tuple(seconds(leaf) for leaf in s), x, 1, 0)) for t, s, x in zip(inv, st, half)]
         width *= 2
     return inv
 

time: 121 us -> 120 us (level)
  no operation moved by 1% of the time
where the time goes in v6:
time: 120 us; the launch traced here: 119 us
  Pallas kernels  50.7 us (42%)
  starting transfers between devices  42.8 us (36%)
  waiting for transfers between devices  15.2 us (13%)
  local copies, waits for them, and re-layouts  5.56 us (5%)
  other arithmetic  4.22 us (4%)
    pallas_call x4, Pallas kernels, call(): pl.pallas_call(functools.partial(kernel, per_key, count), grid=(steps,),...  42.9 us
    all_to_all x5, starting transfers between devices, swap(): return lax.all_to_all(x, 'seq', 0, 0, axis_index_groups=team)  27.8 us
    all_to_all x5, waiting for transfers between devices, swap(): return lax.all_to_all(x, 'seq', 0, 0, axis_index_groups=team)  10.6 us
    ppermute x3, starting transfers between devices, shifted(): lax.ppermute(x, 'seq', [(s, s + by) for s in range(n_seq) if 0 <= s + by...  9.3 us
    ppermute x3, starting transfers between devices, local(): terms.append(lax.ppermute(small, ('dp', 'seq'), perm) if p or q else small)  5.64 us
    ppermute x3, waiting for transfers between devices, local(): terms.append(lax.ppermute(small, ('dp', 'seq'), perm) if p or q else small)  4.62 us
    unnamed x21, local copies, waits for them, and re-layouts  3.09 us
    pallas_call x1, Pallas kernels, local(): pl.pallas_call(functools.partial(unpack_kernel, G, per_key), out_shape=ja...  2.54 us
  transfers between devices with their start and end apart: 11, of which 4 were waited for; matrix products, arithmetic and copies ran while one was open for 5% of the time, Pallas kernels for 41%

profile of v6, /device:TPU:0, one launch (start us, length us, event | category | flops | bytes accessed | tf_op | source)
XLA Modules:
  0.0 119.5 jit_solution(9616788035950511415)
XLA Ops:
  0.6 0.7 convert_bitcast_fusion
  1.4 0.1 broadcast_bitcast_fusion.1
  1.5 0.9 slice_bitcast_fusion
  2.4 0.0 copy-start.6
  2.4 0.0 copy-start.7
  2.4 2.4 %collective-permute-start = (bf16[4,4096]{1,0:T(4,128)(2,1)S(1)}, bf16[4,4096]{1,0:T(4,128)(2,1)S(1)}, u32[]{:S(2)}, u32[]{:S(2)}) collective-permute-start(bf16[4,4096]{1,0:T(4,128)(2,1)S(1)} %pad_maximum_fusion.1), channel_id=1, source_target_pairs={{0,1},{1,2},{2,3},{3,4},{4,5},{5,6},{6,7},{7,8},{8,9},{9,10},{10,1... | collective-permute-start | bytes 98312 | tf_op jit(solution)/shard_map/ppermute | solution.py:511
  4.8 1.6 %copy.43 = bf16[1,128,4096]{1,2,0:T(8,128)(2,1)S(1)} copy(bf16[1,128,4096]{2,1,0:T(8,128)(2,1)} %param.6) | data formatting | bytes 2097152 | tf_op args[0]
  6.5 0.0 copy-start.8
  6.6 0.5 copy-done.8
  7.2 0.2 copy.47
  7.4 0.2 copy.48
  7.6 0.0 collective-permute-done
  7.8 1.1 fusion.4
  8.9 6.2 %all-to-all-start = ((bf16[8,144,384]{2,1,0:T(8,128)(2,1)}), bf16[8,144,384]{2,1,0:T(8,128)(2,1)}, u32[]{:S(2)}, u32[]{:S(2)}) async-start(bf16[8,144,384]{2,1,0:T(8,128)(2,1)} %fusion.4), calls=%async_computation | async-start | bytes 1769472 | tf_op jit(solution)/shard_map/all_to_all | solution.py:523
  15.2 0.3 copy.45
  15.4 0.2 copy.46
  15.7 0.2 copy.44
  15.8 0.6 add_convert_fusion.next_ref
  16.5 0.6 dynamic-slice_bitcast_fusion.1
  17.1 0.6 pad_maximum_fusion.4.w_ref
  17.7 1.0 pad_maximum_fusion
  18.6 9.4 %all-to-all-done.x_ref = bf16[8,144,384]{2,1,0:T(8,128)(2,1)} async-done(((bf16[8,144,384]{2,1,0:T(8,128)(2,1)}), bf16[8,144,384]{2,1,0:T(8,128)(2,1)}, u32[]{:S(2)}, u32[]{:S(2)}) %all-to-all-start) | async-done | bytes 884768 | tf_op jit(solution)/shard_map/all_to_all | solution.py:523
  28.0 4.2 %all-to-all-start.1 = ((bf16[8,128,384]{2,1,0:T(8,128)(2,1)}), bf16[8,128,384]{2,1,0:T(8,128)(2,1)}, u32[]{:S(2)}, u32[]{:S(2)}) async-start(bf16[8,128,384]{2,1,0:T(8,128)(2,1)} %pad_maximum_fusion), calls=%async_computation.1 | async-start | bytes 1572864 | tf_op jit(solution)/shard_map/all_to_all | solution.py:523
  32.3 12.4 %keys.1 = (f32[8,128,128]{2,1,0:T(8,128)}, f32[8,2,128,128]{3,2,1,0:T(8,128)}, f32[8,2,128,128]{3,2,1,0:T(8,128)}, f32[8,2,128,128]{3,2,1,0:T(8,128)}, f32[8,2,1...) custom-call(bf16[8,144,384]{2,1,0:T(8,128)(2,1)} %all-to-all-done.x_ref, ...), custom_call_target="tpu_custom_call" | custom-call | flops 15000000512 | bytes 8388608 | tf_op jit(solution)/shard_map/keys/pallas_call | solution.py:575
  44.7 5.5 %collective-permute-start.2 = (f32[2,128,128]{2,1,0:T(8,128)}, f32[2,128,128]{2,1,0:T(8,128)}, u32[]{:S(2)}, u32[]{:S(2)}) collective-permute-start(f32[2,128,128]{2,1,0:T(8,128)} %get-tuple-element.55), channel_id=1, source_target_pairs={{0,8},{1,9},{2,10},{3,11},{4,12},{5,13},{6,14},{7,15},{16,24},{17,... | collective-permute-start | bytes 393224 | tf_op jit(solution)/shard_map/ppermute | solution.py:511
  50.1 0.0 all-to-all-done.1.y_ref
  50.1 8.1 %queries.1 = (f32[8,2,128,128]{3,2,1,0:T(8,128)}, f32[8,2,128,128]{3,2,1,0:T(8,128)}, f32[8,2,128,128]{3,2,1,0:T(8,128)}, f32[2,128,128]{2,1,0:T(8,128)}) custom-call(bf16[8,144,384]{2,1,0:T(8,128)(2,1)} %all-to-all-done.x_ref, bf16[8,128,384]{2,1,0:T(8,128)(2,1)} %all-to-all-done.1.y_ref, f32[4,128]{1,0:T(4,128)} %get-tuple-element.46.w_ref, ...), custom_call_target="tpu_custom_call" | custom-call | flops 8000000000 | bytes 8388608 | tf_op jit(solution)/shard_map/queries/pallas_call | solution.py:575
  58.2 1.5 %collective-permute-start.1 = (f32[2,128,128]{2,1,0:T(8,128)}, f32[2,128,128]{2,1,0:T(8,128)}, u32[]{:S(2)}, u32[]{:S(2)}) collective-permute-start(f32[2,128,128]{2,1,0:T(8,128)} %get-tuple-element.51), channel_id=1, source_target_pairs={{8,0},{9,1},{10,2},{11,3},{12,4},{13,5},{14,6},{15,7},{24,16},{25,... | collective-permute-start | bytes 393224 | tf_op jit(solution)/shard_map/ppermute | solution.py:511
  59.7 0.0 collective-permute-done.2.in_ref
  59.7 9.2 %reads.1 = (bf16[8,128,384]{2,1,0:T(8,128)(2,1)}, f32[8,2,128,128]{3,2,1,0:T(8,128)}, f32[8,2,128,128]{3,2,1,0:T(8,128)}, f32[8,128,128]{2,1,0:T(8,128)}, f32[8,...) custom-call(f32[2,128,128]{2,1,0:T(8,128)} %collective-permute-done.2.in_ref, ...), custom_call_target="tpu_custom_call" | custom-call | flops 8000000000 | bytes 8388608 | tf_op jit(solution)/shard_map/reads/pallas_call | solution.py:575
  69.0 4.2 %all-to-all-start.2 = ((bf16[8,128,384]{2,1,0:T(8,128)(2,1)}), bf16[8,128,384]{2,1,0:T(8,128)(2,1)}, u32[]{:S(2)}, u32[]{:S(2)}) async-start(bf16[8,128,384]{2,1,0:T(8,128)(2,1)} %get-tuple-element.67), calls=%async_computation.2 | async-start | bytes 1572864 | tf_op jit(solution)/shard_map/all_to_all | solution.py:523
  73.2 0.0 collective-permute-done.1.in_ref
  73.2 13.2 %writes.1 = (bf16[8,128,384]{2,1,0:T(8,128)(2,1)}, f32[8,4,128]{2,1,0:T(4,128)}, f32[8,512]{1,0:T(8,128)}) custom-call(f32[2,128,128]{2,1,0:T(8,128)} %collective-permute-done.1.in_ref, bf16[8,144,384]{2,1,0:T(8,128)(2,1)} %all-to-all-done.x_ref, f32[4,384]{1,0:T(4,128)} %pad_maximum_fusion.4.w_ref, f32[8,128,128]{2,1,0:T(8,128)} %get-tuple-element.48.k_ref, ...), custom_call_target="tpu_custom_call" | custom-call | flops 15000000512 | bytes 8388608 | tf_op jit(solution)/shard_map/writes/pallas_call | solution.py:575
  86.4 4.2 %all-to-all-start.3 = ((bf16[8,128,384]{2,1,0:T(8,128)(2,1)}), bf16[8,128,384]{2,1,0:T(8,128)(2,1)}, u32[]{:S(2)}, u32[]{:S(2)}) async-start(bf16[8,128,384]{2,1,0:T(8,128)(2,1)} %get-tuple-element.69), calls=%async_computation.3 | async-start | bytes 1572864 | tf_op jit(solution)/shard_map/all_to_all | solution.py:523
  90.7 5.0 %collective-permute-start.5 = (f32[8,512]{1,0:T(8,128)S(1)}, f32[8,512]{1,0:T(8,128)S(1)}, u32[]{:S(2)}, u32[]{:S(2)}) collective-permute-start(f32[8,512]{1,0:T(8,128)S(1)} %copy-done.2), channel_id=1, source_target_pairs={{0,24},{1,25},{2,26},{3,27},{4,28},{5,29},{6,30},{7,31},{8,16},{9,... | collective-permute-start | bytes 49160 | tf_op jit(solution)/shard_map/ppermute | solution.py:629
  95.7 0.5 collective-permute-start.4
  96.2 0.1 collective-permute-start.3
  96.3 4.3 %collective-permute-done.5.refs_3_ = f32[8,512]{1,0:T(8,128)S(1)} collective-permute-done((f32[8,512]{1,0:T(8,128)S(1)}, f32[8,512]{1,0:T(8,128)S(1)}, u32[]{:S(2)}, u32[]{:S(2)}) %collective-permute-start.5) | collective-permute-done | bytes 16416 | tf_op jit(solution)/shard_map/ppermute | solution.py:629
  100.7 0.3 collective-permute-done.3.refs_1_
  101.0 0.3 copy-done.3
  101.3 0.0 copy-done.4
  101.3 0.3 copy-done.5
  101.6 1.5 %tails.1 = bf16[8,32,384]{2,1,0:T(8,128)(2,1)} custom-call(f32[2]{0:T(128)} %add_convert_fusion.next_ref, f32[8,4,128]{2,1,0:T(4,128)} %get-tuple-element.71.gates_ref, f32[8,512]{1,0:T(8,128)} %get-tuple-element.72.refs_0_, f32[8,512]{1,0:T(8,128)} %copy-done.5, f32[8,512]{1,0:T(8,128)} %copy-done.4, f32[8,512]{1,0:T(8,128)} %copy-done.3), custom_call_target="tpu_custom_call" | custom-call | tf_op jit(solution)/shard_map/tails/pallas_call | solution.py:630
  103.1 8.9 %all-to-all-start.4 = ((bf16[8,32,384]{2,1,0:T(8,128)(2,1)}), bf16[8,32,384]{2,1,0:T(8,128)(2,1)}, u32[]{:S(2)}, u32[]{:S(2)}) async-start(bf16[8,32,384]{2,1,0:T(8,128)(2,1)} %tails.1), calls=%async_computation.4 | async-start | bytes 393216 | tf_op jit(solution)/shard_map/all_to_all | solution.py:523
  112.0 2.0 %outputs.1 = bf16[128,2048]{1,0:T(8,128)(2,1)} custom-call(bf16[8,128,384]{2,1,0:T(8,128)(2,1)} %all-to-all-done.2.o_ref), custom_call_target="tpu_custom_call" | custom-call | bytes 3145728 | tf_op jit(solution)/shard_map/outputs/pallas_call | solution.py:638
  114.0 2.5 %unpack.1.rows_in = bf16[128,4096]{1,0:T(8,128)(2,1)} custom-call(bf16[8,128,384]{2,1,0:T(8,128)(2,1)} %all-to-all-done.2.o_ref, bf16[8,128,384]{2,1,0:T(8,128)(2,1)} %all-to-all-done.3.dx_ref), custom_call_target="tpu_custom_call" | custom-call | tf_op jit(solution)/shard_map/unpack/pallas_call | solution.py:646
  116.5 1.2 %all-to-all-done.4.tail_ref = bf16[8,32,384]{2,1,0:T(8,128)(2,1)} async-done(((bf16[8,32,384]{2,1,0:T(8,128)(2,1)}), bf16[8,32,384]{2,1,0:T(8,128)(2,1)}, u32[]{:S(2)}, u32[]{:S(2)}) %all-to-all-start.4) | async-done | bytes 196640 | tf_op jit(solution)/shard_map/all_to_all | solution.py:523
  117.8 1.7 %totals.1 = (bf16[128,4096]{1,0:T(8,128)(2,1)}, f32[4,4096]{1,0:T(4,128)}, f32[16,128]{1,0:T(8,128)}, f32[16,128]{1,0:T(8,128)}) custom-call(f32[1]{0:T(128)} %bitcast.32.last_ref, bf16[8,32,384]{2,1,0:T(8,128)(2,1)} %all-to-all-done.4.tail_ref, bf16[128,4096]{1,0:T(8,128)(2,1)} %unpack.1.rows_in), custom_call_target="tpu_custom_call", output_to_operand_aliasing={{0}: (2, {})} | custom-call | tf_op jit(solution)/shard_map/totals/pallas_call | solution.py:654
  (36 shorter events, 0.3 us)
Async XLA Ops:
  2.4 4.1 %copy-start.6 = (f32[1,16,128]{2,1,0:T(8,128)S(1)}, f32[1,16,128]{2,1,0:T(8,128)}, u32[]{:S(2)}) copy-start(f32[1,16,128]{2,1,0:T(8,128)} %param.8) | copy-start | bytes 24580
  2.4 4.1 %copy-start.7 = (f32[1,16,128]{2,1,0:T(8,128)S(1)}, f32[1,16,128]{2,1,0:T(8,128)}, u32[]{:S(2)}) copy-start(f32[1,16,128]{2,1,0:T(8,128)} %param.9) | copy-start | bytes 24580
  2.4 5.2 %collective-permute-start = (bf16[4,4096]{1,0:T(4,128)(2,1)S(1)}, bf16[4,4096]{1,0:T(4,128)(2,1)S(1)}, u32[]{:S(2)}, u32[]{:S(2)}) collective-permute-start(bf16[4,4096]{1,0:T(4,128)(2,1)S(1)} %pad_maximum_fusion.1), channel_id=1, source_target_pairs={{0,1},{1,2},{2,3},{3,4},{4,5},{5,6},{6,7},{7,8},{8,9},{9,10},{10,1... | collective-permute-start | bytes 98312 | tf_op jit(solution)/shard_map/ppermute | solution.py:511
  6.5 0.7 copy-start.8
  8.9 6.2 %copy-start.1 = (bf16[4,4096]{1,0:T(4,128)(2,1)S(1)}, bf16[4,4096]{1,0:T(4,128)(2,1)}, u32[]{:S(2)}) copy-start(bf16[4,4096]{1,0:T(4,128)(2,1)} %param.7) | copy-start | bytes 98308
  8.9 6.2 %copy-start = (bf16[1,128,2048]{2,1,0:T(8,128)(2,1)S(1)}, bf16[1,128,2048]{2,1,0:T(8,128)(2,1)}, u32[]{:S(2)}) copy-start(bf16[1,128,2048]{2,1,0:T(8,128)(2,1)} %param.11) | copy-start | bytes 1572868
  8.9 19.1 %all-to-all-start = ((bf16[8,144,384]{2,1,0:T(8,128)(2,1)}), bf16[8,144,384]{2,1,0:T(8,128)(2,1)}, u32[]{:S(2)}, u32[]{:S(2)}) async-start(bf16[8,144,384]{2,1,0:T(8,128)(2,1)} %fusion.4), calls=%async_computation | async-start | bytes 1769472 | tf_op jit(solution)/shard_map/all_to_all | solution.py:523
  28.0 22.1 %all-to-all-start.1 = ((bf16[8,128,384]{2,1,0:T(8,128)(2,1)}), bf16[8,128,384]{2,1,0:T(8,128)(2,1)}, u32[]{:S(2)}, u32[]{:S(2)}) async-start(bf16[8,128,384]{2,1,0:T(8,128)(2,1)} %pad_maximum_fusion), calls=%async_computation.1 | async-start | bytes 1572864 | tf_op jit(solution)/shard_map/all_to_all | solution.py:523
  44.7 15.1 %collective-permute-start.2 = (f32[2,128,128]{2,1,0:T(8,128)}, f32[2,128,128]{2,1,0:T(8,128)}, u32[]{:S(2)}, u32[]{:S(2)}) collective-permute-start(f32[2,128,128]{2,1,0:T(8,128)} %get-tuple-element.55), channel_id=1, source_target_pairs={{0,8},{1,9},{2,10},{3,11},{4,12},{5,13},{6,14},{7,15},{16,24},{17,... | collective-permute-start | bytes 393224 | tf_op jit(solution)/shard_map/ppermute | solution.py:511
  58.2 15.0 %collective-permute-start.1 = (f32[2,128,128]{2,1,0:T(8,128)}, f32[2,128,128]{2,1,0:T(8,128)}, u32[]{:S(2)}, u32[]{:S(2)}) collective-permute-start(f32[2,128,128]{2,1,0:T(8,128)} %get-tuple-element.51), channel_id=1, source_target_pairs={{8,0},{9,1},{10,2},{11,3},{12,4},{13,5},{14,6},{15,7},{24,16},{25,... | collective-permute-start | bytes 393224 | tf_op jit(solution)/shard_map/ppermute | solution.py:511
  69.0 17.5 %all-to-all-start.2 = ((bf16[8,128,384]{2,1,0:T(8,128)(2,1)}), bf16[8,128,384]{2,1,0:T(8,128)(2,1)}, u32[]{:S(2)}, u32[]{:S(2)}) async-start(bf16[8,128,384]{2,1,0:T(8,128)(2,1)} %get-tuple-element.67), calls=%async_computation.2 | async-start | bytes 1572864 | tf_op jit(solution)/shard_map/all_to_all | solution.py:523
  86.4 4.3 %copy-start.2 = (f32[8,512]{1,0:T(8,128)S(1)}, f32[8,512]{1,0:T(8,128)}, u32[]{:S(2)}) copy-start(f32[8,512]{1,0:T(8,128)} %get-tuple-element.72.refs_0_) | copy-start | bytes 49156
  86.4 16.6 %all-to-all-start.3 = ((bf16[8,128,384]{2,1,0:T(8,128)(2,1)}), bf16[8,128,384]{2,1,0:T(8,128)(2,1)}, u32[]{:S(2)}, u32[]{:S(2)}) async-start(bf16[8,128,384]{2,1,0:T(8,128)(2,1)} %get-tuple-element.69), calls=%async_computation.3 | async-start | bytes 1572864 | tf_op jit(solution)/shard_map/all_to_all | solution.py:523
  90.7 10.0 %collective-permute-start.5 = (f32[8,512]{1,0:T(8,128)S(1)}, f32[8,512]{1,0:T(8,128)S(1)}, u32[]{:S(2)}, u32[]{:S(2)}) collective-permute-start(f32[8,512]{1,0:T(8,128)S(1)} %copy-done.2), channel_id=1, source_target_pairs={{0,24},{1,25},{2,26},{3,27},{4,28},{5,29},{6,30},{7,31},{8,16},{9,... | collective-permute-start | bytes 49160 | tf_op jit(solution)/shard_map/ppermute | solution.py:629
  95.7 5.0 %collective-permute-start.4 = (f32[8,512]{1,0:T(8,128)S(1)}, f32[8,512]{1,0:T(8,128)S(1)}, u32[]{:S(2)}, u32[]{:S(2)}) collective-permute-start(f32[8,512]{1,0:T(8,128)S(1)} %copy-done.2), channel_id=1, source_target_pairs={{0,16},{1,17},{2,18},{3,19},{4,20},{5,21},{6,22},{7,23},{8,24},{9,... | collective-permute-start | bytes 49160 | tf_op jit(solution)/shard_map/ppermute | solution.py:629
  96.2 4.7 %collective-permute-start.3 = (f32[8,512]{1,0:T(8,128)S(1)}, f32[8,512]{1,0:T(8,128)S(1)}, u32[]{:S(2)}, u32[]{:S(2)}) collective-permute-start(f32[8,512]{1,0:T(8,128)S(1)} %copy-done.2), channel_id=1, source_target_pairs={{0,8},{1,9},{2,10},{3,11},{4,12},{5,13},{6,14},{7,15},{8,0},{9,1},... | collective-permute-start | bytes 49160 | tf_op jit(solution)/shard_map/ppermute | solution.py:629
  100.7 0.6 copy-start.3
  100.7 0.6 copy-start.4
  101.0 0.6 copy-start.5
  103.1 14.7 %all-to-all-start.4 = ((bf16[8,32,384]{2,1,0:T(8,128)(2,1)}), bf16[8,32,384]{2,1,0:T(8,128)(2,1)}, u32[]{:S(2)}, u32[]{:S(2)}) async-start(bf16[8,32,384]{2,1,0:T(8,128)(2,1)} %tails.1), calls=%async_computation.4 | async-start | bytes 393216 | tf_op jit(solution)/shard_map/all_to_all | solution.py:523
